TPU v7x, 32 devices: a whole 2x2x4 slice. The times are simulated.
32 devices in a mesh: rep: 2 (over y), own: 4 (over z), tp: 4 (over x, core).
Axes of the slice: x: 2, y: 2, z: 4, core: 2. Of those that a mesh axis runs over, the one named last changes fastest.
Arguments:
- tokens: bfloat16 [4096, 8192], P(('rep', 'own'), 'tp'), parts along dimension 0, may hold values from -6 to 6
- token_adapter_index: int32 [4096], P(('rep', 'own')), parts along dimension 0, may hold values from 0 to 31, as said below
- adapter_storage_row: int32 [64], P('rep'), parts along dimension 0, may hold values from 0 to 31, as said below
- value_matrix: bfloat16 [8192, 512], P('tp'), may hold values from -0.0625 to 0.0625
- down_weight_stored: bfloat16 [64, 8192, 64], P(('rep', 'own'), 'tp'), parts along dimension 0, may hold values from -0.0625 to 0.0625
- up_weight_stored: bfloat16 [64, 64, 512], P(('rep', 'own'), None, 'tp'), parts along dimension 0, may hold values from -0.75 to 0.75
Outputs:
- values: bfloat16 [4096, 512], P(('rep', 'own'), 'tp'), parts along dimension 0
There are 2 independent parts, one for each index of `rep`. A program takes and returns all parts, laid end to end along the dimension named above; an argument that names none is the same for every part. Nothing has to cross between parts.
Inputs may be any that keep to these rules, and one draw needn't show every extreme that they name: Row r of down_weight_stored and up_weight_stored is entry r % 8 of owner r // 8; adapter_storage_row is a permutation. `token_adapter_index`: A token's adapter lies on owner adapter_storage_row[id] // 8. The tokens of one group come in runs of up to 4 tokens that share an adapter. From one group at most 256 tokens use adapters of one owner, and some owner receives exactly 256 tokens from every group.
All inputs are finite; a program needn't handle non-finite values.
Results may differ from a plain program's by a relative error of at most 0.001.
Values may be sent and summed in bfloat16 or wider, within the bound.
No kernel may reach another device: no remote copies, remote signals or barrier semaphores. Data moves between devices by JAX's collectives and lax.ppermute only.
A program may use at most 64 MiB of HBM per device.

v0:
```python
import jax
import jax.numpy as jnp
from jax import lax
from jax.sharding import PartitionSpec as P

CAP = 4


ADAPTER_SCALE = 0.5


def per_device(
    tokens,
    token_adapter_index,
    adapter_storage_row,
    value_matrix,
    down_weight_stored,
    up_weight_stored,
):
    owners = lax.axis_size("own")
    tok_dev, features = tokens.shape
    adapter_holder = down_weight_stored.shape[0]
    rank_width = down_weight_stored.shape[2]
    pair_cap = CAP * (2 * tok_dev // CAP // owners)
    every_slot = owners * pair_cap
    catalog = jnp.arange(adapter_storage_row.shape[0], dtype=jnp.int32)
    storage = jnp.sum(
        jnp.where(
            token_adapter_index[:, None] == catalog[None, :], adapter_storage_row[None, :], 0
        ),
        axis=1,
    )
    home_owner = storage // adapter_holder
    local_index = storage % adapter_holder
    owner_hits = (home_owner[:, None] == jnp.arange(owners, dtype=jnp.int32)[None, :]).astype(
        jnp.int32
    )
    before = jnp.cumsum(owner_hits, axis=0) - owner_hits
    place_index = jnp.sum(before * owner_hits, axis=1)
    destination_rows = home_owner * pair_cap + place_index
    outgoing = jnp.zeros((every_slot, features), tokens.dtype).at[destination_rows].set(tokens)
    outgoing = outgoing.reshape(owners, pair_cap, features)
    which_local = (
        jnp.full((every_slot,), adapter_holder, jnp.int32).at[destination_rows].set(local_index)
    )
    which_local = which_local.reshape(owners, pair_cap)
    holder_range = jnp.arange(adapter_holder, dtype=jnp.int32)
    base_product = jnp.dot(tokens, value_matrix, preferred_element_type=jnp.float32)
    rows_in = lax.all_to_all(outgoing, "own", split_axis=0, concat_axis=0, tiled=True)
    selected_rows = lax.all_to_all(which_local, "own", split_axis=0, concat_axis=0, tiled=True)
    row_count = rows_in.shape[0] * rows_in.shape[1]
    rows_flat = rows_in.reshape(row_count, features)
    selector = (selected_rows.reshape(row_count)[:, None] == holder_range[None, :]).astype(
        jnp.float32
    )
    every_low = jnp.einsum(
        "nf,afr->nar", rows_flat, down_weight_stored, preferred_element_type=jnp.float32
    )
    reduced_state = jnp.sum(every_low * selector[:, :, None], axis=1)
    reduced_state, selector = (reduced_state, selector)
    reduced_state = lax.psum(reduced_state, "tp")
    leading_shape = rows_in.shape
    row_count = reduced_state.shape[0]
    spread = (selector[:, :, None] * reduced_state[:, None, :]).reshape(
        row_count, adapter_holder * rank_width
    )
    stacked = up_weight_stored.reshape(
        adapter_holder * rank_width, up_weight_stored.shape[2]
    ).astype(jnp.float32)
    final_output = jnp.dot(spread, stacked, precision=lax.Precision.HIGHEST)
    final_output = final_output.reshape(
        leading_shape[0], leading_shape[1], up_weight_stored.shape[2]
    )
    gathered_output = lax.all_to_all(final_output, "own", split_axis=0, concat_axis=0, tiled=True)
    adapter_product = gathered_output.reshape(every_slot, gathered_output.shape[2])[
        destination_rows
    ]
    mixed_out = (
        lax.psum_scatter(base_product, "tp", scatter_dimension=1, tiled=True)
        + ADAPTER_SCALE * adapter_product
    )
    return mixed_out.astype(jnp.bfloat16)


def solution(mesh):
    return jax.shard_map(
        per_device,
        mesh=mesh,
        in_specs=(
            P(("rep", "own"), "tp"),
            P(("rep", "own")),
            P("rep"),
            P("tp", None),
            P(("rep", "own"), "tp", None),
            P(("rep", "own"), None, "tp"),
        ),
        out_specs=P(("rep", "own"), "tp"),
        check_vma=False,
    )
```

profile of v0, /device:TPU:0, one launch (start us, length us, event | category | flops | bytes accessed | tf_op | source)
XLA Modules:
  0.0 198.2 jit_solution(283363638253209656)
XLA Ops:
  6.5 0.0 copy-start
  6.5 0.9 select_reduce_fusion
  7.5 1.2 reduce-window.6
  8.7 0.2 slice_reduce_fusion
  9.0 0.2 reduce-window.9
  9.1 0.1 add_bitcast_fusion
  9.3 3.0 %scatter_custom_fusion = s32[1024]{0:T(1024)} fusion(s32[512]{0:T(512)S(1)} %bitcast.64, s32[512]{0:T(512)S(1)} %get-tuple-element.5, s32[]{:T(128)} %constant.34.clone.1), kind=kCustom, calls=%fused_computation.43 | custom fusion | bytes 4100 | tf_op jit(solution)/shard_map/scatter | solution.py:44
  12.3 6.3 %all-to-all-start = ((s32[4,1,256]{2,1,0:T(1,128)}), s32[4,1,256]{2,1,0:T(1,128)S(1)}, u32[]{:S(2)}, u32[]{:S(2)}) async-start(s32[4,1,256]{2,1,0:T(1,128)} %bitcast.5), calls=%async_computation.1 | async-start | bytes 8192 | tf_op jit(solution)/shard_map/all_to_all | solution.py:50
  18.6 7.3 %scatter_custom_fusion.1 = bf16[1024,2048]{1,0:T(8,128)(2,1)} fusion(s32[512]{0:T(512)S(1)} %bitcast.65, bf16[512,2048]{1,0:T(8,128)(2,1)} %param.6, bf16[]{:T(256)} %constant.42.clone.1), kind=kCustom, calls=%fused_computation.6 | custom fusion | bytes 4194816 | tf_op jit(solution)/shard_map/scatter | solution.py:41
  25.8 0.0 all-to-all-done
  25.9 5.1 %all-to-all-start.1 = ((bf16[4,256,2048]{2,1,0:T(8,128)(2,1)}), bf16[4,256,2048]{2,1,0:T(8,128)(2,1)}, u32[]{:S(2)}, u32[]{:S(2)}) async-start(bf16[4,256,2048]{2,1,0:T(8,128)(2,1)} %bitcast.58), calls=%async_computation.2 | async-start | bytes 8388608 | tf_op jit(solution)/shard_map/all_to_all | solution.py:49
  30.9 0.0 all-reduce.2.cloned.1.call-start
  31.0 93.0 %all-to-all-done.1 = bf16[4,256,2048]{2,1,0:T(8,128)(2,1)} async-done(((bf16[4,256,2048]{2,1,0:T(8,128)(2,1)}), bf16[4,256,2048]{2,1,0:T(8,128)(2,1)}, u32[]{:S(2)}, u32[]{:S(2)}) %all-to-all-start.1) | async-done | bytes 4194336 | tf_op jit(solution)/shard_map/all_to_all | solution.py:49
  123.9 0.0 copy-done
  123.9 4.6 %fusion.16 = f32[1024,512]{0,1:S(1)} fusion(bf16[1024,2048]{1,0:T(8,128)(2,1)} %bitcast.8, bf16[2048,512]{0,1:T(8,128)(2,1)S(1)} %bitcast.57), kind=kOutput, calls=%fused_computation.49 | convolution fusion | flops 2147483648 | bytes 8388608
  128.5 1.0 multiply_reduce_fusion
  129.4 0.0 all-reduce.2.cloned.1.call-update
  129.5 0.2 reduce-scatter.2.cloned.1.call-start
  129.7 4.4 %fusion.15 = f32[512,512]{1,0:T(8,128)} fusion(bf16[512,2048]{1,0:T(8,128)(2,1)} %param.6, bf16[2048,512]{1,0:T(8,128)(2,1)} %param.9), kind=kOutput, calls=%fused_computation.48 | convolution fusion | flops 1073741824 | bytes 5242880 | tf_op jit(solution)/shard_map/dot_general | solution.py:48
  134.1 0.0 reduce-scatter.2.cloned.1.call-update
  134.2 26.6 %all-reduce.2.cloned.1.call-done = f32[1024,64]{0,1:T(8,128)} async-done(((f32[1024,64]{0,1:T(8,128)}), f32[1024,64]{0,1:T(8,128)}) %all-reduce.2.cloned.1.call-update) | async-done | bytes 262160 | tf_op jit(solution)/shard_map/psum | solution.py:61
  160.7 2.6 %broadcast_multiply_fusion = f32[1024,8,64]{0,2,1:T(8,128)} fusion(f32[1024,64]{0,1:T(8,128)} %all-reduce.2.cloned.1.call-done, f32[1024,8]{0,1:T(8,128)S(1)} %fusion.4), kind=kLoop, calls=%fused_computation.8 | loop fusion | flops 524288 | bytes 2392064 | tf_op jit(solution)/shard_map/mul | solution.py:64
  163.3 0.0 copy-start.1
  163.3 3.2 %mul.59 = f32[4,256,512]{1,0,2:T(4,128)} reshape(f32[1024,8,64]{0,2,1:T(8,128)} %broadcast_multiply_fusion) | data formatting | bytes 4194304 | tf_op jit(solution)/shard_map/mul | solution.py:64
  166.5 0.0 copy-done.1
  166.5 4.2 %fusion = f32[4,256,128]{2,1,0:T(8,128)} fusion(bf16[512,128,1]{1,0,2:T(8,128)(2,1)S(1)} %bitcast.61, f32[4,256,512]{1,0,2:T(4,128)} %mul.59), kind=kOutput, calls=%fused_computation.3 | convolution fusion | flops 805306368 | bytes 2752512 | tf_op jit(solution)/shard_map/dot_general | solution.py:70
  170.7 4.6 %all-to-all-start.2 = ((f32[4,256,128]{2,1,0:T(8,128)}), f32[4,256,128]{2,1,0:T(8,128)S(1)}, u32[]{:S(2)}, u32[]{:S(2)}) async-start(f32[4,256,128]{2,1,0:T(8,128)} %fusion), calls=%async_computation.3 | async-start | bytes 1048576 | tf_op jit(solution)/shard_map/all_to_all | solution.py:74
  175.3 13.4 %all-to-all-done.2 = f32[4,256,128]{2,1,0:T(8,128)S(1)} async-done(((f32[4,256,128]{2,1,0:T(8,128)}), f32[4,256,128]{2,1,0:T(8,128)S(1)}, u32[]{:S(2)}, u32[]{:S(2)}) %all-to-all-start.2) | async-done | bytes 524320 | tf_op jit(solution)/shard_map/all_to_all | solution.py:74
  188.7 1.0 gather_fusion
  189.7 0.0 reduce-scatter.2.cloned.1.call-done
  189.7 1.6 add_convert_fusion
  (7 shorter events, 0.1 us)
Async XLA Ops:
  6.5 117.4 %copy-start = (bf16[8,2048,64]{1,2,0:T(8,128)(2,1)S(1)}, bf16[8,2048,64]{1,2,0:T(8,128)(2,1)}, u32[]{:S(2)}) copy-start(bf16[8,2048,64]{1,2,0:T(8,128)(2,1)} %param.10) | copy-start | bytes 6291460
  12.3 13.6 %all-to-all-start = ((s32[4,1,256]{2,1,0:T(1,128)}), s32[4,1,256]{2,1,0:T(1,128)S(1)}, u32[]{:S(2)}, u32[]{:S(2)}) async-start(s32[4,1,256]{2,1,0:T(1,128)} %bitcast.5), calls=%async_computation.1 | async-start | bytes 8192 | tf_op jit(solution)/shard_map/all_to_all | solution.py:50
  25.9 98.1 %all-to-all-start.1 = ((bf16[4,256,2048]{2,1,0:T(8,128)(2,1)}), bf16[4,256,2048]{2,1,0:T(8,128)(2,1)}, u32[]{:S(2)}, u32[]{:S(2)}) async-start(bf16[4,256,2048]{2,1,0:T(8,128)(2,1)} %bitcast.58), calls=%async_computation.2 | async-start | bytes 8388608 | tf_op jit(solution)/shard_map/all_to_all | solution.py:49
  30.9 129.8 %all-reduce.2.cloned.1.call-start = ((), (), s32[]{:S(2)}) async-start(), calls=%async_computation.5 | async-start | bytes 524288 | tf_op jit(solution)/shard_map/psum | solution.py:61
  129.5 60.3 %reduce-scatter.2.cloned.1.call-start = ((), (), s32[]{:S(2)}) async-start(), calls=%async_computation.4 | async-start | bytes 1310720 | tf_op jit(solution)/shard_map/reduce_scatter | solution.py:79
  163.3 3.2 %copy-start.1 = (bf16[8,64,128]{2,1,0:T(8,128)(2,1)S(1)}, bf16[8,64,128]{2,1,0:T(8,128)(2,1)}, u32[]{:S(2)}) copy-start(bf16[8,64,128]{2,1,0:T(8,128)(2,1)} %param.11) | copy-start | bytes 393220
  170.7 18.0 %all-to-all-start.2 = ((f32[4,256,128]{2,1,0:T(8,128)}), f32[4,256,128]{2,1,0:T(8,128)S(1)}, u32[]{:S(2)}, u32[]{:S(2)}) async-start(f32[4,256,128]{2,1,0:T(8,128)} %fusion), calls=%async_computation.3 | async-start | bytes 1048576 | tf_op jit(solution)/shard_map/all_to_all | solution.py:74
Sparse Core Ops, SparseCore 0:
  129.6 31.1 all-reduce.1
  163.4 24.8 reduce-scatter.1
where the time goes:
time: 199 us; the launch traced here: 198 us
  waiting for transfers between devices  133 us (67%)
  starting transfers between devices  16.2 us (8%)
  local copies, waits for them, and re-layouts  14.7 us (7%)
  between operations  13.5 us (7%)
  matrix products  13.2 us (7%)
  other arithmetic  7.65 us (4%)
    all_to_all x1, waiting for transfers between devices, per_device(): lax.all_to_all(outgoing, 'own', split_axis=0, concat_axis=0, tiled=True)  93 us
    psum x1, waiting for transfers between devices, per_device(): reduced_state = lax.psum(reduced_state, 'tp')  26.6 us
    all_to_all x1, waiting for transfers between devices, per_device(): lax.all_to_all(final_output, 'own', split_axis=0, concat_axis=0, tiled=True)  13.4 us
    scatter x1, local copies, waits for them, and re-layouts, per_device(): jnp.zeros((every_slot, features), tokens.dtype).at[destination_rows]  7.25 us
    all_to_all x1, starting transfers between devices, per_device(): lax.all_to_all(which_local, 'own', split_axis=0, concat_axis=0, tiled=True)  6.32 us
    all_to_all x1, starting transfers between devices, per_device(): lax.all_to_all(outgoing, 'own', split_axis=0, concat_axis=0, tiled=True)  5.09 us
    all_to_all x1, starting transfers between devices, per_device(): lax.all_to_all(final_output, 'own', split_axis=0, concat_axis=0, tiled=True)  4.6 us
    unnamed x1, matrix products  4.55 us
  transfers between devices with their start and end apart: 5, of which 3 were waited for; matrix products, arithmetic and copies ran while one was open for 11% of the time, Pallas kernels for 0%

commit v1 on v0

v1 whole, which is shorter than its diff:
```python
import functools

import jax
import jax.numpy as jnp
from jax import lax
from jax.experimental import pallas as pl
from jax.experimental.pallas import tpu as pltpu
from jax.sharding import PartitionSpec as P

CAP = 4
ADAPTER_SCALE = 0.5
LINE = 4
BF16 = jnp.bfloat16
F32 = jnp.float32
VMEM_LIMIT = 48 * 2**20
CHEAP = pl.CostEstimate(flops=1, bytes_accessed=1, transcendentals=0)


def params(**kw):
    return pltpu.CompilerParams(vmem_limit_bytes=VMEM_LIMIT, **kw)


def iota(shape, dim):
    return lax.broadcasted_iota(jnp.int32, shape, dim)


def dot(a, b, dims=((1,), (0,))):
    return lax.dot_general(a, b, (dims, ((), ())), preferred_element_type=F32)


def split_bf16(x):
    high = x.astype(BF16)
    return high, (x - high.astype(F32)).astype(BF16)


def one_hot(mask):
    return mask.astype(F32).astype(BF16)


IN_VMEM = pl.BlockSpec(memory_space=pltpu.VMEM)
IN_SMEM = pl.BlockSpec(memory_space=pltpu.SMEM)


def storage_of(index_row, storage_row):
    adapters = storage_row.shape[1]
    square = (adapters, adapters)
    diagonal = jnp.where(iota(square, 0) == iota(square, 1), storage_row.astype(F32), 0.0)
    column = jnp.sum(diagonal, axis=1, keepdims=True)
    shape = (adapters, index_row.shape[1])
    picked = jnp.where(iota(shape, 0) == index_row, column, 0.0)
    return jnp.sum(picked, axis=0, keepdims=True).astype(jnp.int32)


def owner_of(storage, holder, owners):
    owner = jnp.zeros_like(storage)
    for k in range(1, owners):
        owner = owner + (storage >= k * holder).astype(jnp.int32)
    return owner


def earlier(tokens):
    return one_hot(iota((tokens, tokens), 0) < iota((tokens, tokens), 1))


def routes(index_row, storage_row, holder, owners, group, first):
    tokens = index_row.shape[1]
    storage = storage_of(index_row, storage_row)
    owner = owner_of(storage, holder, owners)
    strict = earlier(tokens)
    rows = -(-owners // 8) * 8
    hits = iota((rows, tokens), 0) == owner
    rank = jnp.sum(jnp.where(hits, dot(one_hot(hits), strict), 0.0), axis=0, keepdims=True)
    late = jnp.where((owner != group) & (rank >= first), 1.0, 0.0)
    place = dot(jnp.broadcast_to(late, (8, tokens)).astype(BF16), strict)[0:1, :]
    late_place = jnp.where(late > 0, place, -1.0).astype(jnp.int32)
    return owner, storage, rank.astype(jnp.int32), late_place


def route_pack_kernel(owners, holder, first, pieces, me_ref, index_ref, storage_ref, tokens_ref, *refs):
    outs, dest_ref, pick = refs[: len(pieces)], refs[len(pieces)], refs[len(pieces) + 1]

    @pl.when(pl.program_id(0) == 0)
    def _():
        me = me_ref[0]
        owner, _, rank, late = routes(index_ref[...], storage_ref[...], holder, owners, me, first)
        away = owner - me
        away = jnp.where(away < 0, away + owners, away)
        dest = jnp.where(late >= 0, (owners - 1) * first + late, (away - 1) * first + rank)
        dest = jnp.where(away == 0, -1, dest)
        dest_ref[...] = dest
        pick[...] = one_hot(iota(pick.shape, 0) == dest)

    for (start, rows), out in zip(pieces, outs):
        out[...] = dot(pick[start : start + rows, :], tokens_ref[...]).astype(BF16)


def route_pack(me, index_row, storage_row, tokens, owners, holder, first, pieces):
    count, features = tokens.shape
    tile = features // 4 if features % 512 == 0 else features
    slots = max(start + rows for start, rows in pieces)
    return pl.pallas_call(
        functools.partial(route_pack_kernel, owners, holder, first, pieces),
        grid=(features // tile,),
        out_shape=[jax.ShapeDtypeStruct((rows, features), BF16) for _, rows in pieces]
        + [jax.ShapeDtypeStruct((1, count), jnp.int32)],
        in_specs=[
            IN_SMEM,
            pl.BlockSpec((1, count), lambda i: (0, 0)),
            pl.BlockSpec(storage_row.shape, lambda i: (0, 0)),
            pl.BlockSpec((count, tile), lambda i: (0, i)),
        ],
        out_specs=[pl.BlockSpec((rows, tile), lambda i: (0, i)) for _, rows in pieces]
        + [pl.BlockSpec((1, count), lambda i: (0, 0))],
        scratch_shapes=[pltpu.VMEM((slots, count), BF16)],
        compiler_params=params(),
        cost_estimate=CHEAP,
        name="route_pack",
    )(me, index_row, storage_row, tokens)


def arrivals_kernel(owners, holder, first, late, me_ref, storage_ref, *refs):
    index_refs = refs[:owners]
    ids_ref, late_ids_ref, home_ids_ref, more_ref = refs[owners:]
    tokens = index_refs[0].shape[1]
    me = me_ref[0]
    most = jnp.zeros((1, 1), jnp.int32)
    for shift in range(owners):
        group = lax.rem(me - shift + owners, owners)
        owner, storage, rank, place = routes(
            index_refs[shift][...], storage_ref[...], holder, owners, group, first
        )
        most = jnp.maximum(most, jnp.max(place, axis=1, keepdims=True))
        mine = owner == me
        local = jnp.where(mine, storage - me * holder, -1)
        if shift == 0:
            home_ids_ref[...] = local
            continue
        known = jnp.broadcast_to(jnp.where(mine, local + 1, 0).astype(F32), (8, tokens)).astype(BF16)
        slots = ids_ref.shape[1]
        pick = one_hot(iota((slots, tokens), 0) == jnp.where(mine & (place < 0), rank, -1))
        ids_ref[shift - 1 : shift, :] = dot(known, pick, ((1,), (1,)))[0:1, :].astype(jnp.int32) - 1
        slots = late_ids_ref.shape[1]
        pick = one_hot(iota((slots, tokens), 0) == jnp.where(mine, place, -1))
        late_ids_ref[shift - 1 : shift, :] = dot(known, pick, ((1,), (1,)))[0:1, :].astype(jnp.int32) - 1
    more_ref[0] = (jnp.max(most) >= late).astype(jnp.int32)


def arrivals(me, storage_row, index_rows, owners, holder, first, late):
    count = index_rows[0].shape[1]
    return pl.pallas_call(
        functools.partial(arrivals_kernel, owners, holder, first, late),
        out_shape=[
            jax.ShapeDtypeStruct((owners - 1, first), jnp.int32),
            jax.ShapeDtypeStruct((owners - 1, 2 * late), jnp.int32),
            jax.ShapeDtypeStruct((1, count), jnp.int32),
            jax.ShapeDtypeStruct((1,), jnp.int32),
        ],
        in_specs=[IN_SMEM] + [IN_VMEM] * (1 + owners),
        out_specs=[IN_VMEM, IN_VMEM, IN_VMEM, IN_SMEM],
        compiler_params=params(),
        cost_estimate=CHEAP,
        name="arrivals",
    )(me, storage_row, *index_rows)


def low_rank_kernel(blocks, copies, rank, ids_ref, down_ref, *refs):
    out = refs[-1]
    rows_refs = iter(refs)
    for k, ((row, start, rows, _), number) in enumerate(zip(blocks, copies)):
        rows_in = functools.reduce(jnp.add, [next(rows_refs)[...] for _ in range(number)])
        every = dot(down_ref[...], rows_in, ((1,), (1,)))
        ids = ids_ref[row : row + 1, start : start + rows]
        total = jnp.zeros((rank, rows), F32)
        for a in range(down_ref.shape[0] // rank):
            total = total + jnp.where(ids == a, every[a * rank : (a + 1) * rank, :], 0.0)
        out[k * rank : (k + 1) * rank, :] = total


def low_rank(ids, down, blocks, rows_in, rank):
    rows = blocks[0][2]
    copies = [len(x) for x in rows_in]
    return pl.pallas_call(
        functools.partial(low_rank_kernel, blocks, copies, rank),
        out_shape=jax.ShapeDtypeStruct((len(blocks) * rank, rows), F32),
        in_specs=[IN_VMEM] * (2 + sum(copies)),
        out_specs=IN_VMEM,
        compiler_params=params(),
        cost_estimate=CHEAP,
        name="low_rank",
    )(ids, down, *[x for group in rows_in for x in group])


def up_kernel(pieces, holder, rank, ids_ref, up_ref, a_ref, b_ref, *outs):
    up = up_ref[...]
    for k, ((row, start, rows), out) in enumerate(zip(pieces, outs)):
        own = slice(k * rank, (k + 1) * rank)
        ids = ids_ref[row : row + 1, start : start + rows]
        low = a_ref[own, :] + b_ref[own, :]
        spread = jnp.concatenate([jnp.where(ids == a, low, 0.0) for a in range(holder)], axis=0)
        high, rest = split_bf16(spread)
        out[...] = dot(high, up, ((0,), (0,))) + dot(rest, up, ((0,), (0,)))


def up_project(ids, up, pieces, a, b, holder):
    rank = up.shape[0] // holder
    return pl.pallas_call(
        functools.partial(up_kernel, pieces, holder, rank),
        out_shape=[jax.ShapeDtypeStruct((rows, up.shape[1]), F32) for _, _, rows in pieces],
        in_specs=[IN_VMEM] * 4,
        out_specs=[IN_VMEM] * len(pieces),
        compiler_params=params(),
        cost_estimate=CHEAP,
        name="up_project",
    )(ids, up, a, b)


def base_kernel(parts, me_ref, tokens_ref, value_ref, kept_ref, away_ref, full):
    width = full.shape[1] // parts
    full[...] = dot(tokens_ref[...], value_ref[...])
    for q in range(parts):
        block = me_ref[0] ^ q
        at = pl.ds(q // 2 * width, width)
        (away_ref if q % 2 else kept_ref)[:, at] = full[:, pl.ds(pl.multiple_of(block * width, width), width)]


def base_blocks(me, tokens, value, parts):
    count, columns = tokens.shape[0], value.shape[1]
    return pl.pallas_call(
        functools.partial(base_kernel, parts),
        out_shape=[jax.ShapeDtypeStruct((count, columns // 2), F32)] * 2,
        in_specs=[IN_SMEM, IN_VMEM, IN_VMEM],
        out_specs=[IN_VMEM, IN_VMEM],
        scratch_shapes=[pltpu.VMEM((count, columns), F32)],
        compiler_params=params(),
        cost_estimate=CHEAP,
        name="base_blocks",
    )(me, tokens, value)


def gather_add_kernel(pieces, terms, dest_ref, *refs):
    total = refs[0][...]
    for k in range(1, terms):
        total = total + refs[k][...]
    dest = dest_ref[...]
    returned = iter(refs[terms:])
    for start, rows, copies in pieces:
        piece = next(returned)[...]
        for _ in range(copies - 1):
            piece = piece + next(returned)[...]
        pick = one_hot(iota((rows, dest.shape[1]), 0) + start == dest)
        high, rest = split_bf16(ADAPTER_SCALE * piece)
        total = total + (dot(pick, high, ((0,), (0,))) + dot(pick, rest, ((0,), (0,))))
    refs[-1][...] = total.astype(refs[-1].dtype)


def gather_add(dest, pieces, terms, returned, dtype):
    return pl.pallas_call(
        functools.partial(gather_add_kernel, pieces, len(terms)),
        out_shape=jax.ShapeDtypeStruct(terms[0].shape, dtype),
        in_specs=[IN_VMEM] * (1 + len(terms) + len(returned)),
        out_specs=IN_VMEM,
        compiler_params=params(),
        cost_estimate=CHEAP,
        name="gather_add",
    )(dest, *terms, *returned)


def along(x, pairs):
    return lax.ppermute(x, "own", pairs)


def shifted(x, shift):
    size = lax.axis_size("own")
    return along(x, [(i, (i + shift) % size) for i in range(size)])


def beside(x):
    return shifted(x, 1), shifted(x, -1)


def opposite(before, after):
    return along(before, [(0, 1), (2, 3)]), along(after, [(1, 0), (3, 2)])


def partner(x, bit):
    return lax.ppermute(x, "tp", [(i, i ^ bit) for i in range(lax.axis_size("tp"))])


def two_terms(x):
    bit = 1
    while 2 * bit < lax.axis_size("tp"):
        x = x + partner(x, bit)
        bit *= 2
    return x, partner(x, bit)


def base_terms(me, tokens, value, parts):
    kept, away = base_blocks(me, tokens, value, parts)
    bit = 1
    while 2 * bit < parts:
        total = kept + partner(away, bit)
        blocks = jnp.split(total, parts // (2 * bit), axis=1)
        bit *= 2
        kept, away = (jnp.concatenate(blocks[k::2], axis=1) if len(blocks) > 2 else blocks[k] for k in range(2))
    return kept, partner(away, bit)


def direct(tokens, token_adapter_index, adapter_storage_row, value_matrix, down_stored, up_stored):
    owners, parts = lax.axis_size("own"), lax.axis_size("tp")
    count = tokens.shape[0]
    holder, _, rank = down_stored.shape
    cap = CAP * (2 * count // CAP // owners)
    first = cap * 5 // 8 // 16 * 16
    late = cap - first
    me = lax.axis_index("own").astype(jnp.int32).reshape(1)
    me_part = lax.axis_index("tp").astype(jnp.int32).reshape(1)
    index_row = token_adapter_index.reshape(1, count)
    storage_row = adapter_storage_row.reshape(1, -1)
    down = jnp.swapaxes(down_stored, 1, 2).reshape(holder * rank, -1)
    up = up_stored.reshape(holder * rank, -1)
    shifts = list(range(1, owners))
    late_start = (owners - 1) * first

    pieces = [((s - 1) * first, first) for s in shifts] + [(late_start + k * late, late) for k in range(2)]
    *packed, dest = route_pack(me, index_row, storage_row, tokens, owners, holder, first, pieces)
    index_rows = [index_row] + [shifted(index_row, s) for s in shifts]
    packed, index_rows = lax.optimization_barrier((packed, index_rows))
    before, after = beside(packed[owners - 1])
    rows_in = {s: shifted(packed[s - 1], s) for s in (1, 3, 2)}
    ids, late_ids, home_ids, more = arrivals(me, storage_row, index_rows, owners, holder, first, late)

    def terms(ids, blocks, rows_in):
        lows = two_terms(low_rank(ids, down, blocks, rows_in, rank))
        done = up_project(ids, up, [block[:3] for block in blocks], *lows, holder)
        return [x if block[3] is None else shifted(x, -block[3]) for block, x in zip(blocks, done)]

    base = base_terms(me_part, tokens, value_matrix, parts)
    (stays,) = terms(home_ids, [(0, 0, count, None)], [[tokens]])
    total = gather_add(dest, [], [*base, ADAPTER_SCALE * stays], [], F32)

    def late_terms(k, before, far, after):
        blocks = [(s - 1, k * late, late, s) for s in shifts]
        return terms(late_ids, blocks, [[before], list(far), [after]])

    def second(total, x):
        before, after = beside(x)
        back = late_terms(1, before, opposite(before, after), after)
        return gather_add(dest, [(late_start + late, late, owners - 1)], [total], back, F32)

    back = late_terms(0, before, opposite(before, after), after)
    total = gather_add(dest, [(late_start, late, owners - 1)], [total], back, F32)
    back = terms(ids, [(s - 1, 0, first, s) for s in (1, 3)], [[rows_in[1]], [rows_in[3]]])
    total = gather_add(dest, [((s - 1) * first, first, 1) for s in (1, 3)], [total], back, F32)
    total = lax.cond(more[0] > 0, second, lambda total, x: total, total, packed[owners])
    back = terms(ids, [(1, 0, first, 2)], [[rows_in[2]]])
    return gather_add(dest, [(first, first, 1)], [total], back, BF16)


def by_all_to_all(tokens, token_adapter_index, adapter_storage_row, value_matrix, down_stored, up_stored):
    owners = lax.axis_size("own")
    tok_dev, features = tokens.shape
    holder, _, rank = down_stored.shape
    cap = CAP * (2 * tok_dev // CAP // owners)
    slots = owners * cap
    catalog = jnp.arange(adapter_storage_row.shape[0], dtype=jnp.int32)
    storage = jnp.sum(
        jnp.where(token_adapter_index[:, None] == catalog[None, :], adapter_storage_row[None, :], 0), axis=1
    )
    home_owner = storage // holder
    hits = (home_owner[:, None] == jnp.arange(owners, dtype=jnp.int32)[None, :]).astype(jnp.int32)
    before = jnp.cumsum(hits, axis=0) - hits
    dest = home_owner * cap + jnp.sum(before * hits, axis=1)
    outgoing = jnp.zeros((slots, features), tokens.dtype).at[dest].set(tokens)
    which = jnp.full((slots,), holder, jnp.int32).at[dest].set(storage % holder)
    base = jnp.dot(tokens, value_matrix, preferred_element_type=F32)
    rows_in = lax.all_to_all(
        outgoing.reshape(owners, cap, features), "own", split_axis=0, concat_axis=0, tiled=True
    ).reshape(slots, features)
    which = lax.all_to_all(which.reshape(owners, cap), "own", split_axis=0, concat_axis=0, tiled=True)
    selector = (which.reshape(slots)[:, None] == jnp.arange(holder)[None, :]).astype(F32)
    every = jnp.einsum("nf,afr->nar", rows_in, down_stored, preferred_element_type=F32)
    low = lax.psum(jnp.sum(every * selector[:, :, None], axis=1), "tp")
    spread = (selector[:, :, None] * low[:, None, :]).reshape(slots, holder * rank)
    stacked = up_stored.reshape(holder * rank, -1).astype(F32)
    term = jnp.dot(spread, stacked, precision=lax.Precision.HIGHEST).reshape(owners, cap, -1)
    term = lax.all_to_all(term, "own", split_axis=0, concat_axis=0, tiled=True).reshape(slots, -1)[dest]
    mixed = lax.psum_scatter(base, "tp", scatter_dimension=1, tiled=True) + ADAPTER_SCALE * term
    return mixed.astype(BF16)


def solution(mesh):
    owners, parts = mesh.shape["own"], mesh.shape["tp"]
    on_a_line = owners == LINE and parts > 1 and parts & (parts - 1) == 0
    body = direct if on_a_line else by_all_to_all
    return jax.shard_map(
        body,
        mesh=mesh,
        in_specs=(
            P(("rep", "own"), "tp"),
            P(("rep", "own")),
            P("rep"),
            P("tp", None),
            P(("rep", "own"), "tp", None),
            P(("rep", "own"), None, "tp"),
        ),
        out_specs=P(("rep", "own"), "tp"),
        check_vma=False,
    )
```

time: 199 us -> 118 us (0.59)
  waiting for transfers between devices: 133 us -> 58.3 us
  starting transfers between devices: 16.2 us -> 35.6 us
  Pallas kernels: 0 us -> 16.1 us
  matrix products: 13.2 us -> 0 us
  between operations: 13.5 us -> 0.96 us
  local copies, waits for them, and re-layouts: 14.7 us -> 6.28 us
  other arithmetic: 7.65 us -> 0.15 us
    all_to_all x3 -> x0, waiting for transfers between devices: 106 us -> none  [the longest x1 93 us: per_device(): lax.all_to_all(outgoing, 'own', split_axis=0, concat_axis=0, tiled=True)]
    ppermute x0 -> x26, waiting for transfers between devices: none -> 58.3 us  [the longest x16 55.2 us: along(): return lax.ppermute(x, 'own', pairs)]
    ppermute x0 -> x26, starting transfers between devices: none -> 35.6 us  [the longest x16 29.4 us: along(): return lax.ppermute(x, 'own', pairs)]
    psum x1 -> x0, waiting for transfers between devices: 26.6 us -> none  [per_device(): reduced_state = lax.psum(reduced_state, 'tp')]
    pallas_call x0 -> x15, Pallas kernels: none -> 16.1 us  [the longest x4 5.04 us: low_rank(): pl.pallas_call(functools.partial(low_rank_kernel, blocks, copies, rank),...]
    all_to_all x3 -> x0, starting transfers between devices: 16 us -> none  [the longest x1 6.32 us: per_device(): lax.all_to_all(which_local, 'own', split_axis=0, concat_axis=0, tiled=True)]
    scatter x2 -> x0, local copies, waits for them, and re-layouts: 10.3 us -> none  [the longest x1 7.25 us: per_device(): jnp.zeros((every_slot, features), tokens.dtype).at[destination_rows]]
    dot_general x2 -> x0, matrix products: 8.66 us -> none  [the longest x1 4.45 us: per_device(): jnp.dot(tokens, value_matrix, preferred_element_type=jnp.float32)]
  transfers between devices with their start and end apart: 5 -> 26, of which waited for: 3 -> 7; matrix products, arithmetic and copies ran while one was open for 11% -> 0% of each run, Pallas kernels for 0% -> 13%
where the time goes in v1:
time: 118 us
  waiting for transfers between devices  58.3 us (49%)
  starting transfers between devices  35.6 us (30%)
  Pallas kernels  16.1 us (14%)
  local copies, waits for them, and re-layouts  6.28 us (5%)
    ppermute x16, waiting for transfers between devices, along(): return lax.ppermute(x, 'own', pairs)  55.2 us
    ppermute x16, starting transfers between devices, along(): return lax.ppermute(x, 'own', pairs)  29.4 us
    unnamed x28, local copies, waits for them, and re-layouts  6.24 us
    ppermute x10, starting transfers between devices, partner(): lax.ppermute(x, 'tp', [(i, i ^ bit) for i in range(lax.axis_size('tp'))])  6.23 us
    pallas_call x4, Pallas kernels, low_rank(): pl.pallas_call(functools.partial(low_rank_kernel, blocks, copies, rank),...  5.04 us
    pallas_call x1, Pallas kernels, route_pack(): pl.pallas_call(functools.partial(route_pack_kernel, owners, holder, first...  3.95 us
    ppermute x10, waiting for transfers between devices, partner(): lax.ppermute(x, 'tp', [(i, i ^ bit) for i in range(lax.axis_size('tp'))])  3.13 us
  transfers between devices with their start and end apart: 26, of which 7 were waited for; matrix products, arithmetic and copies ran while one was open for 0% of the time, Pallas kernels for 13%

profile of v1, /device:TPU:0, one launch (start us, length us, event | category | flops | bytes accessed | tf_op | source)
XLA Modules:
  0.0 117.6 jit_solution(7527124493884655822)
XLA Ops:
  0.0 4.0 %collective-permute-start.10 = (s32[1,512]{1,0:T(1,128)}, s32[1,512]{1,0:T(1,128)S(1)}, u32[]{:S(2)}, u32[]{:S(2)}) collective-permute-start(s32[1,512]{1,0:T(1,128)} %bitcast.9), channel_id=1, source_target_pairs={{0,8},{4,12},{8,0},{12,4},{1,9},{5,13},{9,1},{13,5},{2,10},{6,14},... | collective-permute-start | bytes 6152 | tf_op jit(solution)/shard_map/ppermute | solution.py:269
  4.0 1.3 %collective-permute-start.11 = (s32[1,512]{1,0:T(1,128)}, s32[1,512]{1,0:T(1,128)S(1)}, u32[]{:S(2)}, u32[]{:S(2)}) collective-permute-start(s32[1,512]{1,0:T(1,128)} %bitcast.10), channel_id=1, source_target_pairs={{0,12},{4,0},{8,4},{12,8},{1,13},{5,1},{9,5},{13,9},{2,14},{6,2},{... | collective-permute-start | bytes 6152 | tf_op jit(solution)/shard_map/ppermute | solution.py:269
  5.4 0.7 collective-permute-start.9
  6.1 1.6 %copy-done = bf16[512,2048]{1,0:T(8,128)(2,1)S(1)} copy-done((bf16[512,2048]{1,0:T(8,128)(2,1)S(1)}, bf16[512,2048]{1,0:T(8,128)(2,1)}, u32[]{:S(2)}) %copy-start) | copy-done | bytes 2097176
  7.7 0.7 copy-done.3
  8.3 0.7 copy-done.5
  9.0 3.9 %route_pack.1 = (bf16[160,2048]{1,0:T(8,128)(2,1)S(1)}, bf16[160,2048]{1,0:T(8,128)(2,1)S(1)}, bf16[160,2048]{1,0:T(8,128)(2,1)S(1)}, bf16[96,2048]{1,0:T(8,128)...) custom-call(s32[1]{0:T(128)} %bitcast.me_ref, s32[1,512]{1,0:T(1,128)S(1)} %bitcast.12, s32[1,32]{1,0:T(1,128)S(1)} %bitcast.14, ...), custom_call_target="tpu_custom_call" | custom-call | flops 1 | bytes 1 | tf_op jit(solution)/shard_map/route_pack/pallas_call | solution.py:101
  12.9 0.9 copy-done.7
  13.8 0.8 copy-done.9
  14.6 1.6 %collective-permute-start.16 = (bf16[96,2048]{1,0:T(8,128)(2,1)S(1)}, bf16[96,2048]{1,0:T(8,128)(2,1)S(1)}, u32[]{:S(2)}, u32[]{:S(2)}) collective-permute-start(bf16[96,2048]{1,0:T(8,128)(2,1)S(1)} %get-tuple-element.71), channel_id=1, source_target_pairs={{0,4},{4,8},{8,12},{12,0},{1,5},{5,9},{9,13},{13,1},{2,6},{6,10},{... | collective-permute-start | bytes 1179656 | tf_op jit(solution)/shard_map/ppermute | solution.py:269
  16.3 1.6 %copy-done.2 = bf16[2048,512]{1,0:T(8,128)(2,1)S(1)} copy-done((bf16[2048,512]{1,0:T(8,128)(2,1)S(1)}, bf16[2048,512]{1,0:T(8,128)(2,1)}, u32[]{:S(2)}) %copy-start.2) | copy-done | bytes 2097176
  17.9 1.4 %base_blocks.1 = (f32[512,256]{1,0:T(8,128)S(1)}, f32[512,256]{1,0:T(8,128)S(1)}) custom-call(s32[1]{0:T(128)} %bitcast.4.me_ref, bf16[512,2048]{1,0:T(8,128)(2,1)S(1)} %copy-done.1, bf16[2048,512]{1,0:T(8,128)(2,1)S(1)} %copy-done.2), custom_call_target="tpu_custom_call" | custom-call | flops 1 | bytes 1 | tf_op jit(solution)/shard_map/base_blocks/pallas_call | solution.py:228
  19.4 2.3 %collective-permute-start.18 = (bf16[96,2048]{1,0:T(8,128)(2,1)S(1)}, bf16[96,2048]{1,0:T(8,128)(2,1)S(1)}, u32[]{:S(2)}, u32[]{:S(2)}) collective-permute-start(bf16[96,2048]{1,0:T(8,128)(2,1)S(1)} %get-tuple-element.71), channel_id=1, source_target_pairs={{0,12},{4,0},{8,4},{12,8},{1,13},{5,1},{9,5},{13,9},{2,14},{6,2},{... | collective-permute-start | bytes 1179656 | tf_op jit(solution)/shard_map/ppermute | solution.py:269
  21.7 6.9 %collective-permute-done.16.refs_0_ = bf16[96,2048]{1,0:T(8,128)(2,1)S(1)} collective-permute-done((bf16[96,2048]{1,0:T(8,128)(2,1)S(1)}, bf16[96,2048]{1,0:T(8,128)(2,1)S(1)}, u32[]{:S(2)}, u32[]{:S(2)}) %collective-permute-start.16) | collective-permute-done | bytes 393248 | tf_op jit(solution)/shard_map/ppermute | solution.py:269
  28.6 1.3 %collective-permute-start.17 = (bf16[96,2048]{1,0:T(8,128)(2,1)S(1)}, bf16[96,2048]{1,0:T(8,128)(2,1)S(1)}, u32[]{:S(2)}, u32[]{:S(2)}) collective-permute-start(bf16[96,2048]{1,0:T(8,128)(2,1)S(1)} %collective-permute-done.16.refs_0_), channel_id=1, source_target_pairs={{0,4},{8,12},{1,5},{9,13},{2,6},{10,14},{3,7},{11,15},{16,20},{24,... | collective-permute-start | bytes 1179656 | tf_op jit(solution)/shard_map/ppermute | solution.py:269
  30.0 3.8 %collective-permute-start.26 = (bf16[160,2048]{1,0:T(8,128)(2,1)S(1)}, bf16[160,2048]{1,0:T(8,128)(2,1)S(1)}, u32[]{:S(2)}, u32[]{:S(2)}) collective-permute-start(bf16[160,2048]{1,0:T(8,128)(2,1)S(1)} %copy-done.8), channel_id=1, source_target_pairs={{0,12},{4,0},{8,4},{12,8},{1,13},{5,1},{9,5},{13,9},{2,14},{6,2},{... | collective-permute-start | bytes 1966088 | tf_op jit(solution)/shard_map/ppermute | solution.py:269
  33.8 3.3 %collective-permute-done.18.refs_3_ = bf16[96,2048]{1,0:T(8,128)(2,1)S(1)} collective-permute-done((bf16[96,2048]{1,0:T(8,128)(2,1)S(1)}, bf16[96,2048]{1,0:T(8,128)(2,1)S(1)}, u32[]{:S(2)}, u32[]{:S(2)}) %collective-permute-start.18) | collective-permute-done | bytes 393248 | tf_op jit(solution)/shard_map/ppermute | solution.py:269
  37.0 0.5 collective-permute-start.31
  37.6 1.3 %collective-permute-start.19 = (bf16[96,2048]{1,0:T(8,128)(2,1)S(1)}, bf16[96,2048]{1,0:T(8,128)(2,1)S(1)}, u32[]{:S(2)}, u32[]{:S(2)}) collective-permute-start(bf16[96,2048]{1,0:T(8,128)(2,1)S(1)} %collective-permute-done.18.refs_3_), channel_id=1, source_target_pairs={{4,0},{12,8},{5,1},{13,9},{6,2},{14,10},{7,3},{15,11},{20,16},{28,... | collective-permute-start | bytes 1179656 | tf_op jit(solution)/shard_map/ppermute | solution.py:269
  38.9 2.2 %arrivals.1 = (s32[3,160]{1,0:T(4,128)S(1)}, s32[3,192]{1,0:T(4,128)S(1)}, s32[1,512]{1,0:T(1,128)S(1)}, s32[1]{0:T(128)}) custom-call(s32[1]{0:T(128)} %bitcast.me_ref, s32[1,32]{1,0:T(1,128)S(1)} %bitcast.15, s32[1,512]{1,0:T(1,128)S(1)} %bitcast.13, s32[1,512]{1,0:T(1,128)S(1)} %collective-permute-done.9.refs_1_, ...), custom_call_target="tpu_custom_call" | custom-call | flops 1 | bytes 1 | tf_op jit(solution)/shard_map/arrivals/pallas_call | solution.py:150
  41.1 1.3 %low_rank.6 = f32[64,512]{1,0:T(8,128)S(1)} custom-call(s32[1,512]{1,0:T(1,128)S(1)} %get-tuple-element.69.ids_ref, bf16[512,2048]{1,0:T(8,128)(2,1)S(1)} %bitcast.16, bf16[512,2048]{1,0:T(8,128)(2,1)S(1)} %copy-done.1), custom_call_target="tpu_custom_call" | custom-call | flops 1 | bytes 1 | tf_op jit(solution)/shard_map/low_rank/pallas_call | solution.py:182
  42.6 29.0 %collective-permute-done.19.refs_2_ = bf16[96,2048]{1,0:T(8,128)(2,1)S(1)} collective-permute-done((bf16[96,2048]{1,0:T(8,128)(2,1)S(1)}, bf16[96,2048]{1,0:T(8,128)(2,1)S(1)}, u32[]{:S(2)}, u32[]{:S(2)}) %collective-permute-start.19) | collective-permute-done | bytes 393248 | tf_op jit(solution)/shard_map/ppermute | solution.py:269
  71.6 1.5 %collective-permute-start.13 = (f32[512,128]{1,0:T(8,128)S(1)}, f32[512,128]{1,0:T(8,128)S(1)}, u32[]{:S(2)}, u32[]{:S(2)}) collective-permute-start(f32[512,128]{1,0:T(8,128)S(1)} %get-tuple-element.82), channel_id=1, source_target_pairs={{0,2},{1,3},{2,0},{3,1},{4,6},{5,7},{6,4},{7,5},{8,10},{9,11},{10,... | collective-permute-start | bytes 786440 | tf_op jit(solution)/shard_map/ppermute | solution.py:286
  73.1 1.8 %low_rank.7 = f32[192,96]{1,0:T(8,128)S(1)} custom-call(s32[3,192]{1,0:T(4,128)S(1)} %get-tuple-element.70.ids_ref, bf16[512,2048]{1,0:T(8,128)(2,1)S(1)} %bitcast.17, bf16[96,2048]{1,0:T(8,128)(2,1)S(1)} %collective-permute-done.16.refs_0_, bf16[96,2048]{1,0:T(8,128)(2,1)S(1)} %collective-permute-done.17.refs_1_, ...), custom_call_target="tpu_custom_call" | custom-call | flops 1 | bytes 1 | tf_op jit(solution)/shard_map/low_rank/pallas_call | solution.py:182
  75.0 1.3 %low_rank.8 = f32[128,160]{1,0:T(8,128)S(1)} custom-call(s32[3,160]{1,0:T(4,128)S(1)} %get-tuple-element.75.ids_ref, bf16[512,2048]{1,0:T(8,128)(2,1)S(1)} %bitcast.18, bf16[160,2048]{1,0:T(8,128)(2,1)S(1)} %collective-permute-done.25.refs_0_, bf16[160,2048]{1,0:T(8,128)(2,1)S(1)} %collective-permute-done.26.refs_1_), custom_call_target="tpu_custom_call" | custom-call | flops 1 | bytes 1 | tf_op jit(solution)/shard_map/low_rank/pallas_call | solution.py:182
  76.3 0.6 collective-permute-start.27
  76.9 0.6 collective-permute-start.15
  77.5 1.6 %collective-permute-start.21 = (f32[192,96]{1,0:T(8,128)S(1)}, f32[192,96]{1,0:T(8,128)S(1)}, u32[]{:S(2)}, u32[]{:S(2)}) collective-permute-start(f32[192,96]{1,0:T(8,128)S(1)} %add.20.a_ref), channel_id=1, source_target_pairs={{0,2},{1,3},{2,0},{3,1},{4,6},{5,7},{6,4},{7,5},{8,10},{9,11},{10,... | collective-permute-start | bytes 221192 | tf_op jit(solution)/shard_map/ppermute | solution.py:286
  79.1 12.1 %collective-permute-done.31.refs_0_ = bf16[160,2048]{1,0:T(8,128)(2,1)S(1)} collective-permute-done((bf16[160,2048]{1,0:T(8,128)(2,1)S(1)}, bf16[160,2048]{1,0:T(8,128)(2,1)S(1)}, u32[]{:S(2)}, u32[]{:S(2)}) %collective-permute-start.31) | collective-permute-done | bytes 655392 | tf_op jit(solution)/shard_map/ppermute | solution.py:269
  91.1 0.7 low_rank.9
  92.0 1.6 %collective-permute-start.28 = (f32[128,160]{1,0:T(8,128)S(1)}, f32[128,160]{1,0:T(8,128)S(1)}, u32[]{:S(2)}, u32[]{:S(2)}) collective-permute-start(f32[128,160]{1,0:T(8,128)S(1)} %add.21.a_ref), channel_id=1, source_target_pairs={{0,2},{1,3},{2,0},{3,1},{4,6},{5,7},{6,4},{7,5},{8,10},{9,11},{10,... | collective-permute-start | bytes 245768 | tf_op jit(solution)/shard_map/ppermute | solution.py:286
  93.6 0.4 up_project.7
  94.0 5.4 %collective-permute-start.22 = (f32[96,128]{1,0:T(8,128)S(1)}, f32[96,128]{1,0:T(8,128)S(1)}, u32[]{:S(2)}, u32[]{:S(2)}) collective-permute-start(f32[96,128]{1,0:T(8,128)S(1)} %get-tuple-element.72), channel_id=1, source_target_pairs={{0,12},{4,0},{8,4},{12,8},{1,13},{5,1},{9,5},{13,9},{2,14},{6,2},{... | collective-permute-start | bytes 147464 | tf_op jit(solution)/shard_map/ppermute | solution.py:269
  100.1 0.5 up_project.6
  100.6 3.1 %collective-permute-done.33.b_ref = f32[64,160]{1,0:T(8,128)S(1)} collective-permute-done((f32[64,160]{1,0:T(8,128)S(1)}, f32[64,160]{1,0:T(8,128)S(1)}, u32[]{:S(2)}, u32[]{:S(2)}) %collective-permute-start.33) | collective-permute-done | bytes 40992 | tf_op jit(solution)/shard_map/ppermute | solution.py:286
  103.7 0.3 up_project.9
  104.1 1.1 collective-permute-start.34
  105.2 0.5 up_project.8
  105.7 1.5 %collective-permute-start.29 = (f32[160,128]{1,0:T(8,128)S(1)}, f32[160,128]{1,0:T(8,128)S(1)}, u32[]{:S(2)}, u32[]{:S(2)}) collective-permute-start(f32[160,128]{1,0:T(8,128)S(1)} %get-tuple-element.78), channel_id=1, source_target_pairs={{0,12},{4,0},{8,4},{12,8},{1,13},{5,1},{9,5},{13,9},{2,14},{6,2},{... | collective-permute-start | bytes 245768 | tf_op jit(solution)/shard_map/ppermute | solution.py:269
  107.2 0.6 collective-permute-start.30
  107.8 1.8 %collective-permute-start.23 = (f32[96,128]{1,0:T(8,128)S(1)}, f32[96,128]{1,0:T(8,128)S(1)}, u32[]{:S(2)}, u32[]{:S(2)}) collective-permute-start(f32[96,128]{1,0:T(8,128)S(1)} %get-tuple-element.73), channel_id=1, source_target_pairs={{0,8},{4,12},{8,0},{12,4},{1,9},{5,13},{9,1},{13,5},{2,10},{6,14},... | collective-permute-start | bytes 147464 | tf_op jit(solution)/shard_map/ppermute | solution.py:269
  109.6 1.9 %collective-permute-start.24 = (f32[96,128]{1,0:T(8,128)S(1)}, f32[96,128]{1,0:T(8,128)S(1)}, u32[]{:S(2)}, u32[]{:S(2)}) collective-permute-start(f32[96,128]{1,0:T(8,128)S(1)} %get-tuple-element.74), channel_id=1, source_target_pairs={{0,4},{4,8},{8,12},{12,0},{1,5},{5,9},{9,13},{13,1},{2,6},{6,10},{... | collective-permute-start | bytes 147464 | tf_op jit(solution)/shard_map/ppermute | solution.py:269
  111.6 3.3 %collective-permute-done.23.refs_2_ = f32[96,128]{1,0:T(8,128)S(1)} collective-permute-done((f32[96,128]{1,0:T(8,128)S(1)}, f32[96,128]{1,0:T(8,128)S(1)}, u32[]{:S(2)}, u32[]{:S(2)}) %collective-permute-start.23) | collective-permute-done | bytes 49184 | tf_op jit(solution)/shard_map/ppermute | solution.py:269
  115.0 0.5 collective-permute-done.24.refs_3_
  115.5 0.3 gather_add.7.refs_0_
  115.8 0.5 gather_add.8
  116.3 0.2 conditional.1
  116.6 1.0 gather_add.9
  (55 shorter events, 0.8 us)
Async XLA Ops:
  0.0 14.6 %collective-permute-start.10 = (s32[1,512]{1,0:T(1,128)}, s32[1,512]{1,0:T(1,128)S(1)}, u32[]{:S(2)}, u32[]{:S(2)}) collective-permute-start(s32[1,512]{1,0:T(1,128)} %bitcast.9), channel_id=1, source_target_pairs={{0,8},{4,12},{8,0},{12,4},{1,9},{5,13},{9,1},{13,5},{2,10},{6,14},... | collective-permute-start | bytes 6152 | tf_op jit(solution)/shard_map/ppermute | solution.py:269
  4.0 10.6 %collective-permute-start.11 = (s32[1,512]{1,0:T(1,128)}, s32[1,512]{1,0:T(1,128)S(1)}, u32[]{:S(2)}, u32[]{:S(2)}) collective-permute-start(s32[1,512]{1,0:T(1,128)} %bitcast.10), channel_id=1, source_target_pairs={{0,12},{4,0},{8,4},{12,8},{1,13},{5,1},{9,5},{13,9},{2,14},{6,2},{... | collective-permute-start | bytes 6152 | tf_op jit(solution)/shard_map/ppermute | solution.py:269
  5.4 9.3 %collective-permute-start.9 = (s32[1,512]{1,0:T(1,128)}, s32[1,512]{1,0:T(1,128)S(1)}, u32[]{:S(2)}, u32[]{:S(2)}) collective-permute-start(s32[1,512]{1,0:T(1,128)} %bitcast.11), channel_id=1, source_target_pairs={{0,4},{4,8},{8,12},{12,0},{1,5},{5,9},{9,13},{13,1},{2,6},{6,10},{... | collective-permute-start | bytes 6152 | tf_op jit(solution)/shard_map/ppermute | solution.py:269
  6.1 1.6 %copy-start = (bf16[512,2048]{1,0:T(8,128)(2,1)S(1)}, bf16[512,2048]{1,0:T(8,128)(2,1)}, u32[]{:S(2)}) copy-start(bf16[512,2048]{1,0:T(8,128)(2,1)} %refs_0_.1) | copy-start | bytes 6291460
  7.7 0.7 copy-start.3
  8.3 0.7 copy-start.5
  9.0 7.3 %copy-start.1 = (bf16[512,2048]{1,0:T(8,128)(2,1)S(1)}, bf16[512,2048]{1,0:T(8,128)(2,1)}, u32[]{:S(2)}) copy-start(bf16[512,2048]{1,0:T(8,128)(2,1)} %refs_0_.1) | copy-start | bytes 6291460
  12.9 0.9 copy-start.7
  13.8 0.8 copy-start.9
  14.6 13.9 %collective-permute-start.16 = (bf16[96,2048]{1,0:T(8,128)(2,1)S(1)}, bf16[96,2048]{1,0:T(8,128)(2,1)S(1)}, u32[]{:S(2)}, u32[]{:S(2)}) collective-permute-start(bf16[96,2048]{1,0:T(8,128)(2,1)S(1)} %get-tuple-element.71), channel_id=1, source_target_pairs={{0,4},{4,8},{8,12},{12,0},{1,5},{5,9},{9,13},{13,1},{2,6},{6,10},{... | collective-permute-start | bytes 1179656 | tf_op jit(solution)/shard_map/ppermute | solution.py:269
  16.3 1.6 %copy-start.2 = (bf16[2048,512]{1,0:T(8,128)(2,1)S(1)}, bf16[2048,512]{1,0:T(8,128)(2,1)}, u32[]{:S(2)}) copy-start(bf16[2048,512]{1,0:T(8,128)(2,1)} %value_ref.1) | copy-start | bytes 6291460
  17.9 12.0 %copy-start.10 = (bf16[160,2048]{1,0:T(8,128)(2,1)S(1)}, bf16[160,2048]{1,0:T(8,128)(2,1)}, u32[]{:S(2)}) copy-start(bf16[160,2048]{1,0:T(8,128)(2,1)} %copy-done.9) | copy-start | bytes 1966084
  17.9 12.1 %copy-start.8 = (bf16[160,2048]{1,0:T(8,128)(2,1)S(1)}, bf16[160,2048]{1,0:T(8,128)(2,1)}, u32[]{:S(2)}) copy-start(bf16[160,2048]{1,0:T(8,128)(2,1)} %copy-done.7) | copy-start | bytes 1966084
  17.9 21.0 %copy-start.4 = (s32[512]{0:T(512)S(1)}, s32[512]{0:T(512)}, u32[]{:S(2)}) copy-start(s32[512]{0:T(512)} %param.9) | copy-start | bytes 6148
  17.9 21.0 %copy-start.6 = (s32[32]{0:T(128)S(1)}, s32[32]{0:T(128)}, u32[]{:S(2)}) copy-start(s32[32]{0:T(128)} %param.10) | copy-start | bytes 388
  17.9 23.2 %copy-start.11 = (bf16[8,2048,64]{1,2,0:T(8,128)(2,1)S(1)}, bf16[8,2048,64]{1,2,0:T(8,128)(2,1)}, u32[]{:S(2)}) copy-start(bf16[8,2048,64]{1,2,0:T(8,128)(2,1)} %param.12) | copy-start | bytes 6291460
  19.3 18.3 %collective-permute-start.12 = (f32[512,256]{1,0:T(8,128)S(1)}, f32[512,256]{1,0:T(8,128)S(1)}, u32[]{:S(2)}, u32[]{:S(2)}) collective-permute-start(f32[512,256]{1,0:T(8,128)S(1)} %get-tuple-element.68), channel_id=1, source_target_pairs={{0,1},{1,0},{2,3},{3,2},{4,5},{5,4},{6,7},{7,6},{8,9},{9,8},{10,11... | collective-permute-start | bytes 1572872 | tf_op jit(solution)/shard_map/ppermute | solution.py:286
  19.4 17.7 %collective-permute-start.18 = (bf16[96,2048]{1,0:T(8,128)(2,1)S(1)}, bf16[96,2048]{1,0:T(8,128)(2,1)S(1)}, u32[]{:S(2)}, u32[]{:S(2)}) collective-permute-start(bf16[96,2048]{1,0:T(8,128)(2,1)S(1)} %get-tuple-element.71), channel_id=1, source_target_pairs={{0,12},{4,0},{8,4},{12,8},{1,13},{5,1},{9,5},{13,9},{2,14},{6,2},{... | collective-permute-start | bytes 1179656 | tf_op jit(solution)/shard_map/ppermute | solution.py:269
  28.6 13.9 %collective-permute-start.17 = (bf16[96,2048]{1,0:T(8,128)(2,1)S(1)}, bf16[96,2048]{1,0:T(8,128)(2,1)S(1)}, u32[]{:S(2)}, u32[]{:S(2)}) collective-permute-start(bf16[96,2048]{1,0:T(8,128)(2,1)S(1)} %collective-permute-done.16.refs_0_), channel_id=1, source_target_pairs={{0,4},{8,12},{1,5},{9,13},{2,6},{10,14},{3,7},{11,15},{16,20},{24,... | collective-permute-start | bytes 1179656 | tf_op jit(solution)/shard_map/ppermute | solution.py:269
  29.9 45.0 %collective-permute-start.25 = (bf16[160,2048]{1,0:T(8,128)(2,1)S(1)}, bf16[160,2048]{1,0:T(8,128)(2,1)S(1)}, u32[]{:S(2)}, u32[]{:S(2)}) collective-permute-start(bf16[160,2048]{1,0:T(8,128)(2,1)S(1)} %copy-done.10), channel_id=1, source_target_pairs={{0,4},{4,8},{8,12},{12,0},{1,5},{5,9},{9,13},{13,1},{2,6},{6,10},{... | collective-permute-start | bytes 1966088 | tf_op jit(solution)/shard_map/ppermute | solution.py:269
  30.0 45.0 %collective-permute-start.26 = (bf16[160,2048]{1,0:T(8,128)(2,1)S(1)}, bf16[160,2048]{1,0:T(8,128)(2,1)S(1)}, u32[]{:S(2)}, u32[]{:S(2)}) collective-permute-start(bf16[160,2048]{1,0:T(8,128)(2,1)S(1)} %copy-done.8), channel_id=1, source_target_pairs={{0,12},{4,0},{8,4},{12,8},{1,13},{5,1},{9,5},{13,9},{2,14},{6,2},{... | collective-permute-start | bytes 1966088 | tf_op jit(solution)/shard_map/ppermute | solution.py:269
  37.0 54.1 %collective-permute-start.31 = (bf16[160,2048]{1,0:T(8,128)(2,1)S(1)}, bf16[160,2048]{1,0:T(8,128)(2,1)S(1)}, u32[]{:S(2)}, u32[]{:S(2)}) collective-permute-start(bf16[160,2048]{1,0:T(8,128)(2,1)S(1)} %get-tuple-element.81), channel_id=1, source_target_pairs={{0,8},{4,12},{8,0},{12,4},{1,9},{5,13},{9,1},{13,5},{2,10},{6,14},... | collective-permute-start | bytes 1966088 | tf_op jit(solution)/shard_map/ppermute | solution.py:269
  37.6 34.0 %collective-permute-start.19 = (bf16[96,2048]{1,0:T(8,128)(2,1)S(1)}, bf16[96,2048]{1,0:T(8,128)(2,1)S(1)}, u32[]{:S(2)}, u32[]{:S(2)}) collective-permute-start(bf16[96,2048]{1,0:T(8,128)(2,1)S(1)} %collective-permute-done.18.refs_3_), channel_id=1, source_target_pairs={{4,0},{12,8},{5,1},{13,9},{6,2},{14,10},{7,3},{15,11},{20,16},{28,... | collective-permute-start | bytes 1179656 | tf_op jit(solution)/shard_map/ppermute | solution.py:269
  42.5 34.4 %collective-permute-start.14 = (f32[64,512]{1,0:T(8,128)S(1)}, f32[64,512]{1,0:T(8,128)S(1)}, u32[]{:S(2)}, u32[]{:S(2)}) collective-permute-start(f32[64,512]{1,0:T(8,128)S(1)} %low_rank.6), channel_id=1, source_target_pairs={{0,1},{1,0},{2,3},{3,2},{4,5},{5,4},{6,7},{7,6},{8,9},{9,8},{10,11... | collective-permute-start | bytes 393224 | tf_op jit(solution)/shard_map/ppermute | solution.py:286
  71.6 36.2 %collective-permute-start.13 = (f32[512,128]{1,0:T(8,128)S(1)}, f32[512,128]{1,0:T(8,128)S(1)}, u32[]{:S(2)}, u32[]{:S(2)}) collective-permute-start(f32[512,128]{1,0:T(8,128)S(1)} %get-tuple-element.82), channel_id=1, source_target_pairs={{0,2},{1,3},{2,0},{3,1},{4,6},{5,7},{6,4},{7,5},{8,10},{9,11},{10,... | collective-permute-start | bytes 786440 | tf_op jit(solution)/shard_map/ppermute | solution.py:286
  74.9 2.5 %collective-permute-start.20 = (f32[192,96]{1,0:T(8,128)S(1)}, f32[192,96]{1,0:T(8,128)S(1)}, u32[]{:S(2)}, u32[]{:S(2)}) collective-permute-start(f32[192,96]{1,0:T(8,128)S(1)} %low_rank.7), channel_id=1, source_target_pairs={{0,1},{1,0},{2,3},{3,2},{4,5},{5,4},{6,7},{7,6},{8,9},{9,8},{10,11... | collective-permute-start | bytes 221192 | tf_op jit(solution)/shard_map/ppermute | solution.py:286
  76.3 17.3 %copy-start.12 = (bf16[8,64,128]{2,1,0:T(8,128)(2,1)S(1)}, bf16[8,64,128]{2,1,0:T(8,128)(2,1)}, u32[]{:S(2)}) copy-start(bf16[8,64,128]{2,1,0:T(8,128)(2,1)} %param.13) | copy-start | bytes 393220
  76.3 15.7 %collective-permute-start.27 = (f32[128,160]{1,0:T(8,128)S(1)}, f32[128,160]{1,0:T(8,128)S(1)}, u32[]{:S(2)}, u32[]{:S(2)}) collective-permute-start(f32[128,160]{1,0:T(8,128)S(1)} %low_rank.8), channel_id=1, source_target_pairs={{0,1},{1,0},{2,3},{3,2},{4,5},{5,4},{6,7},{7,6},{8,9},{9,8},{10,11... | collective-permute-start | bytes 245768 | tf_op jit(solution)/shard_map/ppermute | solution.py:286
  76.9 23.3 %collective-permute-start.15 = (f32[64,512]{1,0:T(8,128)S(1)}, f32[64,512]{1,0:T(8,128)S(1)}, u32[]{:S(2)}, u32[]{:S(2)}) collective-permute-start(f32[64,512]{1,0:T(8,128)S(1)} %add.19.a_ref), channel_id=1, source_target_pairs={{0,2},{1,3},{2,0},{3,1},{4,6},{5,7},{6,4},{7,5},{8,10},{9,11},{10,... | collective-permute-start | bytes 393224 | tf_op jit(solution)/shard_map/ppermute | solution.py:286
  77.5 16.1 %collective-permute-start.21 = (f32[192,96]{1,0:T(8,128)S(1)}, f32[192,96]{1,0:T(8,128)S(1)}, u32[]{:S(2)}, u32[]{:S(2)}) collective-permute-start(f32[192,96]{1,0:T(8,128)S(1)} %add.20.a_ref), channel_id=1, source_target_pairs={{0,2},{1,3},{2,0},{3,1},{4,6},{5,7},{6,4},{7,5},{8,10},{9,11},{10,... | collective-permute-start | bytes 221192 | tf_op jit(solution)/shard_map/ppermute | solution.py:286
  91.8 7.6 %collective-permute-start.32 = (f32[64,160]{1,0:T(8,128)S(1)}, f32[64,160]{1,0:T(8,128)S(1)}, u32[]{:S(2)}, u32[]{:S(2)}) collective-permute-start(f32[64,160]{1,0:T(8,128)S(1)} %low_rank.9), channel_id=1, source_target_pairs={{0,1},{1,0},{2,3},{3,2},{4,5},{5,4},{6,7},{7,6},{8,9},{9,8},{10,11... | collective-permute-start | bytes 122888 | tf_op jit(solution)/shard_map/ppermute | solution.py:286
  92.0 13.2 %collective-permute-start.28 = (f32[128,160]{1,0:T(8,128)S(1)}, f32[128,160]{1,0:T(8,128)S(1)}, u32[]{:S(2)}, u32[]{:S(2)}) collective-permute-start(f32[128,160]{1,0:T(8,128)S(1)} %add.21.a_ref), channel_id=1, source_target_pairs={{0,2},{1,3},{2,0},{3,1},{4,6},{5,7},{6,4},{7,5},{8,10},{9,11},{10,... | collective-permute-start | bytes 245768 | tf_op jit(solution)/shard_map/ppermute | solution.py:286
  94.0 15.6 %collective-permute-start.22 = (f32[96,128]{1,0:T(8,128)S(1)}, f32[96,128]{1,0:T(8,128)S(1)}, u32[]{:S(2)}, u32[]{:S(2)}) collective-permute-start(f32[96,128]{1,0:T(8,128)S(1)} %get-tuple-element.72), channel_id=1, source_target_pairs={{0,12},{4,0},{8,4},{12,8},{1,13},{5,1},{9,5},{13,9},{2,14},{6,2},{... | collective-permute-start | bytes 147464 | tf_op jit(solution)/shard_map/ppermute | solution.py:269
  99.4 4.3 %collective-permute-start.33 = (f32[64,160]{1,0:T(8,128)S(1)}, f32[64,160]{1,0:T(8,128)S(1)}, u32[]{:S(2)}, u32[]{:S(2)}) collective-permute-start(f32[64,160]{1,0:T(8,128)S(1)} %add.22.a_ref), channel_id=1, source_target_pairs={{0,2},{1,3},{2,0},{3,1},{4,6},{5,7},{6,4},{7,5},{8,10},{9,11},{10,... | collective-permute-start | bytes 122888 | tf_op jit(solution)/shard_map/ppermute | solution.py:286
  100.1 16.2 %copy-start.13 = (bf16[96,2048]{1,0:T(8,128)(2,1)S(1)}, bf16[96,2048]{1,0:T(8,128)(2,1)}, u32[]{:S(2)}) copy-start(bf16[96,2048]{1,0:T(8,128)(2,1)} %get-tuple-element.80) | copy-start | bytes 1179652
  104.1 12.5 %collective-permute-start.34 = (f32[160,128]{1,0:T(8,128)S(1)}, f32[160,128]{1,0:T(8,128)S(1)}, u32[]{:S(2)}, u32[]{:S(2)}) collective-permute-start(f32[160,128]{1,0:T(8,128)S(1)} %up_project.9), channel_id=1, source_target_pairs={{0,8},{4,12},{8,0},{12,4},{1,9},{5,13},{9,1},{13,5},{2,10},{6,14},... | collective-permute-start | bytes 245768 | tf_op jit(solution)/shard_map/ppermute | solution.py:269
  105.7 10.1 %collective-permute-start.29 = (f32[160,128]{1,0:T(8,128)S(1)}, f32[160,128]{1,0:T(8,128)S(1)}, u32[]{:S(2)}, u32[]{:S(2)}) collective-permute-start(f32[160,128]{1,0:T(8,128)S(1)} %get-tuple-element.78), channel_id=1, source_target_pairs={{0,12},{4,0},{8,4},{12,8},{1,13},{5,1},{9,5},{13,9},{2,14},{6,2},{... | collective-permute-start | bytes 245768 | tf_op jit(solution)/shard_map/ppermute | solution.py:269
  107.2 8.6 %collective-permute-start.30 = (f32[160,128]{1,0:T(8,128)S(1)}, f32[160,128]{1,0:T(8,128)S(1)}, u32[]{:S(2)}, u32[]{:S(2)}) collective-permute-start(f32[160,128]{1,0:T(8,128)S(1)} %get-tuple-element.79), channel_id=1, source_target_pairs={{0,4},{4,8},{8,12},{12,0},{1,5},{5,9},{9,13},{13,1},{2,6},{6,10},{... | collective-permute-start | bytes 245768 | tf_op jit(solution)/shard_map/ppermute | solution.py:269
  107.8 7.2 %collective-permute-start.23 = (f32[96,128]{1,0:T(8,128)S(1)}, f32[96,128]{1,0:T(8,128)S(1)}, u32[]{:S(2)}, u32[]{:S(2)}) collective-permute-start(f32[96,128]{1,0:T(8,128)S(1)} %get-tuple-element.73), channel_id=1, source_target_pairs={{0,8},{4,12},{8,0},{12,4},{1,9},{5,13},{9,1},{13,5},{2,10},{6,14},... | collective-permute-start | bytes 147464 | tf_op jit(solution)/shard_map/ppermute | solution.py:269
  109.6 5.9 %collective-permute-start.24 = (f32[96,128]{1,0:T(8,128)S(1)}, f32[96,128]{1,0:T(8,128)S(1)}, u32[]{:S(2)}, u32[]{:S(2)}) collective-permute-start(f32[96,128]{1,0:T(8,128)S(1)} %get-tuple-element.74), channel_id=1, source_target_pairs={{0,4},{4,8},{8,12},{12,0},{1,5},{5,9},{9,13},{13,1},{2,6},{6,10},{... | collective-permute-start | bytes 147464 | tf_op jit(solution)/shard_map/ppermute | solution.py:269

commit v2 on v1

--- a/solution.py
+++ b/solution.py
@@ -12,7 +12,7 @@
 LINE = 4
 BF16 = jnp.bfloat16
 F32 = jnp.float32
-VMEM_LIMIT = 48 * 2**20
+VMEM_LIMIT = 16 * 2**20
 CHEAP = pl.CostEstimate(flops=1, bytes_accessed=1, transcendentals=0)
 
 
@@ -76,51 +76,82 @@
     return owner, storage, rank.astype(jnp.int32), late_place
 
 
-def route_pack_kernel(owners, holder, first, pieces, me_ref, index_ref, storage_ref, tokens_ref, *refs):
-    outs, dest_ref, pick = refs[: len(pieces)], refs[len(pieces)], refs[len(pieces) + 1]
-
-    @pl.when(pl.program_id(0) == 0)
-    def _():
-        me = me_ref[0]
-        owner, _, rank, late = routes(index_ref[...], storage_ref[...], holder, owners, me, first)
-        away = owner - me
-        away = jnp.where(away < 0, away + owners, away)
-        dest = jnp.where(late >= 0, (owners - 1) * first + late, (away - 1) * first + rank)
-        dest = jnp.where(away == 0, -1, dest)
-        dest_ref[...] = dest
-        pick[...] = one_hot(iota(pick.shape, 0) == dest)
-
-    for (start, rows), out in zip(pieces, outs):
-        out[...] = dot(pick[start : start + rows, :], tokens_ref[...]).astype(BF16)
+def route_pack_kernel(owners, holder, first, pieces, me_ref, index_hbm, storage_hbm, tokens_hbm, *refs):
+    outs, (dest_ref, pick, index, storage, tokens, sems) = refs[: len(pieces)], refs[len(pieces) :]
+    tiles = tokens.shape[0]
+    tile = tokens.shape[2]
+    small = [pltpu.make_async_copy(index_hbm, index, sems.at[tiles])]
+    small += [pltpu.make_async_copy(storage_hbm, storage, sems.at[tiles + 1])]
+    large = [
+        pltpu.make_async_copy(tokens_hbm.at[:, pl.ds(i * tile, tile)], tokens.at[i], sems.at[i])
+        for i in range(tiles)
+    ]
+    for copy in small + large:
+        copy.start()
+    for copy in small:
+        copy.wait()
+    me = me_ref[0]
+    owner, _, rank, late = routes(index[...], storage[...], holder, owners, me, first)
+    away = owner - me
+    away = jnp.where(away < 0, away + owners, away)
+    dest = jnp.where(late >= 0, (owners - 1) * first + late, (away - 1) * first + rank)
+    dest = jnp.where(away == 0, -1, dest)
+    dest_ref[...] = dest
+    pick[...] = one_hot(iota(pick.shape, 0) == dest)
+    for i, copy in enumerate(large):
+        copy.wait()
+        for ranges, out in zip(pieces, outs):
+            at = 0
+            for start, rows in ranges:
+                out[at : at + rows, i * tile : (i + 1) * tile] = dot(
+                    pick[start : start + rows, :], tokens[i]
+                ).astype(BF16)
+                at += rows
 
 
 def route_pack(me, index_row, storage_row, tokens, owners, holder, first, pieces):
     count, features = tokens.shape
-    tile = features // 4 if features % 512 == 0 else features
-    slots = max(start + rows for start, rows in pieces)
+    tiles = 4 if features % 512 == 0 else 1
+    slots = max(start + rows for ranges in pieces for start, rows in ranges)
+    in_hbm = pl.BlockSpec(memory_space=pltpu.HBM)
     return pl.pallas_call(
         functools.partial(route_pack_kernel, owners, holder, first, pieces),
-        grid=(features // tile,),
-        out_shape=[jax.ShapeDtypeStruct((rows, features), BF16) for _, rows in pieces]
+        out_shape=[jax.ShapeDtypeStruct((sum(r for _, r in ranges), features), BF16) for ranges in pieces]
         + [jax.ShapeDtypeStruct((1, count), jnp.int32)],
-        in_specs=[
-            IN_SMEM,
-            pl.BlockSpec((1, count), lambda i: (0, 0)),
-            pl.BlockSpec(storage_row.shape, lambda i: (0, 0)),
-            pl.BlockSpec((count, tile), lambda i: (0, i)),
+        in_specs=[IN_SMEM, in_hbm, in_hbm, in_hbm],
+        out_specs=[IN_VMEM] * (len(pieces) + 1),
+        scratch_shapes=[
+            pltpu.VMEM((slots, count), BF16),
+            pltpu.VMEM(index_row.shape, jnp.int32),
+            pltpu.VMEM(storage_row.shape, jnp.int32),
+            pltpu.VMEM((tiles, count, features // tiles), BF16),
+            pltpu.SemaphoreType.DMA((tiles + 2,)),
         ],
-        out_specs=[pl.BlockSpec((rows, tile), lambda i: (0, i)) for _, rows in pieces]
-        + [pl.BlockSpec((1, count), lambda i: (0, 0))],
-        scratch_shapes=[pltpu.VMEM((slots, count), BF16)],
         compiler_params=params(),
         cost_estimate=CHEAP,
         name="route_pack",
     )(me, index_row, storage_row, tokens)
 
 
+def repack_kernel(start, dest_ref, tokens_ref, out):
+    pick = one_hot(iota((out.shape[0], dest_ref.shape[1]), 0) + start == dest_ref[...])
+    out[...] = dot(pick, tokens_ref[...]).astype(BF16)
+
+
+def repack(dest, tokens, start, rows):
+    return pl.pallas_call(
+        functools.partial(repack_kernel, start),
+        out_shape=jax.ShapeDtypeStruct((rows, tokens.shape[1]), BF16),
+        in_specs=[IN_VMEM] * 2,
+        out_specs=IN_VMEM,
+        compiler_params=params(),
+        name="repack",
+    )(dest, tokens)
+
+
 def arrivals_kernel(owners, holder, first, late, me_ref, storage_ref, *refs):
     index_refs = refs[:owners]
-    ids_ref, late_ids_ref, home_ids_ref, more_ref = refs[owners:]
+    ids_ref, home_ids_ref, more_ref = refs[owners:]
     tokens = index_refs[0].shape[1]
     me = me_ref[0]
     most = jnp.zeros((1, 1), jnp.int32)
@@ -136,12 +167,9 @@
             home_ids_ref[...] = local
             continue
         known = jnp.broadcast_to(jnp.where(mine, local + 1, 0).astype(F32), (8, tokens)).astype(BF16)
-        slots = ids_ref.shape[1]
-        pick = one_hot(iota((slots, tokens), 0) == jnp.where(mine & (place < 0), rank, -1))
+        slot = jnp.where(place >= 0, first + place, rank)
+        pick = one_hot(iota((ids_ref.shape[1], tokens), 0) == jnp.where(mine, slot, -1))
         ids_ref[shift - 1 : shift, :] = dot(known, pick, ((1,), (1,)))[0:1, :].astype(jnp.int32) - 1
-        slots = late_ids_ref.shape[1]
-        pick = one_hot(iota((slots, tokens), 0) == jnp.where(mine, place, -1))
-        late_ids_ref[shift - 1 : shift, :] = dot(known, pick, ((1,), (1,)))[0:1, :].astype(jnp.int32) - 1
     more_ref[0] = (jnp.max(most) >= late).astype(jnp.int32)
 
 
@@ -150,13 +178,12 @@
     return pl.pallas_call(
         functools.partial(arrivals_kernel, owners, holder, first, late),
         out_shape=[
-            jax.ShapeDtypeStruct((owners - 1, first), jnp.int32),
-            jax.ShapeDtypeStruct((owners - 1, 2 * late), jnp.int32),
+            jax.ShapeDtypeStruct((owners - 1, first + 2 * late), jnp.int32),
             jax.ShapeDtypeStruct((1, count), jnp.int32),
             jax.ShapeDtypeStruct((1,), jnp.int32),
         ],
         in_specs=[IN_SMEM] + [IN_VMEM] * (1 + owners),
-        out_specs=[IN_VMEM, IN_VMEM, IN_VMEM, IN_SMEM],
+        out_specs=[IN_VMEM, IN_VMEM, IN_SMEM],
         compiler_params=params(),
         cost_estimate=CHEAP,
         name="arrivals",
@@ -242,11 +269,8 @@
     for k in range(1, terms):
         total = total + refs[k][...]
     dest = dest_ref[...]
-    returned = iter(refs[terms:])
-    for start, rows, copies in pieces:
-        piece = next(returned)[...]
-        for _ in range(copies - 1):
-            piece = piece + next(returned)[...]
+    for start, rows, sources in pieces:
+        piece = functools.reduce(jnp.add, [refs[terms + j][at : at + rows, :] for j, at in sources])
         pick = one_hot(iota((rows, dest.shape[1]), 0) + start == dest)
         high, rest = split_bf16(ADAPTER_SCALE * piece)
         total = total + (dot(pick, high, ((0,), (0,))) + dot(pick, rest, ((0,), (0,))))
@@ -272,10 +296,6 @@
 def shifted(x, shift):
     size = lax.axis_size("own")
     return along(x, [(i, (i + shift) % size) for i in range(size)])
-
-
-def beside(x):
-    return shifted(x, 1), shifted(x, -1)
 
 
 def opposite(before, after):
@@ -321,39 +341,39 @@
     shifts = list(range(1, owners))
     late_start = (owners - 1) * first
 
-    pieces = [((s - 1) * first, first) for s in shifts] + [(late_start + k * late, late) for k in range(2)]
+    mains = {s: ((s - 1) * first, first) for s in shifts}
+    pieces = [[mains[1], (late_start, late)], [mains[2]], [mains[3], (late_start, late)]]
     *packed, dest = route_pack(me, index_row, storage_row, tokens, owners, holder, first, pieces)
     index_rows = [index_row] + [shifted(index_row, s) for s in shifts]
     packed, index_rows = lax.optimization_barrier((packed, index_rows))
-    before, after = beside(packed[owners - 1])
-    rows_in = {s: shifted(packed[s - 1], s) for s in (1, 3, 2)}
-    ids, late_ids, home_ids, more = arrivals(me, storage_row, index_rows, owners, holder, first, late)
+    below, above, across = (shifted(packed[s - 1], s) for s in (1, 3, 2))
+    ids, home_ids, more = arrivals(me, storage_row, index_rows, owners, holder, first, late)
 
     def terms(ids, blocks, rows_in):
         lows = two_terms(low_rank(ids, down, blocks, rows_in, rank))
         done = up_project(ids, up, [block[:3] for block in blocks], *lows, holder)
         return [x if block[3] is None else shifted(x, -block[3]) for block, x in zip(blocks, done)]
 
+    def second(total):
+        x = repack(dest, tokens, late_start + late, late)
+        below, above = shifted(x, 1), shifted(x, 3)
+        blocks = [(s - 1, first + late, late, s) for s in shifts]
+        back = terms(ids, blocks, [[below], list(opposite(below, above)), [above]])
+        return gather_add(dest, [(late_start + late, late, [(j, 0) for j in range(3)])], [total], back, F32)
+
     base = base_terms(me_part, tokens, value_matrix, parts)
     (stays,) = terms(home_ids, [(0, 0, count, None)], [[tokens]])
     total = gather_add(dest, [], [*base, ADAPTER_SCALE * stays], [], F32)
-
-    def late_terms(k, before, far, after):
-        blocks = [(s - 1, k * late, late, s) for s in shifts]
-        return terms(late_ids, blocks, [[before], list(far), [after]])
-
-    def second(total, x):
-        before, after = beside(x)
-        back = late_terms(1, before, opposite(before, after), after)
-        return gather_add(dest, [(late_start + late, late, owners - 1)], [total], back, F32)
-
-    back = late_terms(0, before, opposite(before, after), after)
-    total = gather_add(dest, [(late_start, late, owners - 1)], [total], back, F32)
-    back = terms(ids, [(s - 1, 0, first, s) for s in (1, 3)], [[rows_in[1]], [rows_in[3]]])
-    total = gather_add(dest, [((s - 1) * first, first, 1) for s in (1, 3)], [total], back, F32)
-    total = lax.cond(more[0] > 0, second, lambda total, x: total, total, packed[owners])
-    back = terms(ids, [(1, 0, first, 2)], [[rows_in[2]]])
-    return gather_add(dest, [(first, first, 1)], [total], back, BF16)
+    below, above, total = lax.optimization_barrier((below, above, total))
+    passed = opposite(below[first:], above[first:])
+    back = terms(ids, [(s - 1, 0, first + late, s) for s in (1, 3)], [[below], [above]])
+    pieces = [(*mains[1], [(0, 0)]), (*mains[3], [(1, 0)]), (late_start, late, [(0, first), (1, first)])]
+    total = gather_add(dest, pieces, [total], back, F32)
+    back = terms(ids, [(1, first, late, 2)], [list(passed)])
+    total = gather_add(dest, [(late_start, late, [(0, 0)])], [total], back, F32)
+    total = lax.cond(more[0] > 0, second, lambda total: total, total)
+    back = terms(ids, [(1, 0, first, 2)], [[across]])
+    return gather_add(dest, [(*mains[2], [(0, 0)])], [total], back, BF16)
 
 
 def by_all_to_all(tokens, token_adapter_index, adapter_storage_row, value_matrix, down_stored, up_stored):

time: 118 us -> 110 us (0.932)
  waiting for transfers between devices: 58.3 us -> 47.6 us
  local copies, waits for them, and re-layouts: 6.28 us -> 3.31 us
  Pallas kernels: 16.1 us -> 19 us
  starting transfers between devices: 35.6 us -> 38.1 us
    ppermute x16 -> x12, waiting for transfers between devices: 55.2 us -> 32.5 us  [along(): return lax.ppermute(x, 'own', pairs)]
    ppermute x10, waiting for transfers between devices: 3.13 us -> 15.1 us  [partner(): lax.ppermute(x, 'tp', [(i, i ^ bit) for i in range(lax.axis_size('tp'))])]
    unnamed x28 -> x22, local copies, waits for them, and re-layouts: 6.24 us -> 2.22 us
    pallas_call x1, Pallas kernels: 1.38 us -> 3.12 us  [base_blocks(): pl.pallas_call(functools.partial(base_kernel, parts), out_shape=[jax.Shap...]
    ppermute x10, starting transfers between devices: 6.23 us -> 7.64 us  [partner(): lax.ppermute(x, 'tp', [(i, i ^ bit) for i in range(lax.axis_size('tp'))])]
    ppermute x16 -> x12, starting transfers between devices: 29.4 us -> 30.5 us  [along(): return lax.ppermute(x, 'own', pairs)]
  transfers between devices with their start and end apart: 26 -> 22, of which waited for: 7 -> 10; matrix products, arithmetic and copies ran while one was open for 0% -> 1% of each run, Pallas kernels for 13% -> 16%
where the time goes in v2:
time: 110 us; the launch traced here: 109 us
  waiting for transfers between devices  47.6 us (43%)
  starting transfers between devices  38.1 us (35%)
  Pallas kernels  19 us (17%)
  local copies, waits for them, and re-layouts  3.31 us (3%)
    ppermute x12, waiting for transfers between devices, along(): return lax.ppermute(x, 'own', pairs)  32.5 us
    ppermute x12, starting transfers between devices, along(): return lax.ppermute(x, 'own', pairs)  30.5 us
    ppermute x10, waiting for transfers between devices, partner(): lax.ppermute(x, 'tp', [(i, i ^ bit) for i in range(lax.axis_size('tp'))])  15.1 us
    ppermute x10, starting transfers between devices, partner(): lax.ppermute(x, 'tp', [(i, i ^ bit) for i in range(lax.axis_size('tp'))])  7.64 us
    pallas_call x4, Pallas kernels, low_rank(): pl.pallas_call(functools.partial(low_rank_kernel, blocks, copies, rank),...  5.35 us
    pallas_call x1, Pallas kernels, route_pack(): pl.pallas_call(functools.partial(route_pack_kernel, owners, holder, first...  4.62 us
    pallas_call x1, Pallas kernels, base_blocks(): pl.pallas_call(functools.partial(base_kernel, parts), out_shape=[jax.Shap...  3.12 us
    pallas_call x1, Pallas kernels, arrivals(): pl.pallas_call(functools.partial(arrivals_kernel, owners, holder, first,...  2.32 us
  transfers between devices with their start and end apart: 22, of which 10 were waited for; matrix products, arithmetic and copies ran while one was open for 1% of the time, Pallas kernels for 16%

profile of v2, /device:TPU:0, one launch (start us, length us, event | category | flops | bytes accessed | tf_op | source)
XLA Modules:
  0.0 109.2 jit_solution(18135284898623059224)
XLA Ops:
  0.0 5.0 %collective-permute-start.11 = (s32[1,512]{1,0:T(1,128)}, s32[1,512]{1,0:T(1,128)S(1)}, u32[]{:S(2)}, u32[]{:S(2)}) collective-permute-start(s32[1,512]{1,0:T(1,128)} %bitcast.9), channel_id=1, source_target_pairs={{0,12},{4,0},{8,4},{12,8},{1,13},{5,1},{9,5},{13,9},{2,14},{6,2},{... | collective-permute-start | bytes 6152 | tf_op jit(solution)/shard_map/ppermute | solution.py:293
  5.1 1.0 collective-permute-start.9
  6.1 0.7 copy-done.1
  6.8 0.7 copy-done.3
  7.4 4.6 %route_pack.1 = (bf16[256,2048]{1,0:T(8,128)(2,1)}, bf16[160,2048]{1,0:T(8,128)(2,1)S(1)}, bf16[256,2048]{1,0:T(8,128)(2,1)}, s32[1,512]{1,0:T(1,128)S(1)}) custom-call(s32[1]{0:T(128)} %bitcast.me_ref, s32[1,512]{1,0:T(1,128)S(1)} %bitcast.12, s32[1,32]{1,0:T(1,128)S(1)} %bitcast.14, bf16[512,2048]{1,0:T(8,128)(2,1)} %refs_0_.1), custom_call_target="tpu_custom_call" | custom-call | flops 1 | bytes 1 | tf_op jit(solution)/shard_map/route_pack/pallas_call | solution.py:117
  12.1 0.8 copy-done.5
  12.9 2.5 %collective-permute-start.12 = (bf16[256,2048]{1,0:T(8,128)(2,1)}, bf16[256,2048]{1,0:T(8,128)(2,1)S(1)}, u32[]{:S(2)}, u32[]{:S(2)}) collective-permute-start(bf16[256,2048]{1,0:T(8,128)(2,1)} %get-tuple-element.60), channel_id=1, source_target_pairs={{0,4},{4,8},{8,12},{12,0},{1,5},{5,9},{9,13},{13,1},{2,6},{6,10},{... | collective-permute-start | bytes 3145736 | tf_op jit(solution)/shard_map/ppermute | solution.py:293
  15.4 1.3 %collective-permute-start.13 = (bf16[256,2048]{1,0:T(8,128)(2,1)}, bf16[256,2048]{1,0:T(8,128)(2,1)}, u32[]{:S(2)}, u32[]{:S(2)}) collective-permute-start(bf16[256,2048]{1,0:T(8,128)(2,1)} %get-tuple-element.61), channel_id=1, source_target_pairs={{0,12},{4,0},{8,4},{12,8},{1,13},{5,1},{9,5},{13,9},{2,14},{6,2},{... | collective-permute-start | bytes 3145736 | tf_op jit(solution)/shard_map/ppermute | solution.py:293
  16.8 3.1 %base_blocks.1 = (f32[512,256]{1,0:T(8,128)S(1)}, f32[512,256]{1,0:T(8,128)S(1)}) custom-call(s32[1]{0:T(128)} %bitcast.4.me_ref, bf16[512,2048]{1,0:T(8,128)(2,1)} %refs_0_.1, bf16[2048,512]{1,0:T(8,128)(2,1)S(1)} %copy-done), custom_call_target="tpu_custom_call" | custom-call | flops 1 | bytes 1 | tf_op jit(solution)/shard_map/base_blocks/pallas_call | solution.py:255
  19.9 0.1 collective-permute-start.14
  20.0 2.3 %arrivals.1 = (s32[3,352]{1,0:T(4,128)S(1)}, s32[1,512]{1,0:T(1,128)S(1)}, s32[1]{0:T(128)}) custom-call(s32[1]{0:T(128)} %bitcast.me_ref, s32[1,32]{1,0:T(1,128)S(1)} %bitcast.15, s32[1,512]{1,0:T(1,128)S(1)} %bitcast.13, s32[1,512]{1,0:T(1,128)S(1)} %collective-permute-done.9.refs_1_, s32[1,512]{1,0:T(1,128)S(1)} %collective-permute-done.10.refs_2_, ...), custom_call_target="tpu_custom_call" | custom-call | flops 1 | bytes 1 | tf_op jit(solution)/shard_map/arrivals/pallas_call | solution.py:178
  22.4 1.3 %low_rank.6 = f32[64,512]{1,0:T(8,128)S(1)} custom-call(s32[1,512]{1,0:T(1,128)S(1)} %get-tuple-element.64.ids_ref, bf16[512,2048]{1,0:T(8,128)(2,1)S(1)} %bitcast.16, bf16[512,2048]{1,0:T(8,128)(2,1)S(1)} %copy-done.8), custom_call_target="tpu_custom_call" | custom-call | flops 1 | bytes 1 | tf_op jit(solution)/shard_map/low_rank/pallas_call | solution.py:209
  23.7 0.5 collective-permute-start.16
  24.2 0.2 collective-permute-start.27
  24.4 0.8 collective-permute-done.16
  25.2 1.6 %collective-permute-start.17 = (f32[64,512]{1,0:T(8,128)S(1)}, f32[64,512]{1,0:T(8,128)S(1)}, u32[]{:S(2)}, u32[]{:S(2)}) collective-permute-start(f32[64,512]{1,0:T(8,128)S(1)} %add.19.a_ref), channel_id=1, source_target_pairs={{0,2},{1,3},{2,0},{3,1},{4,6},{5,7},{6,4},{7,5},{8,10},{9,11},{10,... | collective-permute-start | bytes 393224 | tf_op jit(solution)/shard_map/ppermute | solution.py:306
  26.9 0.6 collective-permute-start.15
  27.5 4.1 %collective-permute-done.17.b_ref = f32[64,512]{1,0:T(8,128)S(1)} collective-permute-done((f32[64,512]{1,0:T(8,128)S(1)}, f32[64,512]{1,0:T(8,128)S(1)}, u32[]{:S(2)}, u32[]{:S(2)}) %collective-permute-start.17) | collective-permute-done | bytes 131104 | tf_op jit(solution)/shard_map/ppermute | solution.py:306
  31.6 0.5 up_project.6
  32.2 4.5 %collective-permute-done.15.refs_1_ = f32[512,128]{1,0:T(8,128)S(1)} collective-permute-done((f32[512,128]{1,0:T(8,128)S(1)}, f32[512,128]{1,0:T(8,128)S(1)}, u32[]{:S(2)}, u32[]{:S(2)}) %collective-permute-start.15) | collective-permute-done | bytes 262176 | tf_op jit(solution)/shard_map/ppermute | solution.py:306
  36.7 4.3 %collective-permute-done.12.refs_0_ = bf16[256,2048]{1,0:T(8,128)(2,1)S(1)} collective-permute-done((bf16[256,2048]{1,0:T(8,128)(2,1)}, bf16[256,2048]{1,0:T(8,128)(2,1)S(1)}, u32[]{:S(2)}, u32[]{:S(2)}) %collective-permute-start.12) | collective-permute-done | bytes 1048608 | tf_op jit(solution)/shard_map/ppermute | solution.py:293
  41.1 20.8 %collective-permute-done.13.refs_1_ = bf16[256,2048]{1,0:T(8,128)(2,1)} collective-permute-done((bf16[256,2048]{1,0:T(8,128)(2,1)}, bf16[256,2048]{1,0:T(8,128)(2,1)}, u32[]{:S(2)}, u32[]{:S(2)}) %collective-permute-start.13) | collective-permute-done | bytes 1048608 | tf_op jit(solution)/shard_map/ppermute | solution.py:293
  61.9 1.0 slice.7
  62.9 14.0 %collective-permute-start.22 = (bf16[96,2048]{1,0:T(8,128)(2,1)S(1)}, bf16[96,2048]{1,0:T(8,128)(2,1)S(1)}, u32[]{:S(2)}, u32[]{:S(2)}) collective-permute-start(bf16[96,2048]{1,0:T(8,128)(2,1)S(1)} %slice.6), channel_id=1, source_target_pairs={{0,4},{8,12},{1,5},{9,13},{2,6},{10,14},{3,7},{11,15},{16,20},{24,... | collective-permute-start | bytes 1179656 | tf_op jit(solution)/shard_map/ppermute | solution.py:293
  76.9 1.3 %collective-permute-start.23 = (bf16[96,2048]{1,0:T(8,128)(2,1)S(1)}, bf16[96,2048]{1,0:T(8,128)(2,1)S(1)}, u32[]{:S(2)}, u32[]{:S(2)}) collective-permute-start(bf16[96,2048]{1,0:T(8,128)(2,1)S(1)} %slice.7), channel_id=1, source_target_pairs={{4,0},{12,8},{5,1},{13,9},{6,2},{14,10},{7,3},{15,11},{20,16},{28,... | collective-permute-start | bytes 1179656 | tf_op jit(solution)/shard_map/ppermute | solution.py:293
  78.2 2.5 %low_rank.7 = f32[128,256]{1,0:T(8,128)S(1)} custom-call(s32[3,352]{1,0:T(4,128)S(1)} %get-tuple-element.66.ids_ref, bf16[512,2048]{1,0:T(8,128)(2,1)S(1)} %bitcast.17, bf16[256,2048]{1,0:T(8,128)(2,1)S(1)} %collective-permute-done.12.refs_0_, bf16[256,2048]{1,0:T(8,128)(2,1)} %collective-permute-done.13.refs_1_), custom_call_target="tpu_custom_call" | custom-call | flops 1 | bytes 1 | tf_op jit(solution)/shard_map/low_rank/pallas_call | solution.py:209
  80.7 0.1 collective-permute-start.18
  80.8 1.3 %collective-permute-done.18 = f32[128,256]{1,0:T(8,128)S(1)} collective-permute-done((f32[128,256]{1,0:T(8,128)S(1)}, f32[128,256]{1,0:T(8,128)S(1)}, u32[]{:S(2)}, u32[]{:S(2)}) %collective-permute-start.18) | collective-permute-done | bytes 131104 | tf_op jit(solution)/shard_map/ppermute | solution.py:306
  82.2 1.6 %collective-permute-start.19 = (f32[128,256]{1,0:T(8,128)S(1)}, f32[128,256]{1,0:T(8,128)S(1)}, u32[]{:S(2)}, u32[]{:S(2)}) collective-permute-start(f32[128,256]{1,0:T(8,128)S(1)} %add.20.a_ref), channel_id=1, source_target_pairs={{0,2},{1,3},{2,0},{3,1},{4,6},{5,7},{6,4},{7,5},{8,10},{9,11},{10,... | collective-permute-start | bytes 393224 | tf_op jit(solution)/shard_map/ppermute | solution.py:306
  83.7 6.0 %collective-permute-done.27.refs_0_ = bf16[160,2048]{1,0:T(8,128)(2,1)S(1)} collective-permute-done((bf16[160,2048]{1,0:T(8,128)(2,1)S(1)}, bf16[160,2048]{1,0:T(8,128)(2,1)S(1)}, u32[]{:S(2)}, u32[]{:S(2)}) %collective-permute-start.27) | collective-permute-done | bytes 655392 | tf_op jit(solution)/shard_map/ppermute | solution.py:293
  89.7 0.7 low_rank.9
  90.4 0.1 collective-permute-start.28
  90.5 0.5 up_project.7
  91.0 1.4 %collective-permute-start.20 = (f32[256,128]{1,0:T(8,128)S(1)}, f32[256,128]{1,0:T(8,128)S(1)}, u32[]{:S(2)}, u32[]{:S(2)}) collective-permute-start(f32[256,128]{1,0:T(8,128)S(1)} %get-tuple-element.69), channel_id=1, source_target_pairs={{0,12},{4,0},{8,4},{12,8},{1,13},{5,1},{9,5},{13,9},{2,14},{6,2},{... | collective-permute-start | bytes 393224 | tf_op jit(solution)/shard_map/ppermute | solution.py:293
  92.4 0.7 collective-permute-start.21
  93.1 1.6 %collective-permute-start.29 = (f32[64,160]{1,0:T(8,128)S(1)}, f32[64,160]{1,0:T(8,128)S(1)}, u32[]{:S(2)}, u32[]{:S(2)}) collective-permute-start(f32[64,160]{1,0:T(8,128)S(1)} %add.22.a_ref), channel_id=1, source_target_pairs={{0,2},{1,3},{2,0},{3,1},{4,6},{5,7},{6,4},{7,5},{8,10},{9,11},{10,... | collective-permute-start | bytes 122888 | tf_op jit(solution)/shard_map/ppermute | solution.py:306
  94.7 0.8 low_rank.8
  95.5 1.9 %collective-permute-done.29.b_ref = f32[64,160]{1,0:T(8,128)S(1)} collective-permute-done((f32[64,160]{1,0:T(8,128)S(1)}, f32[64,160]{1,0:T(8,128)S(1)}, u32[]{:S(2)}, u32[]{:S(2)}) %collective-permute-start.29) | collective-permute-done | bytes 40992 | tf_op jit(solution)/shard_map/ppermute | solution.py:306
  97.4 0.3 up_project.9
  97.7 0.1 collective-permute-start.30
  97.8 1.6 %collective-permute-start.25 = (f32[64,96]{1,0:T(8,128)S(1)}, f32[64,96]{1,0:T(8,128)S(1)}, u32[]{:S(2)}, u32[]{:S(2)}) collective-permute-start(f32[64,96]{1,0:T(8,128)S(1)} %add.21.a_ref), channel_id=1, source_target_pairs={{0,2},{1,3},{2,0},{3,1},{4,6},{5,7},{6,4},{7,5},{8,10},{9,11},{10,... | collective-permute-start | bytes 73736 | tf_op jit(solution)/shard_map/ppermute | solution.py:306
  99.4 2.4 %collective-permute-done.25.b_ref = f32[64,96]{1,0:T(8,128)S(1)} collective-permute-done((f32[64,96]{1,0:T(8,128)S(1)}, f32[64,96]{1,0:T(8,128)S(1)}, u32[]{:S(2)}, u32[]{:S(2)}) %collective-permute-start.25) | collective-permute-done | bytes 24608 | tf_op jit(solution)/shard_map/ppermute | solution.py:306
  101.8 0.4 up_project.8
  102.3 3.0 %collective-permute-start.26 = (f32[96,128]{1,0:T(8,128)S(1)}, f32[96,128]{1,0:T(8,128)S(1)}, u32[]{:S(2)}, u32[]{:S(2)}) collective-permute-start(f32[96,128]{1,0:T(8,128)S(1)} %up_project.8), channel_id=1, source_target_pairs={{0,8},{4,12},{8,0},{12,4},{1,9},{5,13},{9,1},{13,5},{2,10},{6,14},... | collective-permute-start | bytes 147464 | tf_op jit(solution)/shard_map/ppermute | solution.py:293
  105.9 0.6 gather_add.7.refs_0_
  106.5 1.4 %collective-permute-done.26.refs_1_ = f32[96,128]{1,0:T(8,128)S(1)} collective-permute-done((f32[96,128]{1,0:T(8,128)S(1)}, f32[96,128]{1,0:T(8,128)S(1)}, u32[]{:S(2)}, u32[]{:S(2)}) %collective-permute-start.26) | collective-permute-done | bytes 49184 | tf_op jit(solution)/shard_map/ppermute | solution.py:293
  107.9 0.3 gather_add.8
  108.2 1.0 gather_add.9
  (43 shorter events, 0.4 us)
Async XLA Ops:
  0.0 16.8 %copy-start = (bf16[2048,512]{1,0:T(8,128)(2,1)S(1)}, bf16[2048,512]{1,0:T(8,128)(2,1)}, u32[]{:S(2)}) copy-start(bf16[2048,512]{1,0:T(8,128)(2,1)} %value_ref.1) | copy-start | bytes 6291460
  0.0 12.9 %collective-permute-start.11 = (s32[1,512]{1,0:T(1,128)}, s32[1,512]{1,0:T(1,128)S(1)}, u32[]{:S(2)}, u32[]{:S(2)}) collective-permute-start(s32[1,512]{1,0:T(1,128)} %bitcast.9), channel_id=1, source_target_pairs={{0,12},{4,0},{8,4},{12,8},{1,13},{5,1},{9,5},{13,9},{2,14},{6,2},{... | collective-permute-start | bytes 6152 | tf_op jit(solution)/shard_map/ppermute | solution.py:293
  5.1 7.8 %collective-permute-start.10 = (s32[1,512]{1,0:T(1,128)}, s32[1,512]{1,0:T(1,128)S(1)}, u32[]{:S(2)}, u32[]{:S(2)}) collective-permute-start(s32[1,512]{1,0:T(1,128)} %bitcast.10), channel_id=1, source_target_pairs={{0,8},{4,12},{8,0},{12,4},{1,9},{5,13},{9,1},{13,5},{2,10},{6,14},... | collective-permute-start | bytes 6152 | tf_op jit(solution)/shard_map/ppermute | solution.py:293
  5.1 7.8 %collective-permute-start.9 = (s32[1,512]{1,0:T(1,128)}, s32[1,512]{1,0:T(1,128)S(1)}, u32[]{:S(2)}, u32[]{:S(2)}) collective-permute-start(s32[1,512]{1,0:T(1,128)} %bitcast.11), channel_id=1, source_target_pairs={{0,4},{4,8},{8,12},{12,0},{1,5},{5,9},{9,13},{13,1},{2,6},{6,10},{... | collective-permute-start | bytes 6152 | tf_op jit(solution)/shard_map/ppermute | solution.py:293
  6.1 0.7 copy-start.1
  6.8 0.7 copy-start.3
  12.1 0.8 copy-start.5
  12.9 28.2 %collective-permute-start.12 = (bf16[256,2048]{1,0:T(8,128)(2,1)}, bf16[256,2048]{1,0:T(8,128)(2,1)S(1)}, u32[]{:S(2)}, u32[]{:S(2)}) collective-permute-start(bf16[256,2048]{1,0:T(8,128)(2,1)} %get-tuple-element.60), channel_id=1, source_target_pairs={{0,4},{4,8},{8,12},{12,0},{1,5},{5,9},{9,13},{13,1},{2,6},{6,10},{... | collective-permute-start | bytes 3145736 | tf_op jit(solution)/shard_map/ppermute | solution.py:293
  15.4 46.4 %collective-permute-start.13 = (bf16[256,2048]{1,0:T(8,128)(2,1)}, bf16[256,2048]{1,0:T(8,128)(2,1)}, u32[]{:S(2)}, u32[]{:S(2)}) collective-permute-start(bf16[256,2048]{1,0:T(8,128)(2,1)} %get-tuple-element.61), channel_id=1, source_target_pairs={{0,12},{4,0},{8,4},{12,8},{1,13},{5,1},{9,5},{13,9},{2,14},{6,2},{... | collective-permute-start | bytes 3145736 | tf_op jit(solution)/shard_map/ppermute | solution.py:293
  16.8 3.2 %copy-start.2 = (s32[512]{0:T(512)S(1)}, s32[512]{0:T(512)}, u32[]{:S(2)}) copy-start(s32[512]{0:T(512)} %param.9) | copy-start | bytes 6148
  16.8 3.2 %copy-start.4 = (s32[32]{0:T(128)S(1)}, s32[32]{0:T(128)}, u32[]{:S(2)}) copy-start(s32[32]{0:T(128)} %param.10) | copy-start | bytes 388
  16.8 5.6 %copy-start.7 = (bf16[8,2048,64]{1,2,0:T(8,128)(2,1)S(1)}, bf16[8,2048,64]{1,2,0:T(8,128)(2,1)}, u32[]{:S(2)}) copy-start(bf16[8,2048,64]{1,2,0:T(8,128)(2,1)} %param.12) | copy-start | bytes 6291460
  16.8 5.6 %copy-start.8 = (bf16[512,2048]{1,0:T(8,128)(2,1)S(1)}, bf16[512,2048]{1,0:T(8,128)(2,1)}, u32[]{:S(2)}) copy-start(bf16[512,2048]{1,0:T(8,128)(2,1)} %refs_0_.1) | copy-start | bytes 6291460
  19.9 6.9 %collective-permute-start.14 = (f32[512,256]{1,0:T(8,128)S(1)}, f32[512,256]{1,0:T(8,128)S(1)}, u32[]{:S(2)}, u32[]{:S(2)}) collective-permute-start(f32[512,256]{1,0:T(8,128)S(1)} %get-tuple-element.63), channel_id=1, source_target_pairs={{0,1},{1,0},{2,3},{3,2},{4,5},{5,4},{6,7},{7,6},{8,9},{9,8},{10,11... | collective-permute-start | bytes 1572872 | tf_op jit(solution)/shard_map/ppermute | solution.py:306
  22.4 1.9 %copy-start.6 = (bf16[160,2048]{1,0:T(8,128)(2,1)S(1)}, bf16[160,2048]{1,0:T(8,128)(2,1)}, u32[]{:S(2)}) copy-start(bf16[160,2048]{1,0:T(8,128)(2,1)} %copy-done.5) | copy-start | bytes 1966084
  23.7 8.0 %copy-start.10 = (bf16[8,64,128]{2,1,0:T(8,128)(2,1)S(1)}, bf16[8,64,128]{2,1,0:T(8,128)(2,1)}, u32[]{:S(2)}) copy-start(bf16[8,64,128]{2,1,0:T(8,128)(2,1)} %param.13) | copy-start | bytes 393220
  23.7 1.5 %collective-permute-start.16 = (f32[64,512]{1,0:T(8,128)S(1)}, f32[64,512]{1,0:T(8,128)S(1)}, u32[]{:S(2)}, u32[]{:S(2)}) collective-permute-start(f32[64,512]{1,0:T(8,128)S(1)} %low_rank.6), channel_id=1, source_target_pairs={{0,1},{1,0},{2,3},{3,2},{4,5},{5,4},{6,7},{7,6},{8,9},{9,8},{10,11... | collective-permute-start | bytes 393224 | tf_op jit(solution)/shard_map/ppermute | solution.py:306
  24.2 65.4 %collective-permute-start.27 = (bf16[160,2048]{1,0:T(8,128)(2,1)S(1)}, bf16[160,2048]{1,0:T(8,128)(2,1)S(1)}, u32[]{:S(2)}, u32[]{:S(2)}) collective-permute-start(bf16[160,2048]{1,0:T(8,128)(2,1)S(1)} %copy-done.6), channel_id=1, source_target_pairs={{0,8},{4,12},{8,0},{12,4},{1,9},{5,13},{9,1},{13,5},{2,10},{6,14},... | collective-permute-start | bytes 1966088 | tf_op jit(solution)/shard_map/ppermute | solution.py:293
  25.2 6.4 %collective-permute-start.17 = (f32[64,512]{1,0:T(8,128)S(1)}, f32[64,512]{1,0:T(8,128)S(1)}, u32[]{:S(2)}, u32[]{:S(2)}) collective-permute-start(f32[64,512]{1,0:T(8,128)S(1)} %add.19.a_ref), channel_id=1, source_target_pairs={{0,2},{1,3},{2,0},{3,1},{4,6},{5,7},{6,4},{7,5},{8,10},{9,11},{10,... | collective-permute-start | bytes 393224 | tf_op jit(solution)/shard_map/ppermute | solution.py:306
  26.9 9.8 %collective-permute-start.15 = (f32[512,128]{1,0:T(8,128)S(1)}, f32[512,128]{1,0:T(8,128)S(1)}, u32[]{:S(2)}, u32[]{:S(2)}) collective-permute-start(f32[512,128]{1,0:T(8,128)S(1)} %get-tuple-element.72), channel_id=1, source_target_pairs={{0,2},{1,3},{2,0},{3,1},{4,6},{5,7},{6,4},{7,5},{8,10},{9,11},{10,... | collective-permute-start | bytes 786440 | tf_op jit(solution)/shard_map/ppermute | solution.py:306
  62.9 31.7 %collective-permute-start.22 = (bf16[96,2048]{1,0:T(8,128)(2,1)S(1)}, bf16[96,2048]{1,0:T(8,128)(2,1)S(1)}, u32[]{:S(2)}, u32[]{:S(2)}) collective-permute-start(bf16[96,2048]{1,0:T(8,128)(2,1)S(1)} %slice.6), channel_id=1, source_target_pairs={{0,4},{8,12},{1,5},{9,13},{2,6},{10,14},{3,7},{11,15},{16,20},{24,... | collective-permute-start | bytes 1179656 | tf_op jit(solution)/shard_map/ppermute | solution.py:293
  76.9 17.7 %collective-permute-start.23 = (bf16[96,2048]{1,0:T(8,128)(2,1)S(1)}, bf16[96,2048]{1,0:T(8,128)(2,1)S(1)}, u32[]{:S(2)}, u32[]{:S(2)}) collective-permute-start(bf16[96,2048]{1,0:T(8,128)(2,1)S(1)} %slice.7), channel_id=1, source_target_pairs={{4,0},{12,8},{5,1},{13,9},{6,2},{14,10},{7,3},{15,11},{20,16},{28,... | collective-permute-start | bytes 1179656 | tf_op jit(solution)/shard_map/ppermute | solution.py:293
  80.7 1.4 %collective-permute-start.18 = (f32[128,256]{1,0:T(8,128)S(1)}, f32[128,256]{1,0:T(8,128)S(1)}, u32[]{:S(2)}, u32[]{:S(2)}) collective-permute-start(f32[128,256]{1,0:T(8,128)S(1)} %low_rank.7), channel_id=1, source_target_pairs={{0,1},{1,0},{2,3},{3,2},{4,5},{5,4},{6,7},{7,6},{8,9},{9,8},{10,11... | collective-permute-start | bytes 393224 | tf_op jit(solution)/shard_map/ppermute | solution.py:306
  82.2 8.3 %collective-permute-start.19 = (f32[128,256]{1,0:T(8,128)S(1)}, f32[128,256]{1,0:T(8,128)S(1)}, u32[]{:S(2)}, u32[]{:S(2)}) collective-permute-start(f32[128,256]{1,0:T(8,128)S(1)} %add.20.a_ref), channel_id=1, source_target_pairs={{0,2},{1,3},{2,0},{3,1},{4,6},{5,7},{6,4},{7,5},{8,10},{9,11},{10,... | collective-permute-start | bytes 393224 | tf_op jit(solution)/shard_map/ppermute | solution.py:306
  90.4 2.7 %collective-permute-start.28 = (f32[64,160]{1,0:T(8,128)S(1)}, f32[64,160]{1,0:T(8,128)S(1)}, u32[]{:S(2)}, u32[]{:S(2)}) collective-permute-start(f32[64,160]{1,0:T(8,128)S(1)} %low_rank.9), channel_id=1, source_target_pairs={{0,1},{1,0},{2,3},{3,2},{4,5},{5,4},{6,7},{7,6},{8,9},{9,8},{10,11... | collective-permute-start | bytes 122888 | tf_op jit(solution)/shard_map/ppermute | solution.py:306
  91.0 14.9 %collective-permute-start.20 = (f32[256,128]{1,0:T(8,128)S(1)}, f32[256,128]{1,0:T(8,128)S(1)}, u32[]{:S(2)}, u32[]{:S(2)}) collective-permute-start(f32[256,128]{1,0:T(8,128)S(1)} %get-tuple-element.69), channel_id=1, source_target_pairs={{0,12},{4,0},{8,4},{12,8},{1,13},{5,1},{9,5},{13,9},{2,14},{6,2},{... | collective-permute-start | bytes 393224 | tf_op jit(solution)/shard_map/ppermute | solution.py:293
  92.4 13.5 %collective-permute-start.21 = (f32[256,128]{1,0:T(8,128)S(1)}, f32[256,128]{1,0:T(8,128)S(1)}, u32[]{:S(2)}, u32[]{:S(2)}) collective-permute-start(f32[256,128]{1,0:T(8,128)S(1)} %get-tuple-element.70), channel_id=1, source_target_pairs={{0,4},{4,8},{8,12},{12,0},{1,5},{5,9},{9,13},{13,1},{2,6},{6,10},{... | collective-permute-start | bytes 393224 | tf_op jit(solution)/shard_map/ppermute | solution.py:293
  93.1 15.0 %copy-start.9 = (bf16[512,2048]{1,0:T(8,128)(2,1)S(1)}, bf16[512,2048]{1,0:T(8,128)(2,1)}, u32[]{:S(2)}) copy-start(bf16[512,2048]{1,0:T(8,128)(2,1)} %refs_0_.1) | copy-start | bytes 6291460
  93.1 4.3 %collective-permute-start.29 = (f32[64,160]{1,0:T(8,128)S(1)}, f32[64,160]{1,0:T(8,128)S(1)}, u32[]{:S(2)}, u32[]{:S(2)}) collective-permute-start(f32[64,160]{1,0:T(8,128)S(1)} %add.22.a_ref), channel_id=1, source_target_pairs={{0,2},{1,3},{2,0},{3,1},{4,6},{5,7},{6,4},{7,5},{8,10},{9,11},{10,... | collective-permute-start | bytes 122888 | tf_op jit(solution)/shard_map/ppermute | solution.py:306
  95.5 2.3 %collective-permute-start.24 = (f32[64,96]{1,0:T(8,128)S(1)}, f32[64,96]{1,0:T(8,128)S(1)}, u32[]{:S(2)}, u32[]{:S(2)}) collective-permute-start(f32[64,96]{1,0:T(8,128)S(1)} %low_rank.8), channel_id=1, source_target_pairs={{0,1},{1,0},{2,3},{3,2},{4,5},{5,4},{6,7},{7,6},{8,9},{9,8},{10,11... | collective-permute-start | bytes 73736 | tf_op jit(solution)/shard_map/ppermute | solution.py:306
  97.7 10.4 %collective-permute-start.30 = (f32[160,128]{1,0:T(8,128)S(1)}, f32[160,128]{1,0:T(8,128)S(1)}, u32[]{:S(2)}, u32[]{:S(2)}) collective-permute-start(f32[160,128]{1,0:T(8,128)S(1)} %up_project.9), channel_id=1, source_target_pairs={{0,8},{4,12},{8,0},{12,4},{1,9},{5,13},{9,1},{13,5},{2,10},{6,14},... | collective-permute-start | bytes 245768 | tf_op jit(solution)/shard_map/ppermute | solution.py:293
  97.8 4.0 %collective-permute-start.25 = (f32[64,96]{1,0:T(8,128)S(1)}, f32[64,96]{1,0:T(8,128)S(1)}, u32[]{:S(2)}, u32[]{:S(2)}) collective-permute-start(f32[64,96]{1,0:T(8,128)S(1)} %add.21.a_ref), channel_id=1, source_target_pairs={{0,2},{1,3},{2,0},{3,1},{4,6},{5,7},{6,4},{7,5},{8,10},{9,11},{10,... | collective-permute-start | bytes 73736 | tf_op jit(solution)/shard_map/ppermute | solution.py:306
  102.3 5.6 %collective-permute-start.26 = (f32[96,128]{1,0:T(8,128)S(1)}, f32[96,128]{1,0:T(8,128)S(1)}, u32[]{:S(2)}, u32[]{:S(2)}) collective-permute-start(f32[96,128]{1,0:T(8,128)S(1)} %up_project.8), channel_id=1, source_target_pairs={{0,8},{4,12},{8,0},{12,4},{1,9},{5,13},{9,1},{13,5},{2,10},{6,14},... | collective-permute-start | bytes 147464 | tf_op jit(solution)/shard_map/ppermute | solution.py:293

commit v3 on v2

--- a/solution.py
+++ b/solution.py
@@ -9,6 +9,7 @@
 
 CAP = 4
 ADAPTER_SCALE = 0.5
+TAGS = 16
 LINE = 4
 BF16 = jnp.bfloat16
 F32 = jnp.float32
@@ -76,10 +77,21 @@
     return owner, storage, rank.astype(jnp.int32), late_place
 
 
-def route_pack_kernel(owners, holder, first, pieces, me_ref, index_hbm, storage_hbm, tokens_hbm, *refs):
-    outs, (dest_ref, pick, index, storage, tokens, sems) = refs[: len(pieces)], refs[len(pieces) :]
-    tiles = tokens.shape[0]
-    tile = tokens.shape[2]
+def known_adapters(storage, picks, flag):
+    tokens = storage.shape[1]
+    known = jnp.broadcast_to((storage + 1).astype(F32), (8, tokens)).astype(BF16)
+    width = picks[0].shape[0]
+    which = iota((TAGS, width), 0)
+    tags = jnp.where(which == TAGS - 1, flag, 0.0)
+    for k, pick in enumerate(picks):
+        row = dot(known, pick, ((1,), (1,)))
+        tags = jnp.where(which == k, jnp.concatenate([row] * (TAGS // 8), axis=0), tags)
+    return tags.astype(BF16)
+
+
+def route_pack_kernel(owners, holder, first, late, me_ref, index_hbm, storage_hbm, tokens_hbm, *refs):
+    outs, (dest_ref, home_ids_ref, more_ref, picks, index, storage, tokens, sems) = refs[:3], refs[3:]
+    tiles, _, tile = tokens.shape
     small = [pltpu.make_async_copy(index_hbm, index, sems.at[tiles])]
     small += [pltpu.make_async_copy(storage_hbm, storage, sems.at[tiles + 1])]
     large = [
@@ -91,37 +103,47 @@
     for copy in small:
         copy.wait()
     me = me_ref[0]
-    owner, _, rank, late = routes(index[...], storage[...], holder, owners, me, first)
+    owner, row, rank, place = routes(index[...], storage[...], holder, owners, me, first)
+    home_ids_ref[...] = jnp.where(owner == me, row - me * holder, -1)
     away = owner - me
     away = jnp.where(away < 0, away + owners, away)
-    dest = jnp.where(late >= 0, (owners - 1) * first + late, (away - 1) * first + rank)
-    dest = jnp.where(away == 0, -1, dest)
-    dest_ref[...] = dest
-    pick[...] = one_hot(iota(pick.shape, 0) == dest)
+    dest = jnp.where(place >= 0, (owners - 1) * first + place, (away - 1) * first + rank)
+    dest_ref[...] = jnp.where(away == 0, -1, dest)
+    more = (jnp.max(place) >= late).astype(jnp.int32)
+    more_ref[0] = more
+    for s in range(1, owners):
+        slot = jnp.where(place >= 0, first + place, jnp.where(away == s, rank, -1))
+        picks[s - 1] = one_hot(iota(picks.shape[1:], 0) == slot)
+    tags = known_adapters(row, [picks[s - 1] for s in range(1, owners)], more.astype(F32))
+    size = first + late
+    for out in (outs[0], outs[2]):
+        out[size:, :] = jnp.zeros((TAGS, out.shape[1]), BF16)
+        out[size:, 0:size] = tags
     for i, copy in enumerate(large):
         copy.wait()
-        for ranges, out in zip(pieces, outs):
-            at = 0
-            for start, rows in ranges:
-                out[at : at + rows, i * tile : (i + 1) * tile] = dot(
-                    pick[start : start + rows, :], tokens[i]
-                ).astype(BF16)
-                at += rows
-
-
-def route_pack(me, index_row, storage_row, tokens, owners, holder, first, pieces):
+        at = slice(i * tile, (i + 1) * tile)
+        for s, rows in ((1, size), (3, first), (2, first)):
+            if s == 3:
+                outs[2][0:first, at] = dot(picks[2, 0:first, :], tokens[i]).astype(BF16)
+                outs[2][first:size, at] = outs[0][first:size, at]
+            else:
+                outs[s - 1][0:rows, at] = dot(picks[s - 1, 0:rows, :], tokens[i]).astype(BF16)
+
+
+def route_pack(me, index_row, storage_row, tokens, owners, holder, first, late):
     count, features = tokens.shape
     tiles = 4 if features % 512 == 0 else 1
-    slots = max(start + rows for ranges in pieces for start, rows in ranges)
     in_hbm = pl.BlockSpec(memory_space=pltpu.HBM)
-    return pl.pallas_call(
-        functools.partial(route_pack_kernel, owners, holder, first, pieces),
-        out_shape=[jax.ShapeDtypeStruct((sum(r for _, r in ranges), features), BF16) for ranges in pieces]
-        + [jax.ShapeDtypeStruct((1, count), jnp.int32)],
+    long = first + late + TAGS
+    return pl.pallas_call(
+        functools.partial(route_pack_kernel, owners, holder, first, late),
+        out_shape=[jax.ShapeDtypeStruct((rows, features), BF16) for rows in (long, first, long)]
+        + [jax.ShapeDtypeStruct((1, count), jnp.int32)] * 2
+        + [jax.ShapeDtypeStruct((1,), jnp.int32)],
         in_specs=[IN_SMEM, in_hbm, in_hbm, in_hbm],
-        out_specs=[IN_VMEM] * (len(pieces) + 1),
+        out_specs=[IN_VMEM] * 5 + [IN_SMEM],
         scratch_shapes=[
-            pltpu.VMEM((slots, count), BF16),
+            pltpu.VMEM((owners - 1, first + late, count), BF16),
             pltpu.VMEM(index_row.shape, jnp.int32),
             pltpu.VMEM(storage_row.shape, jnp.int32),
             pltpu.VMEM((tiles, count, features // tiles), BF16),
@@ -133,108 +155,108 @@
     )(me, index_row, storage_row, tokens)
 
 
-def repack_kernel(start, dest_ref, tokens_ref, out):
-    pick = one_hot(iota((out.shape[0], dest_ref.shape[1]), 0) + start == dest_ref[...])
-    out[...] = dot(pick, tokens_ref[...]).astype(BF16)
-
-
-def repack(dest, tokens, start, rows):
+def repack_kernel(start, index_ref, storage_ref, dest_ref, tokens_ref, out):
+    rows = out.shape[0] - TAGS
+    pick = one_hot(iota((rows, dest_ref.shape[1]), 0) + start == dest_ref[...])
+    out[0:rows, :] = dot(pick, tokens_ref[...]).astype(BF16)
+    out[rows:, :] = jnp.zeros((TAGS, out.shape[1]), BF16)
+    out[rows:, 0:rows] = known_adapters(storage_of(index_ref[...], storage_ref[...]), [pick], 0.0)
+
+
+def repack(index_row, storage_row, dest, tokens, start, rows):
     return pl.pallas_call(
         functools.partial(repack_kernel, start),
-        out_shape=jax.ShapeDtypeStruct((rows, tokens.shape[1]), BF16),
-        in_specs=[IN_VMEM] * 2,
+        out_shape=jax.ShapeDtypeStruct((rows + TAGS, tokens.shape[1]), BF16),
+        in_specs=[IN_VMEM] * 4,
         out_specs=IN_VMEM,
         compiler_params=params(),
         name="repack",
-    )(dest, tokens)
-
-
-def arrivals_kernel(owners, holder, first, late, me_ref, storage_ref, *refs):
-    index_refs = refs[:owners]
-    ids_ref, home_ids_ref, more_ref = refs[owners:]
-    tokens = index_refs[0].shape[1]
-    me = me_ref[0]
-    most = jnp.zeros((1, 1), jnp.int32)
-    for shift in range(owners):
-        group = lax.rem(me - shift + owners, owners)
-        owner, storage, rank, place = routes(
-            index_refs[shift][...], storage_ref[...], holder, owners, group, first
-        )
-        most = jnp.maximum(most, jnp.max(place, axis=1, keepdims=True))
-        mine = owner == me
-        local = jnp.where(mine, storage - me * holder, -1)
-        if shift == 0:
-            home_ids_ref[...] = local
-            continue
-        known = jnp.broadcast_to(jnp.where(mine, local + 1, 0).astype(F32), (8, tokens)).astype(BF16)
-        slot = jnp.where(place >= 0, first + place, rank)
-        pick = one_hot(iota((ids_ref.shape[1], tokens), 0) == jnp.where(mine, slot, -1))
-        ids_ref[shift - 1 : shift, :] = dot(known, pick, ((1,), (1,)))[0:1, :].astype(jnp.int32) - 1
-    more_ref[0] = (jnp.max(most) >= late).astype(jnp.int32)
-
-
-def arrivals(me, storage_row, index_rows, owners, holder, first, late):
-    count = index_rows[0].shape[1]
-    return pl.pallas_call(
-        functools.partial(arrivals_kernel, owners, holder, first, late),
+    )(index_row, storage_row, dest, tokens)
+
+
+def low_rank_kernel(blocks, joined, holder, rank, me_ref, down_ref, *refs):
+    out, ids_out, flag = refs[-3:]
+    lead = me_ref[0] * holder + 1
+    flags = jnp.zeros((1, 1), F32)
+    for k, (rows, sources, tagged, row, tag_start) in enumerate(blocks):
+        rows_in = functools.reduce(jnp.add, [refs[j][at : at + rows, :] for j, at in sources])
+        every = dot(down_ref[...], rows_in, ((1,), (1,)))
+        tags = functools.reduce(jnp.add, [refs[j][at : at + TAGS, :].astype(F32) for j, at in tagged])
+        flags = jnp.maximum(flags, tags[TAGS - 1 : TAGS, 0:1])
+        ids = tags[row : row + 1, tag_start : tag_start + rows].astype(jnp.int32) - lead
+        total = jnp.zeros((rank, rows), F32)
+        for a in range(holder):
+            total = total + jnp.where(ids == a, every[a * rank : (a + 1) * rank, :], 0.0)
+        at = slice(tag_start, tag_start + rows)
+        if joined:
+            out[:, at] = total
+            ids_out[:, at] = ids
+        else:
+            out[k * rank : (k + 1) * rank, :] = total
+            ids_out[k : k + 1, :] = ids
+    flag[0] = jnp.max(flags).astype(jnp.int32)
+
+
+def low_rank(me, down, blocks, messages, holder, joined=False):
+    rank = down.shape[0] // holder
+    rows = sum(block[0] for block in blocks) if joined else blocks[0][0]
+    number = 1 if joined else len(blocks)
+    return pl.pallas_call(
+        functools.partial(low_rank_kernel, blocks, joined, holder, rank),
         out_shape=[
-            jax.ShapeDtypeStruct((owners - 1, first + 2 * late), jnp.int32),
-            jax.ShapeDtypeStruct((1, count), jnp.int32),
+            jax.ShapeDtypeStruct((number * rank, rows), F32),
+            jax.ShapeDtypeStruct((number, rows), jnp.int32),
             jax.ShapeDtypeStruct((1,), jnp.int32),
         ],
-        in_specs=[IN_SMEM] + [IN_VMEM] * (1 + owners),
+        in_specs=[IN_SMEM] + [IN_VMEM] * (1 + len(messages)),
         out_specs=[IN_VMEM, IN_VMEM, IN_SMEM],
         compiler_params=params(),
         cost_estimate=CHEAP,
-        name="arrivals",
-    )(me, storage_row, *index_rows)
-
-
-def low_rank_kernel(blocks, copies, rank, ids_ref, down_ref, *refs):
-    out = refs[-1]
-    rows_refs = iter(refs)
-    for k, ((row, start, rows, _), number) in enumerate(zip(blocks, copies)):
-        rows_in = functools.reduce(jnp.add, [next(rows_refs)[...] for _ in range(number)])
-        every = dot(down_ref[...], rows_in, ((1,), (1,)))
-        ids = ids_ref[row : row + 1, start : start + rows]
-        total = jnp.zeros((rank, rows), F32)
-        for a in range(down_ref.shape[0] // rank):
-            total = total + jnp.where(ids == a, every[a * rank : (a + 1) * rank, :], 0.0)
-        out[k * rank : (k + 1) * rank, :] = total
-
-
-def low_rank(ids, down, blocks, rows_in, rank):
-    rows = blocks[0][2]
-    copies = [len(x) for x in rows_in]
-    return pl.pallas_call(
-        functools.partial(low_rank_kernel, blocks, copies, rank),
-        out_shape=jax.ShapeDtypeStruct((len(blocks) * rank, rows), F32),
-        in_specs=[IN_VMEM] * (2 + sum(copies)),
+        name="low_rank",
+    )(me, down, *messages)
+
+
+def low_rank_home_kernel(holder, rank, ids_ref, down_ref, tokens_ref, out):
+    every = dot(down_ref[...], tokens_ref[...], ((1,), (1,)))
+    ids = ids_ref[...]
+    total = jnp.zeros(out.shape, F32)
+    for a in range(holder):
+        total = total + jnp.where(ids == a, every[a * rank : (a + 1) * rank, :], 0.0)
+    out[...] = total
+
+
+def low_rank_home(ids, down, tokens, holder):
+    rank = down.shape[0] // holder
+    return pl.pallas_call(
+        functools.partial(low_rank_home_kernel, holder, rank),
+        out_shape=jax.ShapeDtypeStruct((rank, tokens.shape[0]), F32),
+        in_specs=[IN_VMEM] * 3,
         out_specs=IN_VMEM,
         compiler_params=params(),
         cost_estimate=CHEAP,
-        name="low_rank",
-    )(ids, down, *[x for group in rows_in for x in group])
-
-
-def up_kernel(pieces, holder, rank, ids_ref, up_ref, a_ref, b_ref, *outs):
+        name="low_rank_home",
+    )(ids, down, tokens)
+
+
+def up_kernel(rows, holder, rank, ids_ref, up_ref, a_ref, b_ref, *outs):
     up = up_ref[...]
-    for k, ((row, start, rows), out) in enumerate(zip(pieces, outs)):
+    for k, out in enumerate(outs):
         own = slice(k * rank, (k + 1) * rank)
-        ids = ids_ref[row : row + 1, start : start + rows]
         low = a_ref[own, :] + b_ref[own, :]
+        ids = ids_ref[k : k + 1, :]
         spread = jnp.concatenate([jnp.where(ids == a, low, 0.0) for a in range(holder)], axis=0)
         high, rest = split_bf16(spread)
         out[...] = dot(high, up, ((0,), (0,))) + dot(rest, up, ((0,), (0,)))
 
 
-def up_project(ids, up, pieces, a, b, holder):
+def up_project(ids, up, a, b, holder):
+    blocks, rows = ids.shape
     rank = up.shape[0] // holder
     return pl.pallas_call(
-        functools.partial(up_kernel, pieces, holder, rank),
-        out_shape=[jax.ShapeDtypeStruct((rows, up.shape[1]), F32) for _, _, rows in pieces],
+        functools.partial(up_kernel, rows, holder, rank),
+        out_shape=[jax.ShapeDtypeStruct((rows, up.shape[1]), F32)] * blocks,
         in_specs=[IN_VMEM] * 4,
-        out_specs=[IN_VMEM] * len(pieces),
+        out_specs=[IN_VMEM] * blocks,
         compiler_params=params(),
         cost_estimate=CHEAP,
         name="up_project",
@@ -342,38 +364,46 @@
     late_start = (owners - 1) * first
 
     mains = {s: ((s - 1) * first, first) for s in shifts}
-    pieces = [[mains[1], (late_start, late)], [mains[2]], [mains[3], (late_start, late)]]
-    *packed, dest = route_pack(me, index_row, storage_row, tokens, owners, holder, first, pieces)
-    index_rows = [index_row] + [shifted(index_row, s) for s in shifts]
-    packed, index_rows = lax.optimization_barrier((packed, index_rows))
-    below, above, across = (shifted(packed[s - 1], s) for s in (1, 3, 2))
-    ids, home_ids, more = arrivals(me, storage_row, index_rows, owners, holder, first, late)
-
-    def terms(ids, blocks, rows_in):
-        lows = two_terms(low_rank(ids, down, blocks, rows_in, rank))
-        done = up_project(ids, up, [block[:3] for block in blocks], *lows, holder)
-        return [x if block[3] is None else shifted(x, -block[3]) for block, x in zip(blocks, done)]
-
-    def second(total):
-        x = repack(dest, tokens, late_start + late, late)
-        below, above = shifted(x, 1), shifted(x, 3)
-        blocks = [(s - 1, first + late, late, s) for s in shifts]
-        back = terms(ids, blocks, [[below], list(opposite(below, above)), [above]])
-        return gather_add(dest, [(late_start + late, late, [(j, 0) for j in range(3)])], [total], back, F32)
-
+    size = first + late
+    *packed, dest, home_ids, more = route_pack(me, index_row, storage_row, tokens, owners, holder, first, late)
+    packed, me_part, home_ids = lax.optimization_barrier((packed, me_part, home_ids))
+    below, above = shifted(packed[0], 1), shifted(packed[2], 3)
     base = base_terms(me_part, tokens, value_matrix, parts)
-    (stays,) = terms(home_ids, [(0, 0, count, None)], [[tokens]])
+    lows = two_terms(low_rank_home(home_ids, down, tokens, holder))
+    (stays,) = up_project(home_ids, up, *lows, holder)
     total = gather_add(dest, [], [*base, ADAPTER_SCALE * stays], [], F32)
+    rest, above = lax.optimization_barrier((packed[1], above))
+    across = shifted(rest, 2)
     below, above, total = lax.optimization_barrier((below, above, total))
-    passed = opposite(below[first:], above[first:])
-    back = terms(ids, [(s - 1, 0, first + late, s) for s in (1, 3)], [[below], [above]])
+    far = opposite(below[first:], above[first:])
+    blocks = [(size, [(j, 0)], [(j, size)], s - 1, 0) for j, s in enumerate((1, 3))]
+    lows, ids, near_more = low_rank(me, down, blocks, [below, above], holder)
+    near = up_project(ids, up, *two_terms(lows), holder)
+    back = [shifted(x, -s) for s, x in zip((1, 3), near)]
     pieces = [(*mains[1], [(0, 0)]), (*mains[3], [(1, 0)]), (late_start, late, [(0, first), (1, first)])]
     total = gather_add(dest, pieces, [total], back, F32)
-    back = terms(ids, [(1, first, late, 2)], [list(passed)])
-    total = gather_add(dest, [(late_start, late, [(0, 0)])], [total], back, F32)
-    total = lax.cond(more[0] > 0, second, lambda total: total, total)
-    back = terms(ids, [(1, 0, first, 2)], [[across]])
-    return gather_add(dest, [(*mains[2], [(0, 0)])], [total], back, BF16)
+
+    def second(total):
+        x = repack(index_row, storage_row, dest, tokens, late_start + late, late)
+        below, above = shifted(x, 1), shifted(x, 3)
+        x = [below, *opposite(below, above), above]
+        sources = [[0], [1, 2], [3]]
+        blocks = [(late, [(j, 0) for j in js], [(j, late) for j in js], 0, 0) for js in sources]
+        lows, ids, _ = low_rank(me, down, blocks, x, holder)
+        done = up_project(ids, up, *two_terms(lows), holder)
+        back = [shifted(x, -s) for s, x in zip(shifts, done)]
+        return gather_add(dest, [(late_start + late, late, [(j, 0) for j in range(3)])], [total], back, F32)
+
+    across, far, near = lax.optimization_barrier((across, far, near))
+    tags = [(j, late) for j in (1, 2)]
+    joined = [(first, [(0, 0)], tags, 1, 0), (late, [(1, 0), (2, 0)], tags, 1, first)]
+    lows, ids, far_more = low_rank(me, down, joined, [across, *far], holder, joined=True)
+    (done,) = up_project(ids, up, *two_terms(lows), holder)
+    more = jnp.maximum(more[0], jnp.maximum(near_more[0], far_more[0]))
+    total = lax.cond(more > 0, second, lambda total: total, total)
+    back = shifted(done, -2)
+    pieces = [(*mains[2], [(0, 0)]), (late_start, late, [(0, first)])]
+    return gather_add(dest, pieces, [total], [back], BF16)
 
 
 def by_all_to_all(tokens, token_adapter_index, adapter_storage_row, value_matrix, down_stored, up_stored):

time: 110 us -> 107 us (0.973)
  waiting for transfers between devices: 47.6 us -> 70.4 us
  starting transfers between devices: 38.1 us -> 19.4 us
  Pallas kernels: 19 us -> 14.4 us
  local copies, waits for them, and re-layouts: 3.31 us -> 0.13 us
  between operations: 0.98 us -> 2.08 us
    ppermute x12 -> x8, waiting for transfers between devices: 32.5 us -> 57.9 us  [along(): return lax.ppermute(x, 'own', pairs)]
    ppermute x12 -> x8, starting transfers between devices: 30.5 us -> 13.4 us  [along(): return lax.ppermute(x, 'own', pairs)]
    pallas_call x9 -> x6, Pallas kernels: 9.39 us -> 6.09 us  [the longest x2 3.51 us: low_rank(): pl.pallas_call(functools.partial(low_rank_kernel, blocks, joined, holder,...]
    ppermute x10 -> x8, waiting for transfers between devices: 15.1 us -> 12.5 us  [partner(): lax.ppermute(x, 'tp', [(i, i ^ bit) for i in range(lax.axis_size('tp'))])]
    unnamed x22 -> x12, local copies, waits for them, and re-layouts: 2.22 us -> 0.03 us
    ppermute x10 -> x8, starting transfers between devices: 7.64 us -> 6.04 us  [partner(): lax.ppermute(x, 'tp', [(i, i ^ bit) for i in range(lax.axis_size('tp'))])]
  transfers between devices with their start and end apart: 22 -> 16, of which waited for: 10 -> 13; matrix products, arithmetic and copies ran while one was open for 1% -> 0% of each run, Pallas kernels for 16% -> 7%
where the time goes in v3:
time: 107 us; the launch traced here: 106 us
  waiting for transfers between devices  70.4 us (66%)
  starting transfers between devices  19.4 us (18%)
  Pallas kernels  14.4 us (13%)
  between operations  2.08 us (2%)
    ppermute x8, waiting for transfers between devices, along(): return lax.ppermute(x, 'own', pairs)  57.9 us
    ppermute x8, starting transfers between devices, along(): return lax.ppermute(x, 'own', pairs)  13.4 us
    ppermute x8, waiting for transfers between devices, partner(): lax.ppermute(x, 'tp', [(i, i ^ bit) for i in range(lax.axis_size('tp'))])  12.5 us
    ppermute x8, starting transfers between devices, partner(): lax.ppermute(x, 'tp', [(i, i ^ bit) for i in range(lax.axis_size('tp'))])  6.04 us
    pallas_call x1, Pallas kernels, route_pack(): pl.pallas_call(functools.partial(route_pack_kernel, owners, holder, first...  3.61 us
    pallas_call x2, Pallas kernels, low_rank(): pl.pallas_call(functools.partial(low_rank_kernel, blocks, joined, holder,...  3.51 us
    pallas_call x1, Pallas kernels, base_blocks(): pl.pallas_call(functools.partial(base_kernel, parts), out_shape=[jax.Shap...  2.97 us
  transfers between devices with their start and end apart: 16, of which 13 were waited for; matrix products, arithmetic and copies ran while one was open for 0% of the time, Pallas kernels for 7%

profile of v3, /device:TPU:0, one launch (start us, length us, event | category | flops | bytes accessed | tf_op | source)
XLA Modules:
  0.0 106.5 jit_solution(14002352987387716690)
XLA Ops:
  0.0 3.6 %route_pack.1 = (bf16[272,2048]{1,0:T(8,128)(2,1)S(1)}, bf16[160,2048]{1,0:T(8,128)(2,1)S(1)}, bf16[272,2048]{1,0:T(8,128)(2,1)S(1)}, s32[1,512]{1,0:T(1,128)S(1)}, s32[1,512]{1,0:T(1,128)S(1)}, /*index=5*/s32[1]{0:T(128)}) custom-call(s32[1]{0:T(128)} %bitcast.me_ref, s32[1,512]{1,0:T(1,128)} %bitcast.17, s32[1,32]{1,0:T(1,128)} %bitcast.19, ...), custom_call_target="tpu_custom_call" | custom-call | flops 1 | bytes 1 | tf_op jit(solution)/shard_map/route_pack/pallas_call | solution.py:138
  3.6 0.0 copy-start.1
  3.6 0.0 copy-start.2
  3.6 5.1 %collective-permute-start.10 = (bf16[272,2048]{1,0:T(8,128)(2,1)S(1)}, bf16[272,2048]{1,0:T(8,128)(2,1)S(1)}, u32[]{:S(2)}, u32[]{:S(2)}) collective-permute-start(bf16[272,2048]{1,0:T(8,128)(2,1)S(1)} %get-tuple-element.75), channel_id=1, source_target_pairs={{0,12},{4,0},{8,4},{12,8},{1,13},{5,1},{9,5},{13,9},{2,14},{6,2},{... | collective-permute-start | bytes 3342344 | tf_op jit(solution)/shard_map/ppermute | solution.py:315
  8.7 0.0 collective-permute-start.9
  8.7 0.0 copy-done
  8.7 3.0 %base_blocks.1 = (f32[512,256]{1,0:T(8,128)S(1)}, f32[512,256]{1,0:T(8,128)S(1)}) custom-call(s32[1]{0:T(128)} %bitcast.5.me_ref, bf16[512,2048]{1,0:T(8,128)(2,1)} %tokens_ref.3, bf16[2048,512]{1,0:T(8,128)(2,1)S(1)} %copy-done), custom_call_target="tpu_custom_call" | custom-call | flops 1 | bytes 1 | tf_op jit(solution)/shard_map/base_blocks/pallas_call | solution.py:277
  11.7 0.1 collective-permute-start.11
  11.8 1.3 %low_rank_home.1 = f32[64,512]{1,0:T(8,128)S(1)} custom-call(s32[1,512]{1,0:T(1,128)S(1)} %get-tuple-element.80.ids_ref, bf16[512,2048]{1,0:T(8,128)(2,1)S(1)} %bitcast.9, bf16[512,2048]{1,0:T(8,128)(2,1)S(1)} %copy-done.1), custom_call_target="tpu_custom_call" | custom-call | flops 1 | bytes 1 | tf_op jit(solution)/shard_map/low_rank_home/pallas_call | solution.py:230
  13.1 0.5 collective-permute-start.13
  13.7 1.0 collective-permute-done.13
  14.7 1.6 %collective-permute-start.14 = (f32[64,512]{1,0:T(8,128)S(1)}, f32[64,512]{1,0:T(8,128)S(1)}, u32[]{:S(2)}, u32[]{:S(2)}) collective-permute-start(f32[64,512]{1,0:T(8,128)S(1)} %add.16.a_ref), channel_id=1, source_target_pairs={{0,2},{1,3},{2,0},{3,1},{4,6},{5,7},{6,4},{7,5},{8,10},{9,11},{10,... | collective-permute-start | bytes 393224 | tf_op jit(solution)/shard_map/ppermute | solution.py:328
  16.2 0.0 collective-permute-done.11
  16.2 0.1 add.15
  16.4 0.6 collective-permute-start.12
  17.0 4.1 %collective-permute-done.14.b_ref = f32[64,512]{1,0:T(8,128)S(1)} collective-permute-done((f32[64,512]{1,0:T(8,128)S(1)}, f32[64,512]{1,0:T(8,128)S(1)}, u32[]{:S(2)}, u32[]{:S(2)}) %collective-permute-start.14) | collective-permute-done | bytes 131104 | tf_op jit(solution)/shard_map/ppermute | solution.py:328
  21.1 0.5 up_project.5
  21.6 12.2 %collective-permute-done.10.refs_1_ = bf16[272,2048]{1,0:T(8,128)(2,1)S(1)} collective-permute-done((bf16[272,2048]{1,0:T(8,128)(2,1)S(1)}, bf16[272,2048]{1,0:T(8,128)(2,1)S(1)}, u32[]{:S(2)}, u32[]{:S(2)}) %collective-permute-start.10) | collective-permute-done | bytes 1114144 | tf_op jit(solution)/shard_map/ppermute | solution.py:315
  33.7 1.5 %collective-permute-start.15 = (bf16[160,2048]{1,0:T(8,128)(2,1)S(1)}, bf16[160,2048]{1,0:T(8,128)(2,1)S(1)}, u32[]{:S(2)}, u32[]{:S(2)}) collective-permute-start(bf16[160,2048]{1,0:T(8,128)(2,1)S(1)} %get-tuple-element.84), channel_id=1, source_target_pairs={{0,8},{4,12},{8,0},{12,4},{1,9},{5,13},{9,1},{13,5},{2,10},{6,14},... | collective-permute-start | bytes 1966088 | tf_op jit(solution)/shard_map/ppermute | solution.py:315
  35.2 0.0 collective-permute-done.12.refs_1_
  35.3 23.3 %collective-permute-done.9.refs_0_ = bf16[272,2048]{1,0:T(8,128)(2,1)S(1)} collective-permute-done((bf16[272,2048]{1,0:T(8,128)(2,1)S(1)}, bf16[272,2048]{1,0:T(8,128)(2,1)S(1)}, u32[]{:S(2)}, u32[]{:S(2)}) %collective-permute-start.9) | collective-permute-done | bytes 1114144 | tf_op jit(solution)/shard_map/ppermute | solution.py:315
  58.6 3.4 %collective-permute-start.16 = (bf16[112,2048]{1,0:T(8,128)(2,1)S(1)}, bf16[112,2048]{1,0:T(8,128)(2,1)S(1)}, u32[]{:S(2)}, u32[]{:S(2)}) collective-permute-start(bf16[112,2048]{1,0:T(8,128)(2,1)S(1)} %slice.6), channel_id=1, source_target_pairs={{0,4},{8,12},{1,5},{9,13},{2,6},{10,14},{3,7},{11,15},{16,20},{24,... | collective-permute-start | bytes 1376264 | tf_op jit(solution)/shard_map/ppermute | solution.py:315
  62.1 1.3 %collective-permute-start.17 = (bf16[112,2048]{1,0:T(8,128)(2,1)S(1)}, bf16[112,2048]{1,0:T(8,128)(2,1)S(1)}, u32[]{:S(2)}, u32[]{:S(2)}) collective-permute-start(bf16[112,2048]{1,0:T(8,128)(2,1)S(1)} %slice.7), channel_id=1, source_target_pairs={{4,0},{12,8},{5,1},{13,9},{6,2},{14,10},{7,3},{15,11},{20,16},{28,... | collective-permute-start | bytes 1376264 | tf_op jit(solution)/shard_map/ppermute | solution.py:315
  63.4 1.7 %low_rank.4 = (f32[128,256]{1,0:T(8,128)S(1)}, s32[2,256]{1,0:T(2,128)S(1)}, s32[1]{0:T(128)}) custom-call(s32[1]{0:T(128)} %bitcast.me_ref, bf16[512,2048]{1,0:T(8,128)(2,1)S(1)} %bitcast.10, bf16[272,2048]{1,0:T(8,128)(2,1)S(1)} %collective-permute-done.9.refs_0_, bf16[272,2048]{1,0:T(8,128)(2,1)S(1)} %collective-permute-done.10.refs_1_), custom_call_target="tpu_custom_call" | custom-call | flops 1 | bytes 1 | tf_op jit(solution)/shard_map/low_rank/pallas_call | solution.py:204
  65.1 0.1 collective-permute-start.18
  65.2 1.3 %collective-permute-done.18 = f32[128,256]{1,0:T(8,128)S(1)} collective-permute-done((f32[128,256]{1,0:T(8,128)S(1)}, f32[128,256]{1,0:T(8,128)S(1)}, u32[]{:S(2)}, u32[]{:S(2)}) %collective-permute-start.18) | collective-permute-done | bytes 131104 | tf_op jit(solution)/shard_map/ppermute | solution.py:328
  66.6 1.6 %collective-permute-start.19 = (f32[128,256]{1,0:T(8,128)S(1)}, f32[128,256]{1,0:T(8,128)S(1)}, u32[]{:S(2)}, u32[]{:S(2)}) collective-permute-start(f32[128,256]{1,0:T(8,128)S(1)} %add.17.a_ref), channel_id=1, source_target_pairs={{0,2},{1,3},{2,0},{3,1},{4,6},{5,7},{6,4},{7,5},{8,10},{9,11},{10,... | collective-permute-start | bytes 393224 | tf_op jit(solution)/shard_map/ppermute | solution.py:328
  68.1 4.1 %collective-permute-done.19.b_ref = f32[128,256]{1,0:T(8,128)S(1)} collective-permute-done((f32[128,256]{1,0:T(8,128)S(1)}, f32[128,256]{1,0:T(8,128)S(1)}, u32[]{:S(2)}, u32[]{:S(2)}) %collective-permute-start.19) | collective-permute-done | bytes 131104 | tf_op jit(solution)/shard_map/ppermute | solution.py:328
  72.2 0.5 up_project.6
  72.7 7.7 %collective-permute-done.16.refs_1_ = bf16[112,2048]{1,0:T(8,128)(2,1)S(1)} collective-permute-done((bf16[112,2048]{1,0:T(8,128)(2,1)S(1)}, bf16[112,2048]{1,0:T(8,128)(2,1)S(1)}, u32[]{:S(2)}, u32[]{:S(2)}) %collective-permute-start.16) | collective-permute-done | bytes 458784 | tf_op jit(solution)/shard_map/ppermute | solution.py:315
  80.4 7.6 %collective-permute-done.17.refs_2_ = bf16[112,2048]{1,0:T(8,128)(2,1)S(1)} collective-permute-done((bf16[112,2048]{1,0:T(8,128)(2,1)S(1)}, bf16[112,2048]{1,0:T(8,128)(2,1)S(1)}, u32[]{:S(2)}, u32[]{:S(2)}) %collective-permute-start.17) | collective-permute-done | bytes 458784 | tf_op jit(solution)/shard_map/ppermute | solution.py:315
  88.0 0.0 collective-permute-done.15.refs_0_
  88.0 1.8 %low_rank.5 = (f32[64,256]{1,0:T(8,128)S(1)}, s32[1,256]{1,0:T(1,128)S(1)}, s32[1]{0:T(128)}) custom-call(s32[1]{0:T(128)} %bitcast.me_ref, bf16[512,2048]{1,0:T(8,128)(2,1)S(1)} %bitcast.11, bf16[160,2048]{1,0:T(8,128)(2,1)S(1)} %collective-permute-done.15.refs_0_, bf16[112,2048]{1,0:T(8,128)(2,1)S(1)} %collective-permute-done.16.refs_1_, ...), custom_call_target="tpu_custom_call" | custom-call | flops 1 | bytes 1 | tf_op jit(solution)/shard_map/low_rank/pallas_call | solution.py:204
  89.8 0.0 copy-start.4
  89.8 0.0 copy-start.5
  89.8 0.1 collective-permute-start.22
  89.9 1.2 %collective-permute-done.22 = f32[64,256]{1,0:T(8,128)S(1)} collective-permute-done((f32[64,256]{1,0:T(8,128)S(1)}, f32[64,256]{1,0:T(8,128)S(1)}, u32[]{:S(2)}, u32[]{:S(2)}) %collective-permute-start.22) | collective-permute-done | bytes 65568 | tf_op jit(solution)/shard_map/ppermute | solution.py:328
  91.1 1.5 %collective-permute-start.23 = (f32[64,256]{1,0:T(8,128)S(1)}, f32[64,256]{1,0:T(8,128)S(1)}, u32[]{:S(2)}, u32[]{:S(2)}) collective-permute-start(f32[64,256]{1,0:T(8,128)S(1)} %add.18.a_ref), channel_id=1, source_target_pairs={{0,2},{1,3},{2,0},{3,1},{4,6},{5,7},{6,4},{7,5},{8,10},{9,11},{10,... | collective-permute-start | bytes 196616 | tf_op jit(solution)/shard_map/ppermute | solution.py:328
  92.7 0.0 collective-permute-start.20
  92.7 2.0 %collective-permute-start.21 = (f32[256,128]{1,0:T(8,128)S(1)}, f32[256,128]{1,0:T(8,128)S(1)}, u32[]{:S(2)}, u32[]{:S(2)}) collective-permute-start(f32[256,128]{1,0:T(8,128)S(1)} %get-tuple-element.88), channel_id=1, source_target_pairs={{0,4},{4,8},{8,12},{12,0},{1,5},{5,9},{9,13},{13,1},{2,6},{6,10},{... | collective-permute-start | bytes 393224 | tf_op jit(solution)/shard_map/ppermute | solution.py:315
  94.7 0.8 collective-permute-done.23.b_ref
  95.4 0.3 up_project.7
  95.8 0.1 collective-permute-start.24
  95.9 4.8 %collective-permute-done.20.refs_1_ = f32[256,128]{1,0:T(8,128)S(1)} collective-permute-done((f32[256,128]{1,0:T(8,128)S(1)}, f32[256,128]{1,0:T(8,128)S(1)}, u32[]{:S(2)}, u32[]{:S(2)}) %collective-permute-start.20) | collective-permute-done | bytes 131104 | tf_op jit(solution)/shard_map/ppermute | solution.py:315
  100.7 0.3 collective-permute-done.21.refs_2_
  101.0 0.6 gather_add.6
  103.4 2.0 %collective-permute-done.24.refs_1_ = f32[256,128]{1,0:T(8,128)S(1)} collective-permute-done((f32[256,128]{1,0:T(8,128)S(1)}, f32[256,128]{1,0:T(8,128)S(1)}, u32[]{:S(2)}, u32[]{:S(2)}) %collective-permute-start.24) | collective-permute-done | bytes 131104 | tf_op jit(solution)/shard_map/ppermute | solution.py:315
  105.4 1.1 %gather_add.7 = bf16[512,128]{1,0:T(8,128)(2,1)} custom-call(s32[1,512]{1,0:T(1,128)S(1)} %get-tuple-element.67.dest_ref, f32[512,128]{1,0:T(8,128)S(1)} %get-tuple-element.98.refs_0_, f32[256,128]{1,0:T(8,128)S(1)} %collective-permute-done.24.refs_1_), custom_call_target="tpu_custom_call" | custom-call | flops 1 | bytes 1 | tf_op jit(solution)/shard_map/gather_add/pallas_call | solution.py:303
  (16 shorter events, 0.2 us)
Async XLA Ops:
  0.0 8.7 %copy-start = (bf16[2048,512]{1,0:T(8,128)(2,1)S(1)}, bf16[2048,512]{1,0:T(8,128)(2,1)}, u32[]{:S(2)}) copy-start(bf16[2048,512]{1,0:T(8,128)(2,1)} %value_ref.1) | copy-start | bytes 6291460
  3.6 8.2 %copy-start.1 = (bf16[512,2048]{1,0:T(8,128)(2,1)S(1)}, bf16[512,2048]{1,0:T(8,128)(2,1)}, u32[]{:S(2)}) copy-start(bf16[512,2048]{1,0:T(8,128)(2,1)} %tokens_ref.3) | copy-start | bytes 6291460
  3.6 8.2 %copy-start.2 = (bf16[8,2048,64]{1,2,0:T(8,128)(2,1)S(1)}, bf16[8,2048,64]{1,2,0:T(8,128)(2,1)}, u32[]{:S(2)}) copy-start(bf16[8,2048,64]{1,2,0:T(8,128)(2,1)} %param.12) | copy-start | bytes 6291460
  3.6 30.1 %collective-permute-start.10 = (bf16[272,2048]{1,0:T(8,128)(2,1)S(1)}, bf16[272,2048]{1,0:T(8,128)(2,1)S(1)}, u32[]{:S(2)}, u32[]{:S(2)}) collective-permute-start(bf16[272,2048]{1,0:T(8,128)(2,1)S(1)} %get-tuple-element.75), channel_id=1, source_target_pairs={{0,12},{4,0},{8,4},{12,8},{1,13},{5,1},{9,5},{13,9},{2,14},{6,2},{... | collective-permute-start | bytes 3342344 | tf_op jit(solution)/shard_map/ppermute | solution.py:315
  8.7 49.9 %collective-permute-start.9 = (bf16[272,2048]{1,0:T(8,128)(2,1)S(1)}, bf16[272,2048]{1,0:T(8,128)(2,1)S(1)}, u32[]{:S(2)}, u32[]{:S(2)}) collective-permute-start(bf16[272,2048]{1,0:T(8,128)(2,1)S(1)} %get-tuple-element.73), channel_id=1, source_target_pairs={{0,4},{4,8},{8,12},{12,0},{1,5},{5,9},{9,13},{13,1},{2,6},{6,10},{... | collective-permute-start | bytes 3342344 | tf_op jit(solution)/shard_map/ppermute | solution.py:315
  11.7 4.5 %collective-permute-start.11 = (f32[512,256]{1,0:T(8,128)S(1)}, f32[512,256]{1,0:T(8,128)S(1)}, u32[]{:S(2)}, u32[]{:S(2)}) collective-permute-start(f32[512,256]{1,0:T(8,128)S(1)} %get-tuple-element.79), channel_id=1, source_target_pairs={{0,1},{1,0},{2,3},{3,2},{4,5},{5,4},{6,7},{7,6},{8,9},{9,8},{10,11... | collective-permute-start | bytes 1572872 | tf_op jit(solution)/shard_map/ppermute | solution.py:328
  13.1 1.5 %collective-permute-start.13 = (f32[64,512]{1,0:T(8,128)S(1)}, f32[64,512]{1,0:T(8,128)S(1)}, u32[]{:S(2)}, u32[]{:S(2)}) collective-permute-start(f32[64,512]{1,0:T(8,128)S(1)} %low_rank_home.1), channel_id=1, source_target_pairs={{0,1},{1,0},{2,3},{3,2},{4,5},{5,4},{6,7},{7,6},{8,9},{9,8},{10,11... | collective-permute-start | bytes 393224 | tf_op jit(solution)/shard_map/ppermute | solution.py:328
  14.7 6.4 %collective-permute-start.14 = (f32[64,512]{1,0:T(8,128)S(1)}, f32[64,512]{1,0:T(8,128)S(1)}, u32[]{:S(2)}, u32[]{:S(2)}) collective-permute-start(f32[64,512]{1,0:T(8,128)S(1)} %add.16.a_ref), channel_id=1, source_target_pairs={{0,2},{1,3},{2,0},{3,1},{4,6},{5,7},{6,4},{7,5},{8,10},{9,11},{10,... | collective-permute-start | bytes 393224 | tf_op jit(solution)/shard_map/ppermute | solution.py:328
  16.2 4.8 %copy-start.3 = (bf16[8,64,128]{2,1,0:T(8,128)(2,1)S(1)}, bf16[8,64,128]{2,1,0:T(8,128)(2,1)}, u32[]{:S(2)}) copy-start(bf16[8,64,128]{2,1,0:T(8,128)(2,1)} %param.13) | copy-start | bytes 393220
  16.4 18.9 %collective-permute-start.12 = (f32[512,128]{1,0:T(8,128)S(1)}, f32[512,128]{1,0:T(8,128)S(1)}, u32[]{:S(2)}, u32[]{:S(2)}) collective-permute-start(f32[512,128]{1,0:T(8,128)S(1)} %get-tuple-element.96), channel_id=1, source_target_pairs={{0,2},{1,3},{2,0},{3,1},{4,6},{5,7},{6,4},{7,5},{8,10},{9,11},{10,... | collective-permute-start | bytes 786440 | tf_op jit(solution)/shard_map/ppermute | solution.py:328
  33.7 54.3 %collective-permute-start.15 = (bf16[160,2048]{1,0:T(8,128)(2,1)S(1)}, bf16[160,2048]{1,0:T(8,128)(2,1)S(1)}, u32[]{:S(2)}, u32[]{:S(2)}) collective-permute-start(bf16[160,2048]{1,0:T(8,128)(2,1)S(1)} %get-tuple-element.84), channel_id=1, source_target_pairs={{0,8},{4,12},{8,0},{12,4},{1,9},{5,13},{9,1},{13,5},{2,10},{6,14},... | collective-permute-start | bytes 1966088 | tf_op jit(solution)/shard_map/ppermute | solution.py:315
  58.6 21.8 %collective-permute-start.16 = (bf16[112,2048]{1,0:T(8,128)(2,1)S(1)}, bf16[112,2048]{1,0:T(8,128)(2,1)S(1)}, u32[]{:S(2)}, u32[]{:S(2)}) collective-permute-start(bf16[112,2048]{1,0:T(8,128)(2,1)S(1)} %slice.6), channel_id=1, source_target_pairs={{0,4},{8,12},{1,5},{9,13},{2,6},{10,14},{3,7},{11,15},{16,20},{24,... | collective-permute-start | bytes 1376264 | tf_op jit(solution)/shard_map/ppermute | solution.py:315
  62.1 25.9 %collective-permute-start.17 = (bf16[112,2048]{1,0:T(8,128)(2,1)S(1)}, bf16[112,2048]{1,0:T(8,128)(2,1)S(1)}, u32[]{:S(2)}, u32[]{:S(2)}) collective-permute-start(bf16[112,2048]{1,0:T(8,128)(2,1)S(1)} %slice.7), channel_id=1, source_target_pairs={{4,0},{12,8},{5,1},{13,9},{6,2},{14,10},{7,3},{15,11},{20,16},{28,... | collective-permute-start | bytes 1376264 | tf_op jit(solution)/shard_map/ppermute | solution.py:315
  65.1 1.4 %collective-permute-start.18 = (f32[128,256]{1,0:T(8,128)S(1)}, f32[128,256]{1,0:T(8,128)S(1)}, u32[]{:S(2)}, u32[]{:S(2)}) collective-permute-start(f32[128,256]{1,0:T(8,128)S(1)} %get-tuple-element.86), channel_id=1, source_target_pairs={{0,1},{1,0},{2,3},{3,2},{4,5},{5,4},{6,7},{7,6},{8,9},{9,8},{10,11... | collective-permute-start | bytes 393224 | tf_op jit(solution)/shard_map/ppermute | solution.py:328
  66.6 5.6 %collective-permute-start.19 = (f32[128,256]{1,0:T(8,128)S(1)}, f32[128,256]{1,0:T(8,128)S(1)}, u32[]{:S(2)}, u32[]{:S(2)}) collective-permute-start(f32[128,256]{1,0:T(8,128)S(1)} %add.17.a_ref), channel_id=1, source_target_pairs={{0,2},{1,3},{2,0},{3,1},{4,6},{5,7},{6,4},{7,5},{8,10},{9,11},{10,... | collective-permute-start | bytes 393224 | tf_op jit(solution)/shard_map/ppermute | solution.py:328
  89.8 13.7 %copy-start.4 = (s32[512]{0:T(512)S(1)}, s32[512]{0:T(512)}, u32[]{:S(2)}) copy-start(s32[512]{0:T(512)} %param.9) | copy-start | bytes 6148
  89.8 13.6 %copy-start.5 = (s32[32]{0:T(128)S(1)}, s32[32]{0:T(128)}, u32[]{:S(2)}) copy-start(s32[32]{0:T(128)} %param.10) | copy-start | bytes 388
  89.8 1.3 %collective-permute-start.22 = (f32[64,256]{1,0:T(8,128)S(1)}, f32[64,256]{1,0:T(8,128)S(1)}, u32[]{:S(2)}, u32[]{:S(2)}) collective-permute-start(f32[64,256]{1,0:T(8,128)S(1)} %get-tuple-element.95), channel_id=1, source_target_pairs={{0,1},{1,0},{2,3},{3,2},{4,5},{5,4},{6,7},{7,6},{8,9},{9,8},{10,11... | collective-permute-start | bytes 196616 | tf_op jit(solution)/shard_map/ppermute | solution.py:328
  91.1 4.3 %collective-permute-start.23 = (f32[64,256]{1,0:T(8,128)S(1)}, f32[64,256]{1,0:T(8,128)S(1)}, u32[]{:S(2)}, u32[]{:S(2)}) collective-permute-start(f32[64,256]{1,0:T(8,128)S(1)} %add.18.a_ref), channel_id=1, source_target_pairs={{0,2},{1,3},{2,0},{3,1},{4,6},{5,7},{6,4},{7,5},{8,10},{9,11},{10,... | collective-permute-start | bytes 196616 | tf_op jit(solution)/shard_map/ppermute | solution.py:328
  92.7 8.0 %collective-permute-start.20 = (f32[256,128]{1,0:T(8,128)S(1)}, f32[256,128]{1,0:T(8,128)S(1)}, u32[]{:S(2)}, u32[]{:S(2)}) collective-permute-start(f32[256,128]{1,0:T(8,128)S(1)} %get-tuple-element.87), channel_id=1, source_target_pairs={{0,12},{4,0},{8,4},{12,8},{1,13},{5,1},{9,5},{13,9},{2,14},{6,2},{... | collective-permute-start | bytes 393224 | tf_op jit(solution)/shard_map/ppermute | solution.py:315
  92.7 8.3 %collective-permute-start.21 = (f32[256,128]{1,0:T(8,128)S(1)}, f32[256,128]{1,0:T(8,128)S(1)}, u32[]{:S(2)}, u32[]{:S(2)}) collective-permute-start(f32[256,128]{1,0:T(8,128)S(1)} %get-tuple-element.88), channel_id=1, source_target_pairs={{0,4},{4,8},{8,12},{12,0},{1,5},{5,9},{9,13},{13,1},{2,6},{6,10},{... | collective-permute-start | bytes 393224 | tf_op jit(solution)/shard_map/ppermute | solution.py:315
  95.8 9.6 %collective-permute-start.24 = (f32[256,128]{1,0:T(8,128)S(1)}, f32[256,128]{1,0:T(8,128)S(1)}, u32[]{:S(2)}, u32[]{:S(2)}) collective-permute-start(f32[256,128]{1,0:T(8,128)S(1)} %up_project.7), channel_id=1, source_target_pairs={{0,8},{4,12},{8,0},{12,4},{1,9},{5,13},{9,1},{13,5},{2,10},{6,14},... | collective-permute-start | bytes 393224 | tf_op jit(solution)/shard_map/ppermute | solution.py:315

commit v4 on v3

--- a/solution.py
+++ b/solution.py
@@ -10,6 +10,7 @@
 CAP = 4
 ADAPTER_SCALE = 0.5
 TAGS = 16
+CODE_ROWS = 16
 LINE = 4
 BF16 = jnp.bfloat16
 F32 = jnp.float32
@@ -263,6 +264,38 @@
     )(ids, up, a, b)
 
 
+def up_coded_kernel(holder, rank, ids_ref, up_ref, a_ref, b_ref, *outs):
+    up = up_ref[...]
+    width = up.shape[1]
+    for k, out in enumerate(outs):
+        own = slice(k * rank, (k + 1) * rank)
+        low = a_ref[own, :] + b_ref[own, :]
+        ids = ids_ref[k : k + 1, :]
+        spread = jnp.concatenate([jnp.where(ids == a, low, 0.0) for a in range(holder)], axis=0)
+        high, rest = split_bf16(spread)
+        term = ADAPTER_SCALE * (dot(up, high, ((0,), (0,))) + dot(up, rest, ((0,), (0,))))
+        largest = jnp.maximum(jnp.max(jnp.abs(term), axis=0, keepdims=True), 1e-30)
+        exponent = jnp.floor(jnp.log2(largest)) + 1.0
+        code = jnp.clip(jnp.round(term * jnp.exp2(15.0 - exponent)), -32767.0, 32767.0)
+        out[0:width, :] = code.astype(jnp.int32).astype(jnp.int16)
+        exponents = jnp.broadcast_to(exponent, (out.shape[0] - width, out.shape[1]))
+        out[width:, :] = exponents.astype(jnp.int32).astype(jnp.int16)
+
+
+def up_coded(ids, up, a, b, holder):
+    blocks, rows = ids.shape
+    rank = up.shape[0] // holder
+    return pl.pallas_call(
+        functools.partial(up_coded_kernel, holder, rank),
+        out_shape=[jax.ShapeDtypeStruct((up.shape[1] + CODE_ROWS, rows), jnp.int16)] * blocks,
+        in_specs=[IN_VMEM] * 4,
+        out_specs=[IN_VMEM] * blocks,
+        compiler_params=params(),
+        cost_estimate=CHEAP,
+        name="up_coded",
+    )(ids, up, a, b)
+
+
 def base_kernel(parts, me_ref, tokens_ref, value_ref, kept_ref, away_ref, full):
     width = full.shape[1] // parts
     full[...] = dot(tokens_ref[...], value_ref[...])
@@ -286,22 +319,29 @@
     )(me, tokens, value)
 
 
-def gather_add_kernel(pieces, terms, dest_ref, *refs):
+def gather_add_kernel(ranges, terms, dest_ref, *refs):
     total = refs[0][...]
     for k in range(1, terms):
         total = total + refs[k][...]
     dest = dest_ref[...]
-    for start, rows, sources in pieces:
-        piece = functools.reduce(jnp.add, [refs[terms + j][at : at + rows, :] for j, at in sources])
-        pick = one_hot(iota((rows, dest.shape[1]), 0) + start == dest)
-        high, rest = split_bf16(ADAPTER_SCALE * piece)
-        total = total + (dot(pick, high, ((0,), (0,))) + dot(pick, rest, ((0,), (0,))))
+    found = jnp.zeros((total.shape[1], total.shape[0]), F32)
+    for (start, rows, late_start), ref in zip(ranges, refs[terms:]):
+        width = total.shape[1]
+        exponent = ref[width:, :].astype(jnp.int32).astype(F32)[0:1, :]
+        values = ref[0:width, :].astype(jnp.int32).astype(F32) * jnp.exp2(exponent - 15.0)
+        shape = (values.shape[1], dest.shape[1])
+        row = iota(shape, 0)
+        pick = one_hot(jnp.where(row < rows, row + start, row + (late_start - rows)) == dest)
+        high, rest = split_bf16(values)
+        found = found + (dot(high, pick) + dot(rest, pick))
+    if ranges:
+        total = total + found.T
     refs[-1][...] = total.astype(refs[-1].dtype)
 
 
-def gather_add(dest, pieces, terms, returned, dtype):
-    return pl.pallas_call(
-        functools.partial(gather_add_kernel, pieces, len(terms)),
+def gather_add(dest, ranges, terms, returned, dtype):
+    return pl.pallas_call(
+        functools.partial(gather_add_kernel, ranges, len(terms)),
         out_shape=jax.ShapeDtypeStruct(terms[0].shape, dtype),
         in_specs=[IN_VMEM] * (1 + len(terms) + len(returned)),
         out_specs=IN_VMEM,
@@ -378,10 +418,9 @@
     far = opposite(below[first:], above[first:])
     blocks = [(size, [(j, 0)], [(j, size)], s - 1, 0) for j, s in enumerate((1, 3))]
     lows, ids, near_more = low_rank(me, down, blocks, [below, above], holder)
-    near = up_project(ids, up, *two_terms(lows), holder)
+    near = up_coded(ids, up, *two_terms(lows), holder)
     back = [shifted(x, -s) for s, x in zip((1, 3), near)]
-    pieces = [(*mains[1], [(0, 0)]), (*mains[3], [(1, 0)]), (late_start, late, [(0, first), (1, first)])]
-    total = gather_add(dest, pieces, [total], back, F32)
+    total = gather_add(dest, [(*mains[s], late_start) for s in (1, 3)], [total], back, F32)
 
     def second(total):
         x = repack(index_row, storage_row, dest, tokens, late_start + late, late)
@@ -390,20 +429,19 @@
         sources = [[0], [1, 2], [3]]
         blocks = [(late, [(j, 0) for j in js], [(j, late) for j in js], 0, 0) for js in sources]
         lows, ids, _ = low_rank(me, down, blocks, x, holder)
-        done = up_project(ids, up, *two_terms(lows), holder)
+        done = up_coded(ids, up, *two_terms(lows), holder)
         back = [shifted(x, -s) for s, x in zip(shifts, done)]
-        return gather_add(dest, [(late_start + late, late, [(j, 0) for j in range(3)])], [total], back, F32)
+        return gather_add(dest, [(late_start + late, late, 0)] * len(back), [total], back, F32)
 
     across, far, near = lax.optimization_barrier((across, far, near))
     tags = [(j, late) for j in (1, 2)]
     joined = [(first, [(0, 0)], tags, 1, 0), (late, [(1, 0), (2, 0)], tags, 1, first)]
     lows, ids, far_more = low_rank(me, down, joined, [across, *far], holder, joined=True)
-    (done,) = up_project(ids, up, *two_terms(lows), holder)
+    (done,) = up_coded(ids, up, *two_terms(lows), holder)
     more = jnp.maximum(more[0], jnp.maximum(near_more[0], far_more[0]))
     total = lax.cond(more > 0, second, lambda total: total, total)
     back = shifted(done, -2)
-    pieces = [(*mains[2], [(0, 0)]), (late_start, late, [(0, first)])]
-    return gather_add(dest, pieces, [total], [back], BF16)
+    return gather_add(dest, [(*mains[2], late_start)], [total], [back], BF16)
 
 
 def by_all_to_all(tokens, token_adapter_index, adapter_storage_row, value_matrix, down_stored, up_stored):

time: 107 us -> 103 us (0.963)
  waiting for transfers between devices: 70.4 us -> 66.8 us
    ppermute x8, waiting for transfers between devices: 57.9 us -> 54.3 us  [along(): return lax.ppermute(x, 'own', pairs)]
    pallas_call x3 -> x5, Pallas kernels: 1.71 us -> 2.3 us  [the longest x3 1.51 us: gather_add(): pl.pallas_call(functools.partial(gather_add_kernel, ranges, len(terms)),...]
  transfers between devices with their start and end apart: 16 -> 16, of which waited for: 13 -> 12; matrix products, arithmetic and copies ran while one was open for 0% -> 0% of each run, Pallas kernels for 7% -> 8%
where the time goes in v4:
time: 103 us
  waiting for transfers between devices  66.8 us (65%)
  starting transfers between devices  19.4 us (19%)
  Pallas kernels  14.2 us (14%)
  between operations  2.09 us (2%)
    ppermute x8, waiting for transfers between devices, along(): return lax.ppermute(x, 'own', pairs)  54.3 us
    ppermute x8, starting transfers between devices, along(): return lax.ppermute(x, 'own', pairs)  13.4 us
    ppermute x8, waiting for transfers between devices, partner(): lax.ppermute(x, 'tp', [(i, i ^ bit) for i in range(lax.axis_size('tp'))])  12.5 us
    ppermute x8, starting transfers between devices, partner(): lax.ppermute(x, 'tp', [(i, i ^ bit) for i in range(lax.axis_size('tp'))])  6.04 us
    pallas_call x1, Pallas kernels, route_pack(): pl.pallas_call(functools.partial(route_pack_kernel, owners, holder, first...  3.61 us
    pallas_call x2, Pallas kernels, low_rank(): pl.pallas_call(functools.partial(low_rank_kernel, blocks, joined, holder,...  3.51 us
    pallas_call x1, Pallas kernels, base_blocks(): pl.pallas_call(functools.partial(base_kernel, parts), out_shape=[jax.Shap...  2.97 us
  transfers between devices with their start and end apart: 16, of which 12 were waited for; matrix products, arithmetic and copies ran while one was open for 0% of the time, Pallas kernels for 8%

profile of v4, /device:TPU:0, one launch (start us, length us, event | category | flops | bytes accessed | tf_op | source)
XLA Modules:
  0.0 102.7 jit_solution(17479722154137812113)
XLA Ops:
  0.0 3.6 %route_pack.1 = (bf16[272,2048]{1,0:T(8,128)(2,1)S(1)}, bf16[160,2048]{1,0:T(8,128)(2,1)S(1)}, bf16[272,2048]{1,0:T(8,128)(2,1)S(1)}, s32[1,512]{1,0:T(1,128)S(1)}, s32[1,512]{1,0:T(1,128)S(1)}, /*index=5*/s32[1]{0:T(128)}) custom-call(s32[1]{0:T(128)} %bitcast.me_ref, s32[1,512]{1,0:T(1,128)} %bitcast.17, s32[1,32]{1,0:T(1,128)} %bitcast.19, ...), custom_call_target="tpu_custom_call" | custom-call | flops 1 | bytes 1 | tf_op jit(solution)/shard_map/route_pack/pallas_call | solution.py:139
  3.6 0.0 copy-start.1
  3.6 0.0 copy-start.2
  3.6 5.1 %collective-permute-start.10 = (bf16[272,2048]{1,0:T(8,128)(2,1)S(1)}, bf16[272,2048]{1,0:T(8,128)(2,1)S(1)}, u32[]{:S(2)}, u32[]{:S(2)}) collective-permute-start(bf16[272,2048]{1,0:T(8,128)(2,1)S(1)} %get-tuple-element.75), channel_id=1, source_target_pairs={{0,12},{4,0},{8,4},{12,8},{1,13},{5,1},{9,5},{13,9},{2,14},{6,2},{... | collective-permute-start | bytes 3342344 | tf_op jit(solution)/shard_map/ppermute | solution.py:355
  8.7 0.0 collective-permute-start.9
  8.7 3.0 %base_blocks.1 = (f32[512,256]{1,0:T(8,128)S(1)}, f32[512,256]{1,0:T(8,128)S(1)}) custom-call(s32[1]{0:T(128)} %bitcast.5.me_ref, bf16[512,2048]{1,0:T(8,128)(2,1)} %tokens_ref.3, bf16[2048,512]{1,0:T(8,128)(2,1)S(1)} %copy-done), custom_call_target="tpu_custom_call" | custom-call | flops 1 | bytes 1 | tf_op jit(solution)/shard_map/base_blocks/pallas_call | solution.py:310
  11.7 0.1 collective-permute-start.11
  11.8 1.3 %low_rank_home.1 = f32[64,512]{1,0:T(8,128)S(1)} custom-call(s32[1,512]{1,0:T(1,128)S(1)} %get-tuple-element.80.ids_ref, bf16[512,2048]{1,0:T(8,128)(2,1)S(1)} %bitcast.9, bf16[512,2048]{1,0:T(8,128)(2,1)S(1)} %copy-done.1), custom_call_target="tpu_custom_call" | custom-call | flops 1 | bytes 1 | tf_op jit(solution)/shard_map/low_rank_home/pallas_call | solution.py:231
  13.1 0.5 collective-permute-start.13
  13.7 1.0 collective-permute-done.13
  14.7 1.6 %collective-permute-start.14 = (f32[64,512]{1,0:T(8,128)S(1)}, f32[64,512]{1,0:T(8,128)S(1)}, u32[]{:S(2)}, u32[]{:S(2)}) collective-permute-start(f32[64,512]{1,0:T(8,128)S(1)} %add.16.a_ref), channel_id=1, source_target_pairs={{0,2},{1,3},{2,0},{3,1},{4,6},{5,7},{6,4},{7,5},{8,10},{9,11},{10,... | collective-permute-start | bytes 393224 | tf_op jit(solution)/shard_map/ppermute | solution.py:368
  16.2 0.0 collective-permute-done.11
  16.2 0.1 add.15
  16.4 0.6 collective-permute-start.12
  17.0 4.1 %collective-permute-done.14.b_ref = f32[64,512]{1,0:T(8,128)S(1)} collective-permute-done((f32[64,512]{1,0:T(8,128)S(1)}, f32[64,512]{1,0:T(8,128)S(1)}, u32[]{:S(2)}, u32[]{:S(2)}) %collective-permute-start.14) | collective-permute-done | bytes 131104 | tf_op jit(solution)/shard_map/ppermute | solution.py:368
  21.1 0.5 up_project.1
  21.6 12.2 %collective-permute-done.10.refs_1_ = bf16[272,2048]{1,0:T(8,128)(2,1)S(1)} collective-permute-done((bf16[272,2048]{1,0:T(8,128)(2,1)S(1)}, bf16[272,2048]{1,0:T(8,128)(2,1)S(1)}, u32[]{:S(2)}, u32[]{:S(2)}) %collective-permute-start.10) | collective-permute-done | bytes 1114144 | tf_op jit(solution)/shard_map/ppermute | solution.py:355
  33.7 1.5 %collective-permute-start.15 = (bf16[160,2048]{1,0:T(8,128)(2,1)S(1)}, bf16[160,2048]{1,0:T(8,128)(2,1)S(1)}, u32[]{:S(2)}, u32[]{:S(2)}) collective-permute-start(bf16[160,2048]{1,0:T(8,128)(2,1)S(1)} %get-tuple-element.84), channel_id=1, source_target_pairs={{0,8},{4,12},{8,0},{12,4},{1,9},{5,13},{9,1},{13,5},{2,10},{6,14},... | collective-permute-start | bytes 1966088 | tf_op jit(solution)/shard_map/ppermute | solution.py:355
  35.2 0.0 collective-permute-done.12.refs_1_
  35.2 0.1 gather_add.5.refs_0_
  35.3 23.3 %collective-permute-done.9.refs_0_ = bf16[272,2048]{1,0:T(8,128)(2,1)S(1)} collective-permute-done((bf16[272,2048]{1,0:T(8,128)(2,1)S(1)}, bf16[272,2048]{1,0:T(8,128)(2,1)S(1)}, u32[]{:S(2)}, u32[]{:S(2)}) %collective-permute-start.9) | collective-permute-done | bytes 1114144 | tf_op jit(solution)/shard_map/ppermute | solution.py:355
  58.6 3.4 %collective-permute-start.16 = (bf16[112,2048]{1,0:T(8,128)(2,1)S(1)}, bf16[112,2048]{1,0:T(8,128)(2,1)S(1)}, u32[]{:S(2)}, u32[]{:S(2)}) collective-permute-start(bf16[112,2048]{1,0:T(8,128)(2,1)S(1)} %slice.6), channel_id=1, source_target_pairs={{0,4},{8,12},{1,5},{9,13},{2,6},{10,14},{3,7},{11,15},{16,20},{24,... | collective-permute-start | bytes 1376264 | tf_op jit(solution)/shard_map/ppermute | solution.py:355
  62.1 1.3 %collective-permute-start.17 = (bf16[112,2048]{1,0:T(8,128)(2,1)S(1)}, bf16[112,2048]{1,0:T(8,128)(2,1)S(1)}, u32[]{:S(2)}, u32[]{:S(2)}) collective-permute-start(bf16[112,2048]{1,0:T(8,128)(2,1)S(1)} %slice.7), channel_id=1, source_target_pairs={{4,0},{12,8},{5,1},{13,9},{6,2},{14,10},{7,3},{15,11},{20,16},{28,... | collective-permute-start | bytes 1376264 | tf_op jit(solution)/shard_map/ppermute | solution.py:355
  63.4 1.7 %low_rank.4 = (f32[128,256]{1,0:T(8,128)S(1)}, s32[2,256]{1,0:T(2,128)S(1)}, s32[1]{0:T(128)}) custom-call(s32[1]{0:T(128)} %bitcast.me_ref, bf16[512,2048]{1,0:T(8,128)(2,1)S(1)} %bitcast.10, bf16[272,2048]{1,0:T(8,128)(2,1)S(1)} %collective-permute-done.9.refs_0_, bf16[272,2048]{1,0:T(8,128)(2,1)S(1)} %collective-permute-done.10.refs_1_), custom_call_target="tpu_custom_call" | custom-call | flops 1 | bytes 1 | tf_op jit(solution)/shard_map/low_rank/pallas_call | solution.py:205
  65.1 0.1 collective-permute-start.18
  65.2 1.3 %collective-permute-done.18 = f32[128,256]{1,0:T(8,128)S(1)} collective-permute-done((f32[128,256]{1,0:T(8,128)S(1)}, f32[128,256]{1,0:T(8,128)S(1)}, u32[]{:S(2)}, u32[]{:S(2)}) %collective-permute-start.18) | collective-permute-done | bytes 131104 | tf_op jit(solution)/shard_map/ppermute | solution.py:368
  66.6 1.6 %collective-permute-start.19 = (f32[128,256]{1,0:T(8,128)S(1)}, f32[128,256]{1,0:T(8,128)S(1)}, u32[]{:S(2)}, u32[]{:S(2)}) collective-permute-start(f32[128,256]{1,0:T(8,128)S(1)} %add.17.a_ref), channel_id=1, source_target_pairs={{0,2},{1,3},{2,0},{3,1},{4,6},{5,7},{6,4},{7,5},{8,10},{9,11},{10,... | collective-permute-start | bytes 393224 | tf_op jit(solution)/shard_map/ppermute | solution.py:368
  68.1 4.1 %collective-permute-done.19.b_ref = f32[128,256]{1,0:T(8,128)S(1)} collective-permute-done((f32[128,256]{1,0:T(8,128)S(1)}, f32[128,256]{1,0:T(8,128)S(1)}, u32[]{:S(2)}, u32[]{:S(2)}) %collective-permute-start.19) | collective-permute-done | bytes 131104 | tf_op jit(solution)/shard_map/ppermute | solution.py:368
  72.2 0.5 up_coded.4
  72.7 7.7 %collective-permute-done.16.refs_1_ = bf16[112,2048]{1,0:T(8,128)(2,1)S(1)} collective-permute-done((bf16[112,2048]{1,0:T(8,128)(2,1)S(1)}, bf16[112,2048]{1,0:T(8,128)(2,1)S(1)}, u32[]{:S(2)}, u32[]{:S(2)}) %collective-permute-start.16) | collective-permute-done | bytes 458784 | tf_op jit(solution)/shard_map/ppermute | solution.py:355
  80.4 7.6 %collective-permute-done.17.refs_2_ = bf16[112,2048]{1,0:T(8,128)(2,1)S(1)} collective-permute-done((bf16[112,2048]{1,0:T(8,128)(2,1)S(1)}, bf16[112,2048]{1,0:T(8,128)(2,1)S(1)}, u32[]{:S(2)}, u32[]{:S(2)}) %collective-permute-start.17) | collective-permute-done | bytes 458784 | tf_op jit(solution)/shard_map/ppermute | solution.py:355
  88.0 0.0 collective-permute-done.15.refs_0_
  88.0 1.8 %low_rank.5 = (f32[64,256]{1,0:T(8,128)S(1)}, s32[1,256]{1,0:T(1,128)S(1)}, s32[1]{0:T(128)}) custom-call(s32[1]{0:T(128)} %bitcast.me_ref, bf16[512,2048]{1,0:T(8,128)(2,1)S(1)} %bitcast.11, bf16[160,2048]{1,0:T(8,128)(2,1)S(1)} %collective-permute-done.15.refs_0_, bf16[112,2048]{1,0:T(8,128)(2,1)S(1)} %collective-permute-done.16.refs_1_, ...), custom_call_target="tpu_custom_call" | custom-call | flops 1 | bytes 1 | tf_op jit(solution)/shard_map/low_rank/pallas_call | solution.py:205
  89.8 0.0 copy-start.4
  89.8 0.0 copy-start.5
  89.8 0.1 collective-permute-start.22
  89.9 1.2 %collective-permute-done.22 = f32[64,256]{1,0:T(8,128)S(1)} collective-permute-done((f32[64,256]{1,0:T(8,128)S(1)}, f32[64,256]{1,0:T(8,128)S(1)}, u32[]{:S(2)}, u32[]{:S(2)}) %collective-permute-start.22) | collective-permute-done | bytes 65568 | tf_op jit(solution)/shard_map/ppermute | solution.py:368
  91.1 1.5 %collective-permute-start.23 = (f32[64,256]{1,0:T(8,128)S(1)}, f32[64,256]{1,0:T(8,128)S(1)}, u32[]{:S(2)}, u32[]{:S(2)}) collective-permute-start(f32[64,256]{1,0:T(8,128)S(1)} %add.18.a_ref), channel_id=1, source_target_pairs={{0,2},{1,3},{2,0},{3,1},{4,6},{5,7},{6,4},{7,5},{8,10},{9,11},{10,... | collective-permute-start | bytes 196616 | tf_op jit(solution)/shard_map/ppermute | solution.py:368
  92.7 0.0 collective-permute-start.20
  92.7 2.0 %collective-permute-start.21 = (s16[144,256]{1,0:T(8,128)(2,1)S(1)}, s16[144,256]{1,0:T(8,128)(2,1)S(1)}, u32[]{:S(2)}, u32[]{:S(2)}) collective-permute-start(s16[144,256]{1,0:T(8,128)(2,1)S(1)} %get-tuple-element.88), channel_id=1, source_target_pairs={{0,4},{4,8},{8,12},{12,0},{1,5},{5,9},{9,13},{13,1},{2,6},{6,10},{... | collective-permute-start | bytes 221192 | tf_op jit(solution)/shard_map/ppermute | solution.py:355
  94.7 0.8 collective-permute-done.23.b_ref
  95.4 0.3 up_coded.5
  95.8 0.1 collective-permute-start.24
  95.8 1.2 %collective-permute-done.20.refs_1_ = s16[144,256]{1,0:T(8,128)(2,1)S(1)} collective-permute-done((s16[144,256]{1,0:T(8,128)(2,1)S(1)}, s16[144,256]{1,0:T(8,128)(2,1)S(1)}, u32[]{:S(2)}, u32[]{:S(2)}) %collective-permute-start.20) | collective-permute-done | bytes 73760 | tf_op jit(solution)/shard_map/ppermute | solution.py:355
  97.0 2.4 %collective-permute-done.21.refs_2_ = s16[144,256]{1,0:T(8,128)(2,1)S(1)} collective-permute-done((s16[144,256]{1,0:T(8,128)(2,1)S(1)}, s16[144,256]{1,0:T(8,128)(2,1)S(1)}, u32[]{:S(2)}, u32[]{:S(2)}) %collective-permute-start.21) | collective-permute-done | bytes 73760 | tf_op jit(solution)/shard_map/ppermute | solution.py:355
  99.4 0.4 gather_add.6
  101.7 0.0 collective-permute-done.24.refs_1_
  101.7 1.0 gather_add.7
  (16 shorter events, 0.2 us)
Async XLA Ops:
  0.0 8.7 %copy-start = (bf16[2048,512]{1,0:T(8,128)(2,1)S(1)}, bf16[2048,512]{1,0:T(8,128)(2,1)}, u32[]{:S(2)}) copy-start(bf16[2048,512]{1,0:T(8,128)(2,1)} %value_ref.1) | copy-start | bytes 6291460
  3.6 8.2 %copy-start.1 = (bf16[512,2048]{1,0:T(8,128)(2,1)S(1)}, bf16[512,2048]{1,0:T(8,128)(2,1)}, u32[]{:S(2)}) copy-start(bf16[512,2048]{1,0:T(8,128)(2,1)} %tokens_ref.3) | copy-start | bytes 6291460
  3.6 8.2 %copy-start.2 = (bf16[8,2048,64]{1,2,0:T(8,128)(2,1)S(1)}, bf16[8,2048,64]{1,2,0:T(8,128)(2,1)}, u32[]{:S(2)}) copy-start(bf16[8,2048,64]{1,2,0:T(8,128)(2,1)} %param.12) | copy-start | bytes 6291460
  3.6 30.1 %collective-permute-start.10 = (bf16[272,2048]{1,0:T(8,128)(2,1)S(1)}, bf16[272,2048]{1,0:T(8,128)(2,1)S(1)}, u32[]{:S(2)}, u32[]{:S(2)}) collective-permute-start(bf16[272,2048]{1,0:T(8,128)(2,1)S(1)} %get-tuple-element.75), channel_id=1, source_target_pairs={{0,12},{4,0},{8,4},{12,8},{1,13},{5,1},{9,5},{13,9},{2,14},{6,2},{... | collective-permute-start | bytes 3342344 | tf_op jit(solution)/shard_map/ppermute | solution.py:355
  8.7 49.9 %collective-permute-start.9 = (bf16[272,2048]{1,0:T(8,128)(2,1)S(1)}, bf16[272,2048]{1,0:T(8,128)(2,1)S(1)}, u32[]{:S(2)}, u32[]{:S(2)}) collective-permute-start(bf16[272,2048]{1,0:T(8,128)(2,1)S(1)} %get-tuple-element.73), channel_id=1, source_target_pairs={{0,4},{4,8},{8,12},{12,0},{1,5},{5,9},{9,13},{13,1},{2,6},{6,10},{... | collective-permute-start | bytes 3342344 | tf_op jit(solution)/shard_map/ppermute | solution.py:355
  11.7 4.5 %collective-permute-start.11 = (f32[512,256]{1,0:T(8,128)S(1)}, f32[512,256]{1,0:T(8,128)S(1)}, u32[]{:S(2)}, u32[]{:S(2)}) collective-permute-start(f32[512,256]{1,0:T(8,128)S(1)} %get-tuple-element.79), channel_id=1, source_target_pairs={{0,1},{1,0},{2,3},{3,2},{4,5},{5,4},{6,7},{7,6},{8,9},{9,8},{10,11... | collective-permute-start | bytes 1572872 | tf_op jit(solution)/shard_map/ppermute | solution.py:368
  13.1 1.5 %collective-permute-start.13 = (f32[64,512]{1,0:T(8,128)S(1)}, f32[64,512]{1,0:T(8,128)S(1)}, u32[]{:S(2)}, u32[]{:S(2)}) collective-permute-start(f32[64,512]{1,0:T(8,128)S(1)} %low_rank_home.1), channel_id=1, source_target_pairs={{0,1},{1,0},{2,3},{3,2},{4,5},{5,4},{6,7},{7,6},{8,9},{9,8},{10,11... | collective-permute-start | bytes 393224 | tf_op jit(solution)/shard_map/ppermute | solution.py:368
  14.7 6.4 %collective-permute-start.14 = (f32[64,512]{1,0:T(8,128)S(1)}, f32[64,512]{1,0:T(8,128)S(1)}, u32[]{:S(2)}, u32[]{:S(2)}) collective-permute-start(f32[64,512]{1,0:T(8,128)S(1)} %add.16.a_ref), channel_id=1, source_target_pairs={{0,2},{1,3},{2,0},{3,1},{4,6},{5,7},{6,4},{7,5},{8,10},{9,11},{10,... | collective-permute-start | bytes 393224 | tf_op jit(solution)/shard_map/ppermute | solution.py:368
  16.2 4.8 %copy-start.3 = (bf16[8,64,128]{2,1,0:T(8,128)(2,1)S(1)}, bf16[8,64,128]{2,1,0:T(8,128)(2,1)}, u32[]{:S(2)}) copy-start(bf16[8,64,128]{2,1,0:T(8,128)(2,1)} %param.13) | copy-start | bytes 393220
  16.4 18.8 %collective-permute-start.12 = (f32[512,128]{1,0:T(8,128)S(1)}, f32[512,128]{1,0:T(8,128)S(1)}, u32[]{:S(2)}, u32[]{:S(2)}) collective-permute-start(f32[512,128]{1,0:T(8,128)S(1)} %get-tuple-element.96), channel_id=1, source_target_pairs={{0,2},{1,3},{2,0},{3,1},{4,6},{5,7},{6,4},{7,5},{8,10},{9,11},{10,... | collective-permute-start | bytes 786440 | tf_op jit(solution)/shard_map/ppermute | solution.py:368
  33.7 54.3 %collective-permute-start.15 = (bf16[160,2048]{1,0:T(8,128)(2,1)S(1)}, bf16[160,2048]{1,0:T(8,128)(2,1)S(1)}, u32[]{:S(2)}, u32[]{:S(2)}) collective-permute-start(bf16[160,2048]{1,0:T(8,128)(2,1)S(1)} %get-tuple-element.84), channel_id=1, source_target_pairs={{0,8},{4,12},{8,0},{12,4},{1,9},{5,13},{9,1},{13,5},{2,10},{6,14},... | collective-permute-start | bytes 1966088 | tf_op jit(solution)/shard_map/ppermute | solution.py:355
  58.6 21.8 %collective-permute-start.16 = (bf16[112,2048]{1,0:T(8,128)(2,1)S(1)}, bf16[112,2048]{1,0:T(8,128)(2,1)S(1)}, u32[]{:S(2)}, u32[]{:S(2)}) collective-permute-start(bf16[112,2048]{1,0:T(8,128)(2,1)S(1)} %slice.6), channel_id=1, source_target_pairs={{0,4},{8,12},{1,5},{9,13},{2,6},{10,14},{3,7},{11,15},{16,20},{24,... | collective-permute-start | bytes 1376264 | tf_op jit(solution)/shard_map/ppermute | solution.py:355
  62.1 25.9 %collective-permute-start.17 = (bf16[112,2048]{1,0:T(8,128)(2,1)S(1)}, bf16[112,2048]{1,0:T(8,128)(2,1)S(1)}, u32[]{:S(2)}, u32[]{:S(2)}) collective-permute-start(bf16[112,2048]{1,0:T(8,128)(2,1)S(1)} %slice.7), channel_id=1, source_target_pairs={{4,0},{12,8},{5,1},{13,9},{6,2},{14,10},{7,3},{15,11},{20,16},{28,... | collective-permute-start | bytes 1376264 | tf_op jit(solution)/shard_map/ppermute | solution.py:355
  65.1 1.4 %collective-permute-start.18 = (f32[128,256]{1,0:T(8,128)S(1)}, f32[128,256]{1,0:T(8,128)S(1)}, u32[]{:S(2)}, u32[]{:S(2)}) collective-permute-start(f32[128,256]{1,0:T(8,128)S(1)} %get-tuple-element.86), channel_id=1, source_target_pairs={{0,1},{1,0},{2,3},{3,2},{4,5},{5,4},{6,7},{7,6},{8,9},{9,8},{10,11... | collective-permute-start | bytes 393224 | tf_op jit(solution)/shard_map/ppermute | solution.py:368
  66.6 5.6 %collective-permute-start.19 = (f32[128,256]{1,0:T(8,128)S(1)}, f32[128,256]{1,0:T(8,128)S(1)}, u32[]{:S(2)}, u32[]{:S(2)}) collective-permute-start(f32[128,256]{1,0:T(8,128)S(1)} %add.17.a_ref), channel_id=1, source_target_pairs={{0,2},{1,3},{2,0},{3,1},{4,6},{5,7},{6,4},{7,5},{8,10},{9,11},{10,... | collective-permute-start | bytes 393224 | tf_op jit(solution)/shard_map/ppermute | solution.py:368
  89.8 11.9 %copy-start.4 = (s32[512]{0:T(512)S(1)}, s32[512]{0:T(512)}, u32[]{:S(2)}) copy-start(s32[512]{0:T(512)} %param.9) | copy-start | bytes 6148
  89.8 11.9 %copy-start.5 = (s32[32]{0:T(128)S(1)}, s32[32]{0:T(128)}, u32[]{:S(2)}) copy-start(s32[32]{0:T(128)} %param.10) | copy-start | bytes 388
  89.8 1.3 %collective-permute-start.22 = (f32[64,256]{1,0:T(8,128)S(1)}, f32[64,256]{1,0:T(8,128)S(1)}, u32[]{:S(2)}, u32[]{:S(2)}) collective-permute-start(f32[64,256]{1,0:T(8,128)S(1)} %get-tuple-element.95), channel_id=1, source_target_pairs={{0,1},{1,0},{2,3},{3,2},{4,5},{5,4},{6,7},{7,6},{8,9},{9,8},{10,11... | collective-permute-start | bytes 196616 | tf_op jit(solution)/shard_map/ppermute | solution.py:368
  91.1 4.3 %collective-permute-start.23 = (f32[64,256]{1,0:T(8,128)S(1)}, f32[64,256]{1,0:T(8,128)S(1)}, u32[]{:S(2)}, u32[]{:S(2)}) collective-permute-start(f32[64,256]{1,0:T(8,128)S(1)} %add.18.a_ref), channel_id=1, source_target_pairs={{0,2},{1,3},{2,0},{3,1},{4,6},{5,7},{6,4},{7,5},{8,10},{9,11},{10,... | collective-permute-start | bytes 196616 | tf_op jit(solution)/shard_map/ppermute | solution.py:368
  92.7 4.4 %collective-permute-start.20 = (s16[144,256]{1,0:T(8,128)(2,1)S(1)}, s16[144,256]{1,0:T(8,128)(2,1)S(1)}, u32[]{:S(2)}, u32[]{:S(2)}) collective-permute-start(s16[144,256]{1,0:T(8,128)(2,1)S(1)} %get-tuple-element.87), channel_id=1, source_target_pairs={{0,12},{4,0},{8,4},{12,8},{1,13},{5,1},{9,5},{13,9},{2,14},{6,2},{... | collective-permute-start | bytes 221192 | tf_op jit(solution)/shard_map/ppermute | solution.py:355
  92.7 6.7 %collective-permute-start.21 = (s16[144,256]{1,0:T(8,128)(2,1)S(1)}, s16[144,256]{1,0:T(8,128)(2,1)S(1)}, u32[]{:S(2)}, u32[]{:S(2)}) collective-permute-start(s16[144,256]{1,0:T(8,128)(2,1)S(1)} %get-tuple-element.88), channel_id=1, source_target_pairs={{0,4},{4,8},{8,12},{12,0},{1,5},{5,9},{9,13},{13,1},{2,6},{6,10},{... | collective-permute-start | bytes 221192 | tf_op jit(solution)/shard_map/ppermute | solution.py:355
  95.8 6.0 %collective-permute-start.24 = (s16[144,256]{1,0:T(8,128)(2,1)S(1)}, s16[144,256]{1,0:T(8,128)(2,1)S(1)}, u32[]{:S(2)}, u32[]{:S(2)}) collective-permute-start(s16[144,256]{1,0:T(8,128)(2,1)S(1)} %up_coded.5), channel_id=1, source_target_pairs={{0,8},{4,12},{8,0},{12,4},{1,9},{5,13},{9,1},{13,5},{2,10},{6,14},... | collective-permute-start | bytes 221192 | tf_op jit(solution)/shard_map/ppermute | solution.py:355

commit v5 on v4

--- a/solution.py
+++ b/solution.py
@@ -9,7 +9,6 @@
 
 CAP = 4
 ADAPTER_SCALE = 0.5
-TAGS = 16
 CODE_ROWS = 16
 LINE = 4
 BF16 = jnp.bfloat16
@@ -78,20 +77,30 @@
     return owner, storage, rank.astype(jnp.int32), late_place
 
 
-def known_adapters(storage, picks, flag):
+def lanes(count):
+    return -(-count // 128) * 128
+
+
+def known_adapters(storage, picks, flag, features):
     tokens = storage.shape[1]
     known = jnp.broadcast_to((storage + 1).astype(F32), (8, tokens)).astype(BF16)
-    width = picks[0].shape[0]
-    which = iota((TAGS, width), 0)
-    tags = jnp.where(which == TAGS - 1, flag, 0.0)
-    for k, pick in enumerate(picks):
-        row = dot(known, pick, ((1,), (1,)))
-        tags = jnp.where(which == k, jnp.concatenate([row] * (TAGS // 8), axis=0), tags)
-    return tags.astype(BF16)
+    sections = []
+    for pick in picks:
+        size = pick.shape[0]
+        sections.append(dot(known, pick, ((1,), (1,))))
+        if size % 128:
+            sections.append(jnp.zeros((8, lanes(size) - size), F32))
+    used = sum(x.shape[1] for x in sections)
+    sections += [jnp.full((8, 128), flag, F32), jnp.zeros((8, features - used - 128), F32)]
+    return jnp.concatenate(sections, axis=1)[0:1, :]
+
+
+def last_row(rows, row):
+    return rows + jnp.where(iota(rows.shape, 0) == rows.shape[0] - 1, row, 0.0)
 
 
 def route_pack_kernel(owners, holder, first, late, me_ref, index_hbm, storage_hbm, tokens_hbm, *refs):
-    outs, (dest_ref, home_ids_ref, more_ref, picks, index, storage, tokens, sems) = refs[:3], refs[3:]
+    out, dest_ref, home_ids_ref, more_ref, picks, tags, index, storage, tokens, sems = refs
     tiles, _, tile = tokens.shape
     small = [pltpu.make_async_copy(index_hbm, index, sems.at[tiles])]
     small += [pltpu.make_async_copy(storage_hbm, storage, sems.at[tiles + 1])]
@@ -113,38 +122,31 @@
     more = (jnp.max(place) >= late).astype(jnp.int32)
     more_ref[0] = more
     for s in range(1, owners):
-        slot = jnp.where(place >= 0, first + place, jnp.where(away == s, rank, -1))
+        slot = jnp.where(place >= 0, jnp.where(place < late, first + place, -1), jnp.where(away == s, rank, -1))
         picks[s - 1] = one_hot(iota(picks.shape[1:], 0) == slot)
-    tags = known_adapters(row, [picks[s - 1] for s in range(1, owners)], more.astype(F32))
-    size = first + late
-    for out in (outs[0], outs[2]):
-        out[size:, :] = jnp.zeros((TAGS, out.shape[1]), BF16)
-        out[size:, 0:size] = tags
+    features = out.shape[1]
+    tags[...] = known_adapters(row, [picks[s - 1] for s in range(1, owners)], more.astype(F32), features)
     for i, copy in enumerate(large):
         copy.wait()
         at = slice(i * tile, (i + 1) * tile)
-        for s, rows in ((1, size), (3, first), (2, first)):
-            if s == 3:
-                outs[2][0:first, at] = dot(picks[2, 0:first, :], tokens[i]).astype(BF16)
-                outs[2][first:size, at] = outs[0][first:size, at]
-            else:
-                outs[s - 1][0:rows, at] = dot(picks[s - 1, 0:rows, :], tokens[i]).astype(BF16)
+        out[:, at] = last_row(dot(picks[owners - 2], tokens[i]), tags[:, at]).astype(BF16)
 
 
 def route_pack(me, index_row, storage_row, tokens, owners, holder, first, late):
     count, features = tokens.shape
     tiles = 4 if features % 512 == 0 else 1
     in_hbm = pl.BlockSpec(memory_space=pltpu.HBM)
-    long = first + late + TAGS
+    long = first + late + 1
     return pl.pallas_call(
         functools.partial(route_pack_kernel, owners, holder, first, late),
-        out_shape=[jax.ShapeDtypeStruct((rows, features), BF16) for rows in (long, first, long)]
+        out_shape=[jax.ShapeDtypeStruct((long, features), BF16)]
         + [jax.ShapeDtypeStruct((1, count), jnp.int32)] * 2
         + [jax.ShapeDtypeStruct((1,), jnp.int32)],
         in_specs=[IN_SMEM, in_hbm, in_hbm, in_hbm],
-        out_specs=[IN_VMEM] * 5 + [IN_SMEM],
+        out_specs=[IN_VMEM] * 3 + [IN_SMEM],
         scratch_shapes=[
-            pltpu.VMEM((owners - 1, first + late, count), BF16),
+            pltpu.VMEM((owners - 1, long, count), BF16),
+            pltpu.VMEM((1, features), F32),
             pltpu.VMEM(index_row.shape, jnp.int32),
             pltpu.VMEM(storage_row.shape, jnp.int32),
             pltpu.VMEM((tiles, count, features // tiles), BF16),
@@ -156,18 +158,38 @@
     )(me, index_row, storage_row, tokens)
 
 
+def pack_more_kernel(first, dest_ref, tokens_ref, third_ref, one_out, two_out):
+    dest = dest_ref[...]
+    for s, out in ((1, one_out), (2, two_out)):
+        pick = one_hot(iota((first, dest.shape[1]), 0) + (s - 1) * first == dest)
+        out[0:first, :] = dot(pick, tokens_ref[...]).astype(BF16)
+    one_out[first:, :] = third_ref[first:, :]
+
+
+def pack_more(dest, tokens, third, first):
+    return pl.pallas_call(
+        functools.partial(pack_more_kernel, first),
+        out_shape=[jax.ShapeDtypeStruct(third.shape, BF16), jax.ShapeDtypeStruct((first, tokens.shape[1]), BF16)],
+        in_specs=[IN_VMEM] * 3,
+        out_specs=[IN_VMEM] * 2,
+        compiler_params=params(),
+        cost_estimate=CHEAP,
+        name="pack_more",
+    )(dest, tokens, third)
+
+
 def repack_kernel(start, index_ref, storage_ref, dest_ref, tokens_ref, out):
-    rows = out.shape[0] - TAGS
-    pick = one_hot(iota((rows, dest_ref.shape[1]), 0) + start == dest_ref[...])
-    out[0:rows, :] = dot(pick, tokens_ref[...]).astype(BF16)
-    out[rows:, :] = jnp.zeros((TAGS, out.shape[1]), BF16)
-    out[rows:, 0:rows] = known_adapters(storage_of(index_ref[...], storage_ref[...]), [pick], 0.0)
+    rows = out.shape[0] - 1
+    row = iota((rows + 1, dest_ref.shape[1]), 0)
+    pick = one_hot((row < rows) & (row + start == dest_ref[...]))
+    tags = known_adapters(storage_of(index_ref[...], storage_ref[...]), [pick], 0.0, out.shape[1])
+    out[...] = last_row(dot(pick, tokens_ref[...]), tags).astype(BF16)
 
 
 def repack(index_row, storage_row, dest, tokens, start, rows):
     return pl.pallas_call(
         functools.partial(repack_kernel, start),
-        out_shape=jax.ShapeDtypeStruct((rows + TAGS, tokens.shape[1]), BF16),
+        out_shape=jax.ShapeDtypeStruct((rows + 1, tokens.shape[1]), BF16),
         in_specs=[IN_VMEM] * 4,
         out_specs=IN_VMEM,
         compiler_params=params(),
@@ -179,16 +201,17 @@
     out, ids_out, flag = refs[-3:]
     lead = me_ref[0] * holder + 1
     flags = jnp.zeros((1, 1), F32)
-    for k, (rows, sources, tagged, row, tag_start) in enumerate(blocks):
+    for k, (rows, sources, tagged, section, flag_at, column) in enumerate(blocks):
         rows_in = functools.reduce(jnp.add, [refs[j][at : at + rows, :] for j, at in sources])
         every = dot(down_ref[...], rows_in, ((1,), (1,)))
-        tags = functools.reduce(jnp.add, [refs[j][at : at + TAGS, :].astype(F32) for j, at in tagged])
-        flags = jnp.maximum(flags, tags[TAGS - 1 : TAGS, 0:1])
-        ids = tags[row : row + 1, tag_start : tag_start + rows].astype(jnp.int32) - lead
+        tags = [refs[j][refs[j].shape[0] - 16 :, 0 : flag_at + 128].astype(F32)[15:16, :] for j in tagged]
+        tags = functools.reduce(jnp.add, tags)
+        flags = jnp.maximum(flags, tags[:, flag_at : flag_at + 1])
+        ids = tags[:, section + column : section + column + rows].astype(jnp.int32) - lead
         total = jnp.zeros((rank, rows), F32)
         for a in range(holder):
             total = total + jnp.where(ids == a, every[a * rank : (a + 1) * rank, :], 0.0)
-        at = slice(tag_start, tag_start + rows)
+        at = slice(column, column + rows)
         if joined:
             out[:, at] = total
             ids_out[:, at] = ids
@@ -266,20 +289,24 @@
 
 def up_coded_kernel(holder, rank, ids_ref, up_ref, a_ref, b_ref, *outs):
     up = up_ref[...]
-    width = up.shape[1]
     for k, out in enumerate(outs):
         own = slice(k * rank, (k + 1) * rank)
         low = a_ref[own, :] + b_ref[own, :]
         ids = ids_ref[k : k + 1, :]
         spread = jnp.concatenate([jnp.where(ids == a, low, 0.0) for a in range(holder)], axis=0)
         high, rest = split_bf16(spread)
-        term = ADAPTER_SCALE * (dot(up, high, ((0,), (0,))) + dot(up, rest, ((0,), (0,))))
-        largest = jnp.maximum(jnp.max(jnp.abs(term), axis=0, keepdims=True), 1e-30)
+        term = ADAPTER_SCALE * (dot(high, up, ((0,), (0,))) + dot(rest, up, ((0,), (0,))))
+        largest = jnp.maximum(jnp.max(jnp.abs(term), axis=1, keepdims=True), 1e-30)
         exponent = jnp.floor(jnp.log2(largest)) + 1.0
         code = jnp.clip(jnp.round(term * jnp.exp2(15.0 - exponent)), -32767.0, 32767.0)
-        out[0:width, :] = code.astype(jnp.int32).astype(jnp.int16)
-        exponents = jnp.broadcast_to(exponent, (out.shape[0] - width, out.shape[1]))
-        out[width:, :] = exponents.astype(jnp.int32).astype(jnp.int16)
+        rows = term.shape[0]
+        out[0:rows, :] = code.astype(jnp.int32).astype(jnp.int16)
+        square = (rows, lanes(rows))
+        exponent = jnp.sum(jnp.where(iota(square, 0) == iota(square, 1), exponent, 0.0), axis=0, keepdims=True)
+        tail = jnp.zeros((CODE_ROWS, 128), F32)
+        for j in range(lanes(rows) // 128):
+            tail = jnp.where(iota(tail.shape, 0) == j, exponent[:, j * 128 : (j + 1) * 128], tail)
+        out[rows:, :] = tail.astype(jnp.int32).astype(jnp.int16)
 
 
 def up_coded(ids, up, a, b, holder):
@@ -287,7 +314,7 @@
     rank = up.shape[0] // holder
     return pl.pallas_call(
         functools.partial(up_coded_kernel, holder, rank),
-        out_shape=[jax.ShapeDtypeStruct((up.shape[1] + CODE_ROWS, rows), jnp.int16)] * blocks,
+        out_shape=[jax.ShapeDtypeStruct((rows + CODE_ROWS, up.shape[1]), jnp.int16)] * blocks,
         in_specs=[IN_VMEM] * 4,
         out_specs=[IN_VMEM] * blocks,
         compiler_params=params(),
@@ -324,18 +351,20 @@
     for k in range(1, terms):
         total = total + refs[k][...]
     dest = dest_ref[...]
-    found = jnp.zeros((total.shape[1], total.shape[0]), F32)
     for (start, rows, late_start), ref in zip(ranges, refs[terms:]):
-        width = total.shape[1]
-        exponent = ref[width:, :].astype(jnp.int32).astype(F32)[0:1, :]
-        values = ref[0:width, :].astype(jnp.int32).astype(F32) * jnp.exp2(exponent - 15.0)
-        shape = (values.shape[1], dest.shape[1])
-        row = iota(shape, 0)
+        size = ref.shape[0] - CODE_ROWS
+        tail = ref[size:, :].astype(jnp.int32).astype(F32)
+        diagonal = iota((128, 128), 0) == iota((128, 128), 1)
+        exponents = [
+            jnp.sum(jnp.where(diagonal, tail[j : j + 1, :], 0.0), axis=1, keepdims=True)[0 : min(128, size - j * 128), :]
+            for j in range(lanes(size) // 128)
+        ]
+        scale = jnp.exp2(jnp.concatenate(exponents, axis=0) - 15.0)
+        values = ref[0:size, :].astype(jnp.int32).astype(F32) * scale
+        row = iota((size, dest.shape[1]), 0)
         pick = one_hot(jnp.where(row < rows, row + start, row + (late_start - rows)) == dest)
         high, rest = split_bf16(values)
-        found = found + (dot(high, pick) + dot(rest, pick))
-    if ranges:
-        total = total + found.T
+        total = total + (dot(pick, high, ((0,), (0,))) + dot(pick, rest, ((0,), (0,))))
     refs[-1][...] = total.astype(refs[-1].dtype)
 
 
@@ -361,7 +390,8 @@
 
 
 def opposite(before, after):
-    return along(before, [(0, 1), (2, 3)]), along(after, [(1, 0), (3, 2)])
+    even = lax.axis_index("own") % 2 == 0
+    return along(jnp.where(even, before, after), [(0, 1), (1, 0), (2, 3), (3, 2)])
 
 
 def partner(x, bit):
@@ -376,8 +406,7 @@
     return x, partner(x, bit)
 
 
-def base_terms(me, tokens, value, parts):
-    kept, away = base_blocks(me, tokens, value, parts)
+def base_terms(kept, away, parts):
     bit = 1
     while 2 * bit < parts:
         total = kept + partner(away, bit)
@@ -392,8 +421,8 @@
     count = tokens.shape[0]
     holder, _, rank = down_stored.shape
     cap = CAP * (2 * count // CAP // owners)
-    first = cap * 5 // 8 // 16 * 16
-    late = cap - first
+    first = cap * 9 // 16 // 16 * 16
+    late = cap - first + 15
     me = lax.axis_index("own").astype(jnp.int32).reshape(1)
     me_part = lax.axis_index("tp").astype(jnp.int32).reshape(1)
     index_row = token_adapter_index.reshape(1, count)
@@ -404,39 +433,55 @@
     late_start = (owners - 1) * first
 
     mains = {s: ((s - 1) * first, first) for s in shifts}
-    size = first + late
-    *packed, dest, home_ids, more = route_pack(me, index_row, storage_row, tokens, owners, holder, first, late)
-    packed, me_part, home_ids = lax.optimization_barrier((packed, me_part, home_ids))
-    below, above = shifted(packed[0], 1), shifted(packed[2], 3)
-    base = base_terms(me_part, tokens, value_matrix, parts)
+    size = first + late + 1
+    part = lanes(size)
+    flag_at = 3 * part
+    third, dest, home_ids, more = route_pack(me, index_row, storage_row, tokens, owners, holder, first, late)
+    third, me_part, home_ids = lax.optimization_barrier((third, me_part, home_ids))
+    above = shifted(third, 3)
+    blocks = base_blocks(me_part, tokens, value_matrix, parts)
+    blocks, dest = lax.optimization_barrier((blocks, dest))
+    one, two = pack_more(dest, tokens, third, first)
+    below = shifted(one, 1)
+    base = base_terms(*blocks, parts)
     lows = two_terms(low_rank_home(home_ids, down, tokens, holder))
     (stays,) = up_project(home_ids, up, *lows, holder)
     total = gather_add(dest, [], [*base, ADAPTER_SCALE * stays], [], F32)
-    rest, above = lax.optimization_barrier((packed[1], above))
+    rest, above, total = lax.optimization_barrier((two, above, total))
     across = shifted(rest, 2)
-    below, above, total = lax.optimization_barrier((below, above, total))
+
+    def near_round(s, message):
+        lows, ids, more = low_rank(me, down, [(size, [(0, 0)], [0], (s - 1) * part, flag_at, 0)], [message], holder)
+        (done,) = up_coded(ids, up, *two_terms(lows), holder)
+        return done, more
+
+    above_done, above_more = near_round(3, above)
+    above_back = shifted(above_done, -3)
+    below, above_done = lax.optimization_barrier((below, above_done))
     far = opposite(below[first:], above[first:])
-    blocks = [(size, [(j, 0)], [(j, size)], s - 1, 0) for j, s in enumerate((1, 3))]
-    lows, ids, near_more = low_rank(me, down, blocks, [below, above], holder)
-    near = up_coded(ids, up, *two_terms(lows), holder)
-    back = [shifted(x, -s) for s, x in zip((1, 3), near)]
+    below_done, below_more = near_round(1, below)
+    near = [below_done, above_done]
+    near_more = jnp.maximum(below_more, above_more)
+    back = [shifted(below_done, -1), above_back]
     total = gather_add(dest, [(*mains[s], late_start) for s in (1, 3)], [total], back, F32)
 
     def second(total):
         x = repack(index_row, storage_row, dest, tokens, late_start + late, late)
         below, above = shifted(x, 1), shifted(x, 3)
-        x = [below, *opposite(below, above), above]
-        sources = [[0], [1, 2], [3]]
-        blocks = [(late, [(j, 0) for j in js], [(j, late) for j in js], 0, 0) for js in sources]
+        x = [below, opposite(below, above), above]
+        sources = [[0], [1], [2]]
+        blocks = [(late + 1, [(j, 0) for j in js], js, 0, lanes(late + 1), 0) for js in sources]
         lows, ids, _ = low_rank(me, down, blocks, x, holder)
         done = up_coded(ids, up, *two_terms(lows), holder)
         back = [shifted(x, -s) for s, x in zip(shifts, done)]
-        return gather_add(dest, [(late_start + late, late, 0)] * len(back), [total], back, F32)
+        return gather_add(dest, [(late_start + late, late + 1, 0)] * len(back), [total], back, F32)
 
     across, far, near = lax.optimization_barrier((across, far, near))
-    tags = [(j, late) for j in (1, 2)]
-    joined = [(first, [(0, 0)], tags, 1, 0), (late, [(1, 0), (2, 0)], tags, 1, first)]
-    lows, ids, far_more = low_rank(me, down, joined, [across, *far], holder, joined=True)
+    joined = [
+        (first, [(0, 0)], [1], part, flag_at, 0),
+        (late + 1, [(1, 0)], [1], part, flag_at, first),
+    ]
+    lows, ids, far_more = low_rank(me, down, joined, [across, far], holder, joined=True)
     (done,) = up_coded(ids, up, *two_terms(lows), holder)
     more = jnp.maximum(more[0], jnp.maximum(near_more[0], far_more[0]))
     total = lax.cond(more > 0, second, lambda total: total, total)
@@ -476,12 +521,20 @@
     return mixed.astype(BF16)
 
 
+def per_device(tokens, token_adapter_index, adapter_storage_row, value_matrix, down_stored, up_stored):
+    owners, parts = lax.axis_size("own"), lax.axis_size("tp")
+    count, features = tokens.shape
+    cap = CAP * (2 * count // CAP // owners)
+    on_a_line = owners == LINE and parts > 1 and parts & (parts - 1) == 0
+    whole_tiles = cap % 256 == 0 and up_stored.shape[2] == 128 and features >= 3 * lanes(cap + 16) + 128
+    countable = adapter_storage_row.shape[0] < 256 and cap + 16 <= CODE_ROWS * 128
+    body = direct if on_a_line and whole_tiles and countable else by_all_to_all
+    return body(tokens, token_adapter_index, adapter_storage_row, value_matrix, down_stored, up_stored)
+
+
 def solution(mesh):
-    owners, parts = mesh.shape["own"], mesh.shape["tp"]
-    on_a_line = owners == LINE and parts > 1 and parts & (parts - 1) == 0
-    body = direct if on_a_line else by_all_to_all
     return jax.shard_map(
-        body,
+        per_device,
         mesh=mesh,
         in_specs=(
             P(("rep", "own"), "tp"),

time: 103 us -> 99.9 us (0.970)
  waiting for transfers between devices: 66.8 us -> 55.1 us
  Pallas kernels: 14.2 us -> 20.3 us
  starting transfers between devices: 19.4 us -> 21.1 us
    ppermute x8 -> x7, waiting for transfers between devices: 54.3 us -> 36.3 us  [along(): return lax.ppermute(x, 'own', pairs)]
    ppermute x8 -> x10, waiting for transfers between devices: 12.5 us -> 18.8 us  [partner(): lax.ppermute(x, 'tp', [(i, i ^ bit) for i in range(lax.axis_size('tp'))])]
    pallas_call x2 -> x3, Pallas kernels: 3.51 us -> 6.94 us  [low_rank(): pl.pallas_call(functools.partial(low_rank_kernel, blocks, joined, holder,...]
    pallas_call x0 -> x1, Pallas kernels: none -> 1.76 us  [pack_more(): pl.pallas_call(functools.partial(pack_more_kernel, first), out_shape=[jax...]
    ppermute x8 -> x10, starting transfers between devices: 6.04 us -> 7.67 us  [partner(): lax.ppermute(x, 'tp', [(i, i ^ bit) for i in range(lax.axis_size('tp'))])]
    ppermute x8 -> x7, starting transfers between devices: 13.4 us -> 13.4 us  [along(): return lax.ppermute(x, 'own', pairs)]
  transfers between devices with their start and end apart: 16 -> 17, of which waited for: 12 -> 13; matrix products, arithmetic and copies ran while one was open for 0% -> 0% of each run, Pallas kernels for 8% -> 14%
where the time goes in v5:
time: 99.9 us; the launch traced here: 99.8 us
  waiting for transfers between devices  55.1 us (55%)
  starting transfers between devices  21.1 us (21%)
  Pallas kernels  20.3 us (20%)
  between operations  2.78 us (3%)
    ppermute x7, waiting for transfers between devices, along(): return lax.ppermute(x, 'own', pairs)  36.3 us
    ppermute x10, waiting for transfers between devices, partner(): lax.ppermute(x, 'tp', [(i, i ^ bit) for i in range(lax.axis_size('tp'))])  18.8 us
    ppermute x7, starting transfers between devices, along(): return lax.ppermute(x, 'own', pairs)  13.4 us
    ppermute x10, starting transfers between devices, partner(): lax.ppermute(x, 'tp', [(i, i ^ bit) for i in range(lax.axis_size('tp'))])  7.67 us
    pallas_call x3, Pallas kernels, low_rank(): pl.pallas_call(functools.partial(low_rank_kernel, blocks, joined, holder,...  6.94 us
    pallas_call x1, Pallas kernels, route_pack(): pl.pallas_call(functools.partial(route_pack_kernel, owners, holder, first...  3.17 us
    pallas_call x1, Pallas kernels, base_blocks(): pl.pallas_call(functools.partial(base_kernel, parts), out_shape=[jax.Shap...  2.97 us
    pallas_call x3, Pallas kernels, gather_add(): pl.pallas_call(functools.partial(gather_add_kernel, ranges, len(terms)),...  2.09 us
  transfers between devices with their start and end apart: 17, of which 13 were waited for; matrix products, arithmetic and copies ran while one was open for 0% of the time, Pallas kernels for 14%

profile of v5, /device:TPU:0, one launch (start us, length us, event | category | flops | bytes accessed | tf_op | source)
XLA Modules:
  0.0 99.8 jit_solution(5431796410132013460)
XLA Ops:
  0.0 3.2 %route_pack.1 = (bf16[272,2048]{1,0:T(8,128)(2,1)S(1)}, s32[1,512]{1,0:T(1,128)S(1)}, s32[1,512]{1,0:T(1,128)S(1)}, s32[1]{0:T(128)}) custom-call(s32[1]{0:T(128)} %bitcast.me_ref, s32[1,512]{1,0:T(1,128)} %bitcast.19, s32[1,32]{1,0:T(1,128)} %bitcast.21, bf16[512,2048]{1,0:T(8,128)(2,1)} %tokens_ref.5), custom_call_target="tpu_custom_call" | custom-call | flops 1 | bytes 1 | tf_op jit(solution)/shard_map/route_pack/pallas_call | solution.py:140
  3.2 5.1 %collective-permute-start.9 = (bf16[272,2048]{1,0:T(8,128)(2,1)S(1)}, bf16[272,2048]{1,0:T(8,128)(2,1)S(1)}, u32[]{:S(2)}, u32[]{:S(2)}) collective-permute-start(bf16[272,2048]{1,0:T(8,128)(2,1)S(1)} %get-tuple-element.75.third_ref), channel_id=1, source_target_pairs={{0,12},{4,0},{8,4},{12,8},{1,13},{5,1},{9,5},{13,9},{2,14},{6,2},{... | collective-permute-start | bytes 3342344 | tf_op jit(solution)/shard_map/ppermute | solution.py:384
  8.3 3.0 %base_blocks.1 = (f32[512,256]{1,0:T(8,128)S(1)}, f32[512,256]{1,0:T(8,128)S(1)}) custom-call(s32[1]{0:T(128)} %bitcast.3.me_ref, bf16[512,2048]{1,0:T(8,128)(2,1)} %tokens_ref.5, bf16[2048,512]{1,0:T(8,128)(2,1)S(1)} %copy-done), custom_call_target="tpu_custom_call" | custom-call | flops 1 | bytes 1 | tf_op jit(solution)/shard_map/base_blocks/pallas_call | solution.py:337
  11.3 0.0 copy-start.2
  11.3 0.1 collective-permute-start.10
  11.4 1.8 %pack_more.1 = (bf16[272,2048]{1,0:T(8,128)(2,1)}, bf16[144,2048]{1,0:T(8,128)(2,1)S(1)}) custom-call(s32[1,512]{1,0:T(1,128)S(1)} %get-tuple-element.73.dest_ref, bf16[512,2048]{1,0:T(8,128)(2,1)S(1)} %copy-done.1, bf16[272,2048]{1,0:T(8,128)(2,1)S(1)} %get-tuple-element.75.third_ref), custom_call_target="tpu_custom_call" | custom-call | flops 1 | bytes 1 | tf_op jit(solution)/shard_map/pack_more/pallas_call | solution.py:170
  13.1 1.3 %low_rank_home.1 = f32[64,512]{1,0:T(8,128)S(1)} custom-call(s32[1,512]{1,0:T(1,128)S(1)} %get-tuple-element.80.ids_ref, bf16[512,2048]{1,0:T(8,128)(2,1)S(1)} %bitcast.10, bf16[512,2048]{1,0:T(8,128)(2,1)S(1)} %copy-done.1), custom_call_target="tpu_custom_call" | custom-call | flops 1 | bytes 1 | tf_op jit(solution)/shard_map/low_rank_home/pallas_call | solution.py:254
  14.4 0.5 collective-permute-start.12
  15.0 1.0 collective-permute-done.12
  16.0 0.0 copy-start.5
  16.0 1.6 %collective-permute-start.13 = (f32[64,512]{1,0:T(8,128)S(1)}, f32[64,512]{1,0:T(8,128)S(1)}, u32[]{:S(2)}, u32[]{:S(2)}) collective-permute-start(f32[64,512]{1,0:T(8,128)S(1)} %add.26.a_ref), channel_id=1, source_target_pairs={{0,2},{1,3},{2,0},{3,1},{4,6},{5,7},{6,4},{7,5},{8,10},{9,11},{10,... | collective-permute-start | bytes 393224 | tf_op jit(solution)/shard_map/ppermute | solution.py:398
  17.6 0.1 add.25
  17.7 0.6 collective-permute-start.11
  18.3 4.1 %collective-permute-done.13.b_ref = f32[64,512]{1,0:T(8,128)S(1)} collective-permute-done((f32[64,512]{1,0:T(8,128)S(1)}, f32[64,512]{1,0:T(8,128)S(1)}, u32[]{:S(2)}, u32[]{:S(2)}) %collective-permute-start.13) | collective-permute-done | bytes 131104 | tf_op jit(solution)/shard_map/ppermute | solution.py:398
  22.4 0.5 up_project.1
  22.9 4.5 %collective-permute-done.11.refs_1_ = f32[512,128]{1,0:T(8,128)S(1)} collective-permute-done((f32[512,128]{1,0:T(8,128)S(1)}, f32[512,128]{1,0:T(8,128)S(1)}, u32[]{:S(2)}, u32[]{:S(2)}) %collective-permute-start.11) | collective-permute-done | bytes 262176 | tf_op jit(solution)/shard_map/ppermute | solution.py:398
  27.5 5.8 %collective-permute-done.9.refs_0_ = bf16[272,2048]{1,0:T(8,128)(2,1)S(1)} collective-permute-done((bf16[272,2048]{1,0:T(8,128)(2,1)S(1)}, bf16[272,2048]{1,0:T(8,128)(2,1)S(1)}, u32[]{:S(2)}, u32[]{:S(2)}) %collective-permute-start.9) | collective-permute-done | bytes 1114144 | tf_op jit(solution)/shard_map/ppermute | solution.py:384
  33.3 1.7 %low_rank.5 = (f32[64,272]{1,0:T(8,128)S(1)}, s32[1,272]{1,0:T(1,128)S(1)}, s32[1]{0:T(128)}) custom-call(s32[1]{0:T(128)} %bitcast.me_ref, bf16[512,2048]{1,0:T(8,128)(2,1)S(1)} %bitcast.11, bf16[272,2048]{1,0:T(8,128)(2,1)S(1)} %collective-permute-done.9.refs_0_), custom_call_target="tpu_custom_call" | custom-call | flops 1 | bytes 1 | tf_op jit(solution)/shard_map/low_rank/pallas_call | solution.py:228
  35.0 0.1 collective-permute-start.14
  35.1 1.3 %collective-permute-done.14 = f32[64,272]{1,0:T(8,128)S(1)} collective-permute-done((f32[64,272]{1,0:T(8,128)S(1)}, f32[64,272]{1,0:T(8,128)S(1)}, u32[]{:S(2)}, u32[]{:S(2)}) %collective-permute-start.14) | collective-permute-done | bytes 69664 | tf_op jit(solution)/shard_map/ppermute | solution.py:398
  36.4 1.6 %collective-permute-start.15 = (f32[64,272]{1,0:T(8,128)S(1)}, f32[64,272]{1,0:T(8,128)S(1)}, u32[]{:S(2)}, u32[]{:S(2)}) collective-permute-start(f32[64,272]{1,0:T(8,128)S(1)} %add.27.a_ref), channel_id=1, source_target_pairs={{0,2},{1,3},{2,0},{3,1},{4,6},{5,7},{6,4},{7,5},{8,10},{9,11},{10,... | collective-permute-start | bytes 208904 | tf_op jit(solution)/shard_map/ppermute | solution.py:398
  38.0 1.4 %collective-permute-start.16 = (bf16[144,2048]{1,0:T(8,128)(2,1)S(1)}, bf16[144,2048]{1,0:T(8,128)(2,1)S(1)}, u32[]{:S(2)}, u32[]{:S(2)}) collective-permute-start(bf16[144,2048]{1,0:T(8,128)(2,1)S(1)} %get-tuple-element.87), channel_id=1, source_target_pairs={{0,8},{4,12},{8,0},{12,4},{1,9},{5,13},{9,1},{13,5},{2,10},{6,14},... | collective-permute-start | bytes 1769480 | tf_op jit(solution)/shard_map/ppermute | solution.py:384
  39.4 1.9 %collective-permute-done.15.b_ref = f32[64,272]{1,0:T(8,128)S(1)} collective-permute-done((f32[64,272]{1,0:T(8,128)S(1)}, f32[64,272]{1,0:T(8,128)S(1)}, u32[]{:S(2)}, u32[]{:S(2)}) %collective-permute-start.15) | collective-permute-done | bytes 69664 | tf_op jit(solution)/shard_map/ppermute | solution.py:398
  41.3 0.5 up_coded.5
  41.9 16.3 %collective-permute-done.8.refs_0_ = bf16[272,2048]{1,0:T(8,128)(2,1)S(1)} collective-permute-done((bf16[272,2048]{1,0:T(8,128)(2,1)}, bf16[272,2048]{1,0:T(8,128)(2,1)S(1)}, u32[]{:S(2)}, u32[]{:S(2)}) %collective-permute-start.8) | collective-permute-done | bytes 1114144 | tf_op jit(solution)/shard_map/ppermute | solution.py:384
  58.1 0.1 slice_select_fusion
  58.2 1.6 %collective-permute-start.17 = (bf16[128,2048]{1,0:T(8,128)(2,1)S(1)}, bf16[128,2048]{1,0:T(8,128)(2,1)S(1)}, u32[]{:S(2)}, u32[]{:S(2)}) collective-permute-start(bf16[128,2048]{1,0:T(8,128)(2,1)S(1)} %slice_select_fusion), channel_id=1, source_target_pairs={{0,4},{4,0},{8,12},{12,8},{1,5},{5,1},{9,13},{13,9},{2,6},{6,2},{1... | collective-permute-start | bytes 1572872 | tf_op jit(solution)/shard_map/ppermute | solution.py:384
  59.8 3.5 %low_rank.6 = (f32[64,272]{1,0:T(8,128)S(1)}, s32[1,272]{1,0:T(1,128)S(1)}, s32[1]{0:T(128)}) custom-call(s32[1]{0:T(128)} %bitcast.me_ref, bf16[512,2048]{1,0:T(8,128)(2,1)} %bitcast.9, bf16[272,2048]{1,0:T(8,128)(2,1)S(1)} %collective-permute-done.8.refs_0_), custom_call_target="tpu_custom_call" | custom-call | flops 1 | bytes 1 | tf_op jit(solution)/shard_map/low_rank/pallas_call | solution.py:228
  63.3 0.1 collective-permute-start.18
  63.3 1.3 %collective-permute-done.18 = f32[64,272]{1,0:T(8,128)S(1)} collective-permute-done((f32[64,272]{1,0:T(8,128)S(1)}, f32[64,272]{1,0:T(8,128)S(1)}, u32[]{:S(2)}, u32[]{:S(2)}) %collective-permute-start.18) | collective-permute-done | bytes 69664 | tf_op jit(solution)/shard_map/ppermute | solution.py:398
  64.6 1.6 %collective-permute-start.19 = (f32[64,272]{1,0:T(8,128)S(1)}, f32[64,272]{1,0:T(8,128)S(1)}, u32[]{:S(2)}, u32[]{:S(2)}) collective-permute-start(f32[64,272]{1,0:T(8,128)S(1)} %add.29.a_ref), channel_id=1, source_target_pairs={{0,2},{1,3},{2,0},{3,1},{4,6},{5,7},{6,4},{7,5},{8,10},{9,11},{10,... | collective-permute-start | bytes 208904 | tf_op jit(solution)/shard_map/ppermute | solution.py:398
  66.2 3.4 %collective-permute-done.19.b_ref = f32[64,272]{1,0:T(8,128)S(1)} collective-permute-done((f32[64,272]{1,0:T(8,128)S(1)}, f32[64,272]{1,0:T(8,128)S(1)}, u32[]{:S(2)}, u32[]{:S(2)}) %collective-permute-start.19) | collective-permute-done | bytes 69664 | tf_op jit(solution)/shard_map/ppermute | solution.py:398
  69.6 0.5 up_coded.6
  70.1 12.2 %collective-permute-done.16.refs_0_ = bf16[144,2048]{1,0:T(8,128)(2,1)S(1)} collective-permute-done((bf16[144,2048]{1,0:T(8,128)(2,1)S(1)}, bf16[144,2048]{1,0:T(8,128)(2,1)S(1)}, u32[]{:S(2)}, u32[]{:S(2)}) %collective-permute-start.16) | collective-permute-done | bytes 589856 | tf_op jit(solution)/shard_map/ppermute | solution.py:384
  82.3 0.7 collective-permute-done.17.refs_1_
  83.0 1.8 %low_rank.7 = (f32[64,272]{1,0:T(8,128)S(1)}, s32[1,272]{1,0:T(1,128)S(1)}, s32[1]{0:T(128)}) custom-call(s32[1]{0:T(128)} %bitcast.me_ref, bf16[512,2048]{1,0:T(8,128)(2,1)S(1)} %bitcast.12, bf16[144,2048]{1,0:T(8,128)(2,1)S(1)} %collective-permute-done.16.refs_0_, bf16[128,2048]{1,0:T(8,128)(2,1)S(1)} %collective-permute-done.17.refs_1_), custom_call_target="tpu_custom_call" | custom-call | flops 1 | bytes 1 | tf_op jit(solution)/shard_map/low_rank/pallas_call | solution.py:228
  84.7 0.0 copy-start.6
  84.7 0.0 copy-start.7
  84.8 0.1 collective-permute-start.22
  84.8 1.3 %collective-permute-done.22 = f32[64,272]{1,0:T(8,128)S(1)} collective-permute-done((f32[64,272]{1,0:T(8,128)S(1)}, f32[64,272]{1,0:T(8,128)S(1)}, u32[]{:S(2)}, u32[]{:S(2)}) %collective-permute-start.22) | collective-permute-done | bytes 69664 | tf_op jit(solution)/shard_map/ppermute | solution.py:398
  86.1 1.6 %collective-permute-start.23 = (f32[64,272]{1,0:T(8,128)S(1)}, f32[64,272]{1,0:T(8,128)S(1)}, u32[]{:S(2)}, u32[]{:S(2)}) collective-permute-start(f32[64,272]{1,0:T(8,128)S(1)} %add.30.a_ref), channel_id=1, source_target_pairs={{0,2},{1,3},{2,0},{3,1},{4,6},{5,7},{6,4},{7,5},{8,10},{9,11},{10,... | collective-permute-start | bytes 208904 | tf_op jit(solution)/shard_map/ppermute | solution.py:398
  87.7 3.8 %collective-permute-start.20 = (s16[288,128]{1,0:T(8,128)(2,1)S(1)}, s16[288,128]{1,0:T(8,128)(2,1)S(1)}, u32[]{:S(2)}, u32[]{:S(2)}) collective-permute-start(s16[288,128]{1,0:T(8,128)(2,1)S(1)} %up_coded.6), channel_id=1, source_target_pairs={{0,12},{4,0},{8,4},{12,8},{1,13},{5,1},{9,5},{13,9},{2,14},{6,2},{... | collective-permute-start | bytes 221192 | tf_op jit(solution)/shard_map/ppermute | solution.py:384
  91.5 0.5 up_coded.7
  92.1 1.5 %collective-permute-start.24 = (s16[288,128]{1,0:T(8,128)(2,1)S(1)}, s16[288,128]{1,0:T(8,128)(2,1)S(1)}, u32[]{:S(2)}, u32[]{:S(2)}) collective-permute-start(s16[288,128]{1,0:T(8,128)(2,1)S(1)} %up_coded.7), channel_id=1, source_target_pairs={{0,8},{4,12},{8,0},{12,4},{1,9},{5,13},{9,1},{13,5},{2,10},{6,14},... | collective-permute-start | bytes 221192 | tf_op jit(solution)/shard_map/ppermute | solution.py:384
  94.9 0.8 gather_add.6
  96.9 0.2 conditional.1
  97.2 1.4 %collective-permute-done.24.refs_1_ = s16[288,128]{1,0:T(8,128)(2,1)S(1)} collective-permute-done((s16[288,128]{1,0:T(8,128)(2,1)S(1)}, s16[288,128]{1,0:T(8,128)(2,1)S(1)}, u32[]{:S(2)}, u32[]{:S(2)}) %collective-permute-start.24) | collective-permute-done | bytes 73760 | tf_op jit(solution)/shard_map/ppermute | solution.py:384
  98.5 1.2 %gather_add.7 = bf16[512,128]{1,0:T(8,128)(2,1)} custom-call(s32[1,512]{1,0:T(1,128)S(1)} %get-tuple-element.73.dest_ref, f32[512,128]{1,0:T(8,128)S(1)} %get-tuple-element.98.refs_0_, s16[288,128]{1,0:T(8,128)(2,1)S(1)} %collective-permute-done.24.refs_1_), custom_call_target="tpu_custom_call" | custom-call | flops 1 | bytes 1 | tf_op jit(solution)/shard_map/gather_add/pallas_call | solution.py:372
  (23 shorter events, 0.2 us)
Async XLA Ops:
  0.0 8.3 %copy-start = (bf16[2048,512]{1,0:T(8,128)(2,1)S(1)}, bf16[2048,512]{1,0:T(8,128)(2,1)}, u32[]{:S(2)}) copy-start(bf16[2048,512]{1,0:T(8,128)(2,1)} %value_ref.1) | copy-start | bytes 6291460
  3.2 8.2 %copy-start.1 = (bf16[512,2048]{1,0:T(8,128)(2,1)S(1)}, bf16[512,2048]{1,0:T(8,128)(2,1)}, u32[]{:S(2)}) copy-start(bf16[512,2048]{1,0:T(8,128)(2,1)} %tokens_ref.5) | copy-start | bytes 6291460
  3.2 30.1 %collective-permute-start.9 = (bf16[272,2048]{1,0:T(8,128)(2,1)S(1)}, bf16[272,2048]{1,0:T(8,128)(2,1)S(1)}, u32[]{:S(2)}, u32[]{:S(2)}) collective-permute-start(bf16[272,2048]{1,0:T(8,128)(2,1)S(1)} %get-tuple-element.75.third_ref), channel_id=1, source_target_pairs={{0,12},{4,0},{8,4},{12,8},{1,13},{5,1},{9,5},{13,9},{2,14},{6,2},{... | collective-permute-start | bytes 3342344 | tf_op jit(solution)/shard_map/ppermute | solution.py:384
  11.3 1.9 %copy-start.2 = (bf16[8,2048,64]{1,2,0:T(8,128)(2,1)S(1)}, bf16[8,2048,64]{1,2,0:T(8,128)(2,1)}, u32[]{:S(2)}) copy-start(bf16[8,2048,64]{1,2,0:T(8,128)(2,1)} %param.12) | copy-start | bytes 6291460
  11.3 6.3 %collective-permute-start.10 = (f32[512,256]{1,0:T(8,128)S(1)}, f32[512,256]{1,0:T(8,128)S(1)}, u32[]{:S(2)}, u32[]{:S(2)}) collective-permute-start(f32[512,256]{1,0:T(8,128)S(1)} %get-tuple-element.79), channel_id=1, source_target_pairs={{0,1},{1,0},{2,3},{3,2},{4,5},{5,4},{6,7},{7,6},{8,9},{9,8},{10,11... | collective-permute-start | bytes 1572872 | tf_op jit(solution)/shard_map/ppermute | solution.py:398
  13.1 45.0 %collective-permute-start.8 = (bf16[272,2048]{1,0:T(8,128)(2,1)}, bf16[272,2048]{1,0:T(8,128)(2,1)S(1)}, u32[]{:S(2)}, u32[]{:S(2)}) collective-permute-start(bf16[272,2048]{1,0:T(8,128)(2,1)} %get-tuple-element.76), channel_id=1, source_target_pairs={{0,4},{4,8},{8,12},{12,0},{1,5},{5,9},{9,13},{13,1},{2,6},{6,10},{... | collective-permute-start | bytes 3342344 | tf_op jit(solution)/shard_map/ppermute | solution.py:384
  14.4 1.5 %collective-permute-start.12 = (f32[64,512]{1,0:T(8,128)S(1)}, f32[64,512]{1,0:T(8,128)S(1)}, u32[]{:S(2)}, u32[]{:S(2)}) collective-permute-start(f32[64,512]{1,0:T(8,128)S(1)} %low_rank_home.1), channel_id=1, source_target_pairs={{0,1},{1,0},{2,3},{3,2},{4,5},{5,4},{6,7},{7,6},{8,9},{9,8},{10,11... | collective-permute-start | bytes 393224 | tf_op jit(solution)/shard_map/ppermute | solution.py:398
  16.0 6.4 %copy-start.5 = (bf16[8,64,128]{2,1,0:T(8,128)(2,1)S(1)}, bf16[8,64,128]{2,1,0:T(8,128)(2,1)}, u32[]{:S(2)}) copy-start(bf16[8,64,128]{2,1,0:T(8,128)(2,1)} %param.13) | copy-start | bytes 393220
  16.0 6.4 %collective-permute-start.13 = (f32[64,512]{1,0:T(8,128)S(1)}, f32[64,512]{1,0:T(8,128)S(1)}, u32[]{:S(2)}, u32[]{:S(2)}) collective-permute-start(f32[64,512]{1,0:T(8,128)S(1)} %add.26.a_ref), channel_id=1, source_target_pairs={{0,2},{1,3},{2,0},{3,1},{4,6},{5,7},{6,4},{7,5},{8,10},{9,11},{10,... | collective-permute-start | bytes 393224 | tf_op jit(solution)/shard_map/ppermute | solution.py:398
  17.7 9.8 %collective-permute-start.11 = (f32[512,128]{1,0:T(8,128)S(1)}, f32[512,128]{1,0:T(8,128)S(1)}, u32[]{:S(2)}, u32[]{:S(2)}) collective-permute-start(f32[512,128]{1,0:T(8,128)S(1)} %get-tuple-element.96), channel_id=1, source_target_pairs={{0,2},{1,3},{2,0},{3,1},{4,6},{5,7},{6,4},{7,5},{8,10},{9,11},{10,... | collective-permute-start | bytes 786440 | tf_op jit(solution)/shard_map/ppermute | solution.py:398
  35.0 1.4 %collective-permute-start.14 = (f32[64,272]{1,0:T(8,128)S(1)}, f32[64,272]{1,0:T(8,128)S(1)}, u32[]{:S(2)}, u32[]{:S(2)}) collective-permute-start(f32[64,272]{1,0:T(8,128)S(1)} %get-tuple-element.83), channel_id=1, source_target_pairs={{0,1},{1,0},{2,3},{3,2},{4,5},{5,4},{6,7},{7,6},{8,9},{9,8},{10,11... | collective-permute-start | bytes 208904 | tf_op jit(solution)/shard_map/ppermute | solution.py:398
  36.4 4.9 %collective-permute-start.15 = (f32[64,272]{1,0:T(8,128)S(1)}, f32[64,272]{1,0:T(8,128)S(1)}, u32[]{:S(2)}, u32[]{:S(2)}) collective-permute-start(f32[64,272]{1,0:T(8,128)S(1)} %add.27.a_ref), channel_id=1, source_target_pairs={{0,2},{1,3},{2,0},{3,1},{4,6},{5,7},{6,4},{7,5},{8,10},{9,11},{10,... | collective-permute-start | bytes 208904 | tf_op jit(solution)/shard_map/ppermute | solution.py:398
  38.0 44.3 %collective-permute-start.16 = (bf16[144,2048]{1,0:T(8,128)(2,1)S(1)}, bf16[144,2048]{1,0:T(8,128)(2,1)S(1)}, u32[]{:S(2)}, u32[]{:S(2)}) collective-permute-start(bf16[144,2048]{1,0:T(8,128)(2,1)S(1)} %get-tuple-element.87), channel_id=1, source_target_pairs={{0,8},{4,12},{8,0},{12,4},{1,9},{5,13},{9,1},{13,5},{2,10},{6,14},... | collective-permute-start | bytes 1769480 | tf_op jit(solution)/shard_map/ppermute | solution.py:384
  58.2 24.8 %collective-permute-start.17 = (bf16[128,2048]{1,0:T(8,128)(2,1)S(1)}, bf16[128,2048]{1,0:T(8,128)(2,1)S(1)}, u32[]{:S(2)}, u32[]{:S(2)}) collective-permute-start(bf16[128,2048]{1,0:T(8,128)(2,1)S(1)} %slice_select_fusion), channel_id=1, source_target_pairs={{0,4},{4,0},{8,12},{12,8},{1,5},{5,1},{9,13},{13,9},{2,6},{6,2},{1... | collective-permute-start | bytes 1572872 | tf_op jit(solution)/shard_map/ppermute | solution.py:384
  59.8 23.2 %copy-start.3 = (bf16[8,2048,64]{1,2,0:T(8,128)(2,1)S(1)}, bf16[8,2048,64]{1,2,0:T(8,128)(2,1)}, u32[]{:S(2)}) copy-start(bf16[8,2048,64]{1,2,0:T(8,128)(2,1)} %param.12) | copy-start | bytes 6291460
  63.3 1.4 %collective-permute-start.18 = (f32[64,272]{1,0:T(8,128)S(1)}, f32[64,272]{1,0:T(8,128)S(1)}, u32[]{:S(2)}, u32[]{:S(2)}) collective-permute-start(f32[64,272]{1,0:T(8,128)S(1)} %get-tuple-element.89), channel_id=1, source_target_pairs={{0,1},{1,0},{2,3},{3,2},{4,5},{5,4},{6,7},{7,6},{8,9},{9,8},{10,11... | collective-permute-start | bytes 208904 | tf_op jit(solution)/shard_map/ppermute | solution.py:398
  64.6 4.9 %collective-permute-start.19 = (f32[64,272]{1,0:T(8,128)S(1)}, f32[64,272]{1,0:T(8,128)S(1)}, u32[]{:S(2)}, u32[]{:S(2)}) collective-permute-start(f32[64,272]{1,0:T(8,128)S(1)} %add.29.a_ref), channel_id=1, source_target_pairs={{0,2},{1,3},{2,0},{3,1},{4,6},{5,7},{6,4},{7,5},{8,10},{9,11},{10,... | collective-permute-start | bytes 208904 | tf_op jit(solution)/shard_map/ppermute | solution.py:398
  84.7 12.2 %copy-start.6 = (s32[512]{0:T(512)S(1)}, s32[512]{0:T(512)}, u32[]{:S(2)}) copy-start(s32[512]{0:T(512)} %param.9) | copy-start | bytes 6148
  84.7 12.2 %copy-start.7 = (s32[32]{0:T(128)S(1)}, s32[32]{0:T(128)}, u32[]{:S(2)}) copy-start(s32[32]{0:T(128)} %param.10) | copy-start | bytes 388
  84.8 1.4 %collective-permute-start.22 = (f32[64,272]{1,0:T(8,128)S(1)}, f32[64,272]{1,0:T(8,128)S(1)}, u32[]{:S(2)}, u32[]{:S(2)}) collective-permute-start(f32[64,272]{1,0:T(8,128)S(1)} %get-tuple-element.95), channel_id=1, source_target_pairs={{0,1},{1,0},{2,3},{3,2},{4,5},{5,4},{6,7},{7,6},{8,9},{9,8},{10,11... | collective-permute-start | bytes 208904 | tf_op jit(solution)/shard_map/ppermute | solution.py:398
  86.1 5.4 %collective-permute-start.23 = (f32[64,272]{1,0:T(8,128)S(1)}, f32[64,272]{1,0:T(8,128)S(1)}, u32[]{:S(2)}, u32[]{:S(2)}) collective-permute-start(f32[64,272]{1,0:T(8,128)S(1)} %add.30.a_ref), channel_id=1, source_target_pairs={{0,2},{1,3},{2,0},{3,1},{4,6},{5,7},{6,4},{7,5},{8,10},{9,11},{10,... | collective-permute-start | bytes 208904 | tf_op jit(solution)/shard_map/ppermute | solution.py:398
  87.7 7.2 %collective-permute-start.21 = (s16[288,128]{1,0:T(8,128)(2,1)S(1)}, s16[288,128]{1,0:T(8,128)(2,1)S(1)}, u32[]{:S(2)}, u32[]{:S(2)}) collective-permute-start(s16[288,128]{1,0:T(8,128)(2,1)S(1)} %up_coded.5), channel_id=1, source_target_pairs={{0,4},{4,8},{8,12},{12,0},{1,5},{5,9},{9,13},{13,1},{2,6},{6,10},{... | collective-permute-start | bytes 221192 | tf_op jit(solution)/shard_map/ppermute | solution.py:384
  87.7 7.2 %collective-permute-start.20 = (s16[288,128]{1,0:T(8,128)(2,1)S(1)}, s16[288,128]{1,0:T(8,128)(2,1)S(1)}, u32[]{:S(2)}, u32[]{:S(2)}) collective-permute-start(s16[288,128]{1,0:T(8,128)(2,1)S(1)} %up_coded.6), channel_id=1, source_target_pairs={{0,12},{4,0},{8,4},{12,8},{1,13},{5,1},{9,5},{13,9},{2,14},{6,2},{... | collective-permute-start | bytes 221192 | tf_op jit(solution)/shard_map/ppermute | solution.py:384
  92.1 6.5 %collective-permute-start.24 = (s16[288,128]{1,0:T(8,128)(2,1)S(1)}, s16[288,128]{1,0:T(8,128)(2,1)S(1)}, u32[]{:S(2)}, u32[]{:S(2)}) collective-permute-start(s16[288,128]{1,0:T(8,128)(2,1)S(1)} %up_coded.7), channel_id=1, source_target_pairs={{0,8},{4,12},{8,0},{12,4},{1,9},{5,13},{9,1},{13,5},{2,10},{6,14},... | collective-permute-start | bytes 221192 | tf_op jit(solution)/shard_map/ppermute | solution.py:384

commit v6 on v5

--- a/solution.py
+++ b/solution.py
@@ -63,11 +63,10 @@
     return one_hot(iota((tokens, tokens), 0) < iota((tokens, tokens), 1))
 
 
-def routes(index_row, storage_row, holder, owners, group, first):
+def routes(index_row, storage_row, holder, owners, group, first, strict):
     tokens = index_row.shape[1]
     storage = storage_of(index_row, storage_row)
     owner = owner_of(storage, holder, owners)
-    strict = earlier(tokens)
     rows = -(-owners // 8) * 8
     hits = iota((rows, tokens), 0) == owner
     rank = jnp.sum(jnp.where(hits, dot(one_hot(hits), strict), 0.0), axis=0, keepdims=True)
@@ -110,10 +109,11 @@
     ]
     for copy in small + large:
         copy.start()
+    strict = earlier(index.shape[1])
     for copy in small:
         copy.wait()
     me = me_ref[0]
-    owner, row, rank, place = routes(index[...], storage[...], holder, owners, me, first)
+    owner, row, rank, place = routes(index[...], storage[...], holder, owners, me, first, strict)
     home_ids_ref[...] = jnp.where(owner == me, row - me * holder, -1)
     away = owner - me
     away = jnp.where(away < 0, away + owners, away)
@@ -134,7 +134,7 @@
 
 def route_pack(me, index_row, storage_row, tokens, owners, holder, first, late):
     count, features = tokens.shape
-    tiles = 4 if features % 512 == 0 else 1
+    tiles = 2 if features % 512 == 0 else 1
     in_hbm = pl.BlockSpec(memory_space=pltpu.HBM)
     long = first + late + 1
     return pl.pallas_call(

time: 99.9 us -> 99.4 us (level)
  no operation moved by 1% of the time
where the time goes in v6:
time: 99.4 us; the launch traced here: 99.3 us
  waiting for transfers between devices  55.1 us (55%)
  starting transfers between devices  21.1 us (21%)
  Pallas kernels  19.8 us (20%)
  between operations  2.78 us (3%)
    ppermute x7, waiting for transfers between devices, along(): return lax.ppermute(x, 'own', pairs)  36.3 us
    ppermute x10, waiting for transfers between devices, partner(): lax.ppermute(x, 'tp', [(i, i ^ bit) for i in range(lax.axis_size('tp'))])  18.8 us
    ppermute x7, starting transfers between devices, along(): return lax.ppermute(x, 'own', pairs)  13.4 us
    ppermute x10, starting transfers between devices, partner(): lax.ppermute(x, 'tp', [(i, i ^ bit) for i in range(lax.axis_size('tp'))])  7.66 us
    pallas_call x3, Pallas kernels, low_rank(): pl.pallas_call(functools.partial(low_rank_kernel, blocks, joined, holder,...  6.94 us
    pallas_call x1, Pallas kernels, base_blocks(): pl.pallas_call(functools.partial(base_kernel, parts), out_shape=[jax.Shap...  2.97 us
    pallas_call x1, Pallas kernels, route_pack(): pl.pallas_call(functools.partial(route_pack_kernel, owners, holder, first...  2.67 us
    pallas_call x3, Pallas kernels, gather_add(): pl.pallas_call(functools.partial(gather_add_kernel, ranges, len(terms)),...  2.09 us
  transfers between devices with their start and end apart: 17, of which 13 were waited for; matrix products, arithmetic and copies ran while one was open for 0% of the time, Pallas kernels for 14%

profile of v6, /device:TPU:0, one launch (start us, length us, event | category | flops | bytes accessed | tf_op | source)
XLA Modules:
  0.0 99.3 jit_solution(4703495415857904463)
XLA Ops:
  0.0 2.7 %route_pack.1 = (bf16[272,2048]{1,0:T(8,128)(2,1)S(1)}, s32[1,512]{1,0:T(1,128)S(1)}, s32[1,512]{1,0:T(1,128)S(1)}, s32[1]{0:T(128)}) custom-call(s32[1]{0:T(128)} %bitcast.me_ref, s32[1,512]{1,0:T(1,128)} %bitcast.19, s32[1,32]{1,0:T(1,128)} %bitcast.21, bf16[512,2048]{1,0:T(8,128)(2,1)} %tokens_ref.5), custom_call_target="tpu_custom_call" | custom-call | flops 1 | bytes 1 | tf_op jit(solution)/shard_map/route_pack/pallas_call | solution.py:140
  2.7 0.0 copy-start.1
  2.7 5.1 %collective-permute-start.9 = (bf16[272,2048]{1,0:T(8,128)(2,1)S(1)}, bf16[272,2048]{1,0:T(8,128)(2,1)S(1)}, u32[]{:S(2)}, u32[]{:S(2)}) collective-permute-start(bf16[272,2048]{1,0:T(8,128)(2,1)S(1)} %get-tuple-element.75.third_ref), channel_id=1, source_target_pairs={{0,12},{4,0},{8,4},{12,8},{1,13},{5,1},{9,5},{13,9},{2,14},{6,2},{... | collective-permute-start | bytes 3342344 | tf_op jit(solution)/shard_map/ppermute | solution.py:384
  7.8 3.0 %base_blocks.1 = (f32[512,256]{1,0:T(8,128)S(1)}, f32[512,256]{1,0:T(8,128)S(1)}) custom-call(s32[1]{0:T(128)} %bitcast.3.me_ref, bf16[512,2048]{1,0:T(8,128)(2,1)} %tokens_ref.5, bf16[2048,512]{1,0:T(8,128)(2,1)S(1)} %copy-done), custom_call_target="tpu_custom_call" | custom-call | flops 1 | bytes 1 | tf_op jit(solution)/shard_map/base_blocks/pallas_call | solution.py:337
  10.8 0.0 copy-start.2
  10.8 0.1 collective-permute-start.10
  10.9 1.8 %pack_more.1 = (bf16[272,2048]{1,0:T(8,128)(2,1)}, bf16[144,2048]{1,0:T(8,128)(2,1)S(1)}) custom-call(s32[1,512]{1,0:T(1,128)S(1)} %get-tuple-element.73.dest_ref, bf16[512,2048]{1,0:T(8,128)(2,1)S(1)} %copy-done.1, bf16[272,2048]{1,0:T(8,128)(2,1)S(1)} %get-tuple-element.75.third_ref), custom_call_target="tpu_custom_call" | custom-call | flops 1 | bytes 1 | tf_op jit(solution)/shard_map/pack_more/pallas_call | solution.py:170
  12.6 1.3 %low_rank_home.1 = f32[64,512]{1,0:T(8,128)S(1)} custom-call(s32[1,512]{1,0:T(1,128)S(1)} %get-tuple-element.80.ids_ref, bf16[512,2048]{1,0:T(8,128)(2,1)S(1)} %bitcast.10, bf16[512,2048]{1,0:T(8,128)(2,1)S(1)} %copy-done.1), custom_call_target="tpu_custom_call" | custom-call | flops 1 | bytes 1 | tf_op jit(solution)/shard_map/low_rank_home/pallas_call | solution.py:254
  13.9 0.5 collective-permute-start.12
  14.5 1.0 collective-permute-done.12
  15.5 0.0 copy-start.5
  15.5 1.6 %collective-permute-start.13 = (f32[64,512]{1,0:T(8,128)S(1)}, f32[64,512]{1,0:T(8,128)S(1)}, u32[]{:S(2)}, u32[]{:S(2)}) collective-permute-start(f32[64,512]{1,0:T(8,128)S(1)} %add.26.a_ref), channel_id=1, source_target_pairs={{0,2},{1,3},{2,0},{3,1},{4,6},{5,7},{6,4},{7,5},{8,10},{9,11},{10,... | collective-permute-start | bytes 393224 | tf_op jit(solution)/shard_map/ppermute | solution.py:398
  17.1 0.1 add.25
  17.2 0.6 collective-permute-start.11
  17.8 4.1 %collective-permute-done.13.b_ref = f32[64,512]{1,0:T(8,128)S(1)} collective-permute-done((f32[64,512]{1,0:T(8,128)S(1)}, f32[64,512]{1,0:T(8,128)S(1)}, u32[]{:S(2)}, u32[]{:S(2)}) %collective-permute-start.13) | collective-permute-done | bytes 131104 | tf_op jit(solution)/shard_map/ppermute | solution.py:398
  21.9 0.5 up_project.1
  22.4 4.5 %collective-permute-done.11.refs_1_ = f32[512,128]{1,0:T(8,128)S(1)} collective-permute-done((f32[512,128]{1,0:T(8,128)S(1)}, f32[512,128]{1,0:T(8,128)S(1)}, u32[]{:S(2)}, u32[]{:S(2)}) %collective-permute-start.11) | collective-permute-done | bytes 262176 | tf_op jit(solution)/shard_map/ppermute | solution.py:398
  27.0 5.8 %collective-permute-done.9.refs_0_ = bf16[272,2048]{1,0:T(8,128)(2,1)S(1)} collective-permute-done((bf16[272,2048]{1,0:T(8,128)(2,1)S(1)}, bf16[272,2048]{1,0:T(8,128)(2,1)S(1)}, u32[]{:S(2)}, u32[]{:S(2)}) %collective-permute-start.9) | collective-permute-done | bytes 1114144 | tf_op jit(solution)/shard_map/ppermute | solution.py:384
  32.8 1.7 %low_rank.5 = (f32[64,272]{1,0:T(8,128)S(1)}, s32[1,272]{1,0:T(1,128)S(1)}, s32[1]{0:T(128)}) custom-call(s32[1]{0:T(128)} %bitcast.me_ref, bf16[512,2048]{1,0:T(8,128)(2,1)S(1)} %bitcast.11, bf16[272,2048]{1,0:T(8,128)(2,1)S(1)} %collective-permute-done.9.refs_0_), custom_call_target="tpu_custom_call" | custom-call | flops 1 | bytes 1 | tf_op jit(solution)/shard_map/low_rank/pallas_call | solution.py:228
  34.5 0.1 collective-permute-start.14
  34.6 1.3 %collective-permute-done.14 = f32[64,272]{1,0:T(8,128)S(1)} collective-permute-done((f32[64,272]{1,0:T(8,128)S(1)}, f32[64,272]{1,0:T(8,128)S(1)}, u32[]{:S(2)}, u32[]{:S(2)}) %collective-permute-start.14) | collective-permute-done | bytes 69664 | tf_op jit(solution)/shard_map/ppermute | solution.py:398
  35.9 1.6 %collective-permute-start.15 = (f32[64,272]{1,0:T(8,128)S(1)}, f32[64,272]{1,0:T(8,128)S(1)}, u32[]{:S(2)}, u32[]{:S(2)}) collective-permute-start(f32[64,272]{1,0:T(8,128)S(1)} %add.27.a_ref), channel_id=1, source_target_pairs={{0,2},{1,3},{2,0},{3,1},{4,6},{5,7},{6,4},{7,5},{8,10},{9,11},{10,... | collective-permute-start | bytes 208904 | tf_op jit(solution)/shard_map/ppermute | solution.py:398
  37.5 1.4 %collective-permute-start.16 = (bf16[144,2048]{1,0:T(8,128)(2,1)S(1)}, bf16[144,2048]{1,0:T(8,128)(2,1)S(1)}, u32[]{:S(2)}, u32[]{:S(2)}) collective-permute-start(bf16[144,2048]{1,0:T(8,128)(2,1)S(1)} %get-tuple-element.87), channel_id=1, source_target_pairs={{0,8},{4,12},{8,0},{12,4},{1,9},{5,13},{9,1},{13,5},{2,10},{6,14},... | collective-permute-start | bytes 1769480 | tf_op jit(solution)/shard_map/ppermute | solution.py:384
  38.9 1.9 %collective-permute-done.15.b_ref = f32[64,272]{1,0:T(8,128)S(1)} collective-permute-done((f32[64,272]{1,0:T(8,128)S(1)}, f32[64,272]{1,0:T(8,128)S(1)}, u32[]{:S(2)}, u32[]{:S(2)}) %collective-permute-start.15) | collective-permute-done | bytes 69664 | tf_op jit(solution)/shard_map/ppermute | solution.py:398
  40.8 0.5 up_coded.5
  41.4 16.3 %collective-permute-done.8.refs_0_ = bf16[272,2048]{1,0:T(8,128)(2,1)S(1)} collective-permute-done((bf16[272,2048]{1,0:T(8,128)(2,1)}, bf16[272,2048]{1,0:T(8,128)(2,1)S(1)}, u32[]{:S(2)}, u32[]{:S(2)}) %collective-permute-start.8) | collective-permute-done | bytes 1114144 | tf_op jit(solution)/shard_map/ppermute | solution.py:384
  57.6 0.1 slice_select_fusion
  57.7 1.6 %collective-permute-start.17 = (bf16[128,2048]{1,0:T(8,128)(2,1)S(1)}, bf16[128,2048]{1,0:T(8,128)(2,1)S(1)}, u32[]{:S(2)}, u32[]{:S(2)}) collective-permute-start(bf16[128,2048]{1,0:T(8,128)(2,1)S(1)} %slice_select_fusion), channel_id=1, source_target_pairs={{0,4},{4,0},{8,12},{12,8},{1,5},{5,1},{9,13},{13,9},{2,6},{6,2},{1... | collective-permute-start | bytes 1572872 | tf_op jit(solution)/shard_map/ppermute | solution.py:384
  59.3 3.5 %low_rank.6 = (f32[64,272]{1,0:T(8,128)S(1)}, s32[1,272]{1,0:T(1,128)S(1)}, s32[1]{0:T(128)}) custom-call(s32[1]{0:T(128)} %bitcast.me_ref, bf16[512,2048]{1,0:T(8,128)(2,1)} %bitcast.9, bf16[272,2048]{1,0:T(8,128)(2,1)S(1)} %collective-permute-done.8.refs_0_), custom_call_target="tpu_custom_call" | custom-call | flops 1 | bytes 1 | tf_op jit(solution)/shard_map/low_rank/pallas_call | solution.py:228
  62.8 0.1 collective-permute-start.18
  62.8 1.3 %collective-permute-done.18 = f32[64,272]{1,0:T(8,128)S(1)} collective-permute-done((f32[64,272]{1,0:T(8,128)S(1)}, f32[64,272]{1,0:T(8,128)S(1)}, u32[]{:S(2)}, u32[]{:S(2)}) %collective-permute-start.18) | collective-permute-done | bytes 69664 | tf_op jit(solution)/shard_map/ppermute | solution.py:398
  64.1 1.6 %collective-permute-start.19 = (f32[64,272]{1,0:T(8,128)S(1)}, f32[64,272]{1,0:T(8,128)S(1)}, u32[]{:S(2)}, u32[]{:S(2)}) collective-permute-start(f32[64,272]{1,0:T(8,128)S(1)} %add.29.a_ref), channel_id=1, source_target_pairs={{0,2},{1,3},{2,0},{3,1},{4,6},{5,7},{6,4},{7,5},{8,10},{9,11},{10,... | collective-permute-start | bytes 208904 | tf_op jit(solution)/shard_map/ppermute | solution.py:398
  65.7 3.4 %collective-permute-done.19.b_ref = f32[64,272]{1,0:T(8,128)S(1)} collective-permute-done((f32[64,272]{1,0:T(8,128)S(1)}, f32[64,272]{1,0:T(8,128)S(1)}, u32[]{:S(2)}, u32[]{:S(2)}) %collective-permute-start.19) | collective-permute-done | bytes 69664 | tf_op jit(solution)/shard_map/ppermute | solution.py:398
  69.1 0.5 up_coded.6
  69.6 12.2 %collective-permute-done.16.refs_0_ = bf16[144,2048]{1,0:T(8,128)(2,1)S(1)} collective-permute-done((bf16[144,2048]{1,0:T(8,128)(2,1)S(1)}, bf16[144,2048]{1,0:T(8,128)(2,1)S(1)}, u32[]{:S(2)}, u32[]{:S(2)}) %collective-permute-start.16) | collective-permute-done | bytes 589856 | tf_op jit(solution)/shard_map/ppermute | solution.py:384
  81.8 0.7 collective-permute-done.17.refs_1_
  82.5 1.8 %low_rank.7 = (f32[64,272]{1,0:T(8,128)S(1)}, s32[1,272]{1,0:T(1,128)S(1)}, s32[1]{0:T(128)}) custom-call(s32[1]{0:T(128)} %bitcast.me_ref, bf16[512,2048]{1,0:T(8,128)(2,1)S(1)} %bitcast.12, bf16[144,2048]{1,0:T(8,128)(2,1)S(1)} %collective-permute-done.16.refs_0_, bf16[128,2048]{1,0:T(8,128)(2,1)S(1)} %collective-permute-done.17.refs_1_), custom_call_target="tpu_custom_call" | custom-call | flops 1 | bytes 1 | tf_op jit(solution)/shard_map/low_rank/pallas_call | solution.py:228
  84.2 0.0 copy-start.6
  84.3 0.1 collective-permute-start.22
  84.3 1.3 %collective-permute-done.22 = f32[64,272]{1,0:T(8,128)S(1)} collective-permute-done((f32[64,272]{1,0:T(8,128)S(1)}, f32[64,272]{1,0:T(8,128)S(1)}, u32[]{:S(2)}, u32[]{:S(2)}) %collective-permute-start.22) | collective-permute-done | bytes 69664 | tf_op jit(solution)/shard_map/ppermute | solution.py:398
  85.6 1.6 %collective-permute-start.23 = (f32[64,272]{1,0:T(8,128)S(1)}, f32[64,272]{1,0:T(8,128)S(1)}, u32[]{:S(2)}, u32[]{:S(2)}) collective-permute-start(f32[64,272]{1,0:T(8,128)S(1)} %add.30.a_ref), channel_id=1, source_target_pairs={{0,2},{1,3},{2,0},{3,1},{4,6},{5,7},{6,4},{7,5},{8,10},{9,11},{10,... | collective-permute-start | bytes 208904 | tf_op jit(solution)/shard_map/ppermute | solution.py:398
  87.2 3.8 %collective-permute-start.20 = (s16[288,128]{1,0:T(8,128)(2,1)S(1)}, s16[288,128]{1,0:T(8,128)(2,1)S(1)}, u32[]{:S(2)}, u32[]{:S(2)}) collective-permute-start(s16[288,128]{1,0:T(8,128)(2,1)S(1)} %up_coded.6), channel_id=1, source_target_pairs={{0,12},{4,0},{8,4},{12,8},{1,13},{5,1},{9,5},{13,9},{2,14},{6,2},{... | collective-permute-start | bytes 221192 | tf_op jit(solution)/shard_map/ppermute | solution.py:384
  91.0 0.5 up_coded.7
  91.6 1.5 %collective-permute-start.24 = (s16[288,128]{1,0:T(8,128)(2,1)S(1)}, s16[288,128]{1,0:T(8,128)(2,1)S(1)}, u32[]{:S(2)}, u32[]{:S(2)}) collective-permute-start(s16[288,128]{1,0:T(8,128)(2,1)S(1)} %up_coded.7), channel_id=1, source_target_pairs={{0,8},{4,12},{8,0},{12,4},{1,9},{5,13},{9,1},{13,5},{2,10},{6,14},... | collective-permute-start | bytes 221192 | tf_op jit(solution)/shard_map/ppermute | solution.py:384
  94.4 0.8 gather_add.6
  96.4 0.2 conditional.1
  96.7 1.4 %collective-permute-done.24.refs_1_ = s16[288,128]{1,0:T(8,128)(2,1)S(1)} collective-permute-done((s16[288,128]{1,0:T(8,128)(2,1)S(1)}, s16[288,128]{1,0:T(8,128)(2,1)S(1)}, u32[]{:S(2)}, u32[]{:S(2)}) %collective-permute-start.24) | collective-permute-done | bytes 73760 | tf_op jit(solution)/shard_map/ppermute | solution.py:384
  98.0 1.2 %gather_add.7 = bf16[512,128]{1,0:T(8,128)(2,1)} custom-call(s32[1,512]{1,0:T(1,128)S(1)} %get-tuple-element.73.dest_ref, f32[512,128]{1,0:T(8,128)S(1)} %get-tuple-element.98.refs_0_, s16[288,128]{1,0:T(8,128)(2,1)S(1)} %collective-permute-done.24.refs_1_), custom_call_target="tpu_custom_call" | custom-call | flops 1 | bytes 1 | tf_op jit(solution)/shard_map/gather_add/pallas_call | solution.py:372
  (23 shorter events, 0.2 us)
Async XLA Ops:
  0.0 7.8 %copy-start = (bf16[2048,512]{1,0:T(8,128)(2,1)S(1)}, bf16[2048,512]{1,0:T(8,128)(2,1)}, u32[]{:S(2)}) copy-start(bf16[2048,512]{1,0:T(8,128)(2,1)} %value_ref.1) | copy-start | bytes 6291460
  2.7 8.2 %copy-start.1 = (bf16[512,2048]{1,0:T(8,128)(2,1)S(1)}, bf16[512,2048]{1,0:T(8,128)(2,1)}, u32[]{:S(2)}) copy-start(bf16[512,2048]{1,0:T(8,128)(2,1)} %tokens_ref.5) | copy-start | bytes 6291460
  2.7 30.1 %collective-permute-start.9 = (bf16[272,2048]{1,0:T(8,128)(2,1)S(1)}, bf16[272,2048]{1,0:T(8,128)(2,1)S(1)}, u32[]{:S(2)}, u32[]{:S(2)}) collective-permute-start(bf16[272,2048]{1,0:T(8,128)(2,1)S(1)} %get-tuple-element.75.third_ref), channel_id=1, source_target_pairs={{0,12},{4,0},{8,4},{12,8},{1,13},{5,1},{9,5},{13,9},{2,14},{6,2},{... | collective-permute-start | bytes 3342344 | tf_op jit(solution)/shard_map/ppermute | solution.py:384
  10.8 1.9 %copy-start.2 = (bf16[8,2048,64]{1,2,0:T(8,128)(2,1)S(1)}, bf16[8,2048,64]{1,2,0:T(8,128)(2,1)}, u32[]{:S(2)}) copy-start(bf16[8,2048,64]{1,2,0:T(8,128)(2,1)} %param.12) | copy-start | bytes 6291460
  10.8 6.3 %collective-permute-start.10 = (f32[512,256]{1,0:T(8,128)S(1)}, f32[512,256]{1,0:T(8,128)S(1)}, u32[]{:S(2)}, u32[]{:S(2)}) collective-permute-start(f32[512,256]{1,0:T(8,128)S(1)} %get-tuple-element.79), channel_id=1, source_target_pairs={{0,1},{1,0},{2,3},{3,2},{4,5},{5,4},{6,7},{7,6},{8,9},{9,8},{10,11... | collective-permute-start | bytes 1572872 | tf_op jit(solution)/shard_map/ppermute | solution.py:398
  12.6 45.0 %collective-permute-start.8 = (bf16[272,2048]{1,0:T(8,128)(2,1)}, bf16[272,2048]{1,0:T(8,128)(2,1)S(1)}, u32[]{:S(2)}, u32[]{:S(2)}) collective-permute-start(bf16[272,2048]{1,0:T(8,128)(2,1)} %get-tuple-element.76), channel_id=1, source_target_pairs={{0,4},{4,8},{8,12},{12,0},{1,5},{5,9},{9,13},{13,1},{2,6},{6,10},{... | collective-permute-start | bytes 3342344 | tf_op jit(solution)/shard_map/ppermute | solution.py:384
  13.9 1.5 %collective-permute-start.12 = (f32[64,512]{1,0:T(8,128)S(1)}, f32[64,512]{1,0:T(8,128)S(1)}, u32[]{:S(2)}, u32[]{:S(2)}) collective-permute-start(f32[64,512]{1,0:T(8,128)S(1)} %low_rank_home.1), channel_id=1, source_target_pairs={{0,1},{1,0},{2,3},{3,2},{4,5},{5,4},{6,7},{7,6},{8,9},{9,8},{10,11... | collective-permute-start | bytes 393224 | tf_op jit(solution)/shard_map/ppermute | solution.py:398
  15.5 6.4 %copy-start.5 = (bf16[8,64,128]{2,1,0:T(8,128)(2,1)S(1)}, bf16[8,64,128]{2,1,0:T(8,128)(2,1)}, u32[]{:S(2)}) copy-start(bf16[8,64,128]{2,1,0:T(8,128)(2,1)} %param.13) | copy-start | bytes 393220
  15.5 6.4 %collective-permute-start.13 = (f32[64,512]{1,0:T(8,128)S(1)}, f32[64,512]{1,0:T(8,128)S(1)}, u32[]{:S(2)}, u32[]{:S(2)}) collective-permute-start(f32[64,512]{1,0:T(8,128)S(1)} %add.26.a_ref), channel_id=1, source_target_pairs={{0,2},{1,3},{2,0},{3,1},{4,6},{5,7},{6,4},{7,5},{8,10},{9,11},{10,... | collective-permute-start | bytes 393224 | tf_op jit(solution)/shard_map/ppermute | solution.py:398
  17.2 9.8 %collective-permute-start.11 = (f32[512,128]{1,0:T(8,128)S(1)}, f32[512,128]{1,0:T(8,128)S(1)}, u32[]{:S(2)}, u32[]{:S(2)}) collective-permute-start(f32[512,128]{1,0:T(8,128)S(1)} %get-tuple-element.96), channel_id=1, source_target_pairs={{0,2},{1,3},{2,0},{3,1},{4,6},{5,7},{6,4},{7,5},{8,10},{9,11},{10,... | collective-permute-start | bytes 786440 | tf_op jit(solution)/shard_map/ppermute | solution.py:398
  34.5 1.4 %collective-permute-start.14 = (f32[64,272]{1,0:T(8,128)S(1)}, f32[64,272]{1,0:T(8,128)S(1)}, u32[]{:S(2)}, u32[]{:S(2)}) collective-permute-start(f32[64,272]{1,0:T(8,128)S(1)} %get-tuple-element.83), channel_id=1, source_target_pairs={{0,1},{1,0},{2,3},{3,2},{4,5},{5,4},{6,7},{7,6},{8,9},{9,8},{10,11... | collective-permute-start | bytes 208904 | tf_op jit(solution)/shard_map/ppermute | solution.py:398
  35.9 4.9 %collective-permute-start.15 = (f32[64,272]{1,0:T(8,128)S(1)}, f32[64,272]{1,0:T(8,128)S(1)}, u32[]{:S(2)}, u32[]{:S(2)}) collective-permute-start(f32[64,272]{1,0:T(8,128)S(1)} %add.27.a_ref), channel_id=1, source_target_pairs={{0,2},{1,3},{2,0},{3,1},{4,6},{5,7},{6,4},{7,5},{8,10},{9,11},{10,... | collective-permute-start | bytes 208904 | tf_op jit(solution)/shard_map/ppermute | solution.py:398
  37.5 44.3 %collective-permute-start.16 = (bf16[144,2048]{1,0:T(8,128)(2,1)S(1)}, bf16[144,2048]{1,0:T(8,128)(2,1)S(1)}, u32[]{:S(2)}, u32[]{:S(2)}) collective-permute-start(bf16[144,2048]{1,0:T(8,128)(2,1)S(1)} %get-tuple-element.87), channel_id=1, source_target_pairs={{0,8},{4,12},{8,0},{12,4},{1,9},{5,13},{9,1},{13,5},{2,10},{6,14},... | collective-permute-start | bytes 1769480 | tf_op jit(solution)/shard_map/ppermute | solution.py:384
  57.7 24.8 %collective-permute-start.17 = (bf16[128,2048]{1,0:T(8,128)(2,1)S(1)}, bf16[128,2048]{1,0:T(8,128)(2,1)S(1)}, u32[]{:S(2)}, u32[]{:S(2)}) collective-permute-start(bf16[128,2048]{1,0:T(8,128)(2,1)S(1)} %slice_select_fusion), channel_id=1, source_target_pairs={{0,4},{4,0},{8,12},{12,8},{1,5},{5,1},{9,13},{13,9},{2,6},{6,2},{1... | collective-permute-start | bytes 1572872 | tf_op jit(solution)/shard_map/ppermute | solution.py:384
  59.3 23.2 %copy-start.3 = (bf16[8,2048,64]{1,2,0:T(8,128)(2,1)S(1)}, bf16[8,2048,64]{1,2,0:T(8,128)(2,1)}, u32[]{:S(2)}) copy-start(bf16[8,2048,64]{1,2,0:T(8,128)(2,1)} %param.12) | copy-start | bytes 6291460
  62.8 1.4 %collective-permute-start.18 = (f32[64,272]{1,0:T(8,128)S(1)}, f32[64,272]{1,0:T(8,128)S(1)}, u32[]{:S(2)}, u32[]{:S(2)}) collective-permute-start(f32[64,272]{1,0:T(8,128)S(1)} %get-tuple-element.89), channel_id=1, source_target_pairs={{0,1},{1,0},{2,3},{3,2},{4,5},{5,4},{6,7},{7,6},{8,9},{9,8},{10,11... | collective-permute-start | bytes 208904 | tf_op jit(solution)/shard_map/ppermute | solution.py:398
  64.1 4.9 %collective-permute-start.19 = (f32[64,272]{1,0:T(8,128)S(1)}, f32[64,272]{1,0:T(8,128)S(1)}, u32[]{:S(2)}, u32[]{:S(2)}) collective-permute-start(f32[64,272]{1,0:T(8,128)S(1)} %add.29.a_ref), channel_id=1, source_target_pairs={{0,2},{1,3},{2,0},{3,1},{4,6},{5,7},{6,4},{7,5},{8,10},{9,11},{10,... | collective-permute-start | bytes 208904 | tf_op jit(solution)/shard_map/ppermute | solution.py:398
  84.2 12.2 %copy-start.6 = (s32[512]{0:T(512)S(1)}, s32[512]{0:T(512)}, u32[]{:S(2)}) copy-start(s32[512]{0:T(512)} %param.9) | copy-start | bytes 6148
  84.2 12.2 %copy-start.7 = (s32[32]{0:T(128)S(1)}, s32[32]{0:T(128)}, u32[]{:S(2)}) copy-start(s32[32]{0:T(128)} %param.10) | copy-start | bytes 388
  84.3 1.4 %collective-permute-start.22 = (f32[64,272]{1,0:T(8,128)S(1)}, f32[64,272]{1,0:T(8,128)S(1)}, u32[]{:S(2)}, u32[]{:S(2)}) collective-permute-start(f32[64,272]{1,0:T(8,128)S(1)} %get-tuple-element.95), channel_id=1, source_target_pairs={{0,1},{1,0},{2,3},{3,2},{4,5},{5,4},{6,7},{7,6},{8,9},{9,8},{10,11... | collective-permute-start | bytes 208904 | tf_op jit(solution)/shard_map/ppermute | solution.py:398
  85.6 5.4 %collective-permute-start.23 = (f32[64,272]{1,0:T(8,128)S(1)}, f32[64,272]{1,0:T(8,128)S(1)}, u32[]{:S(2)}, u32[]{:S(2)}) collective-permute-start(f32[64,272]{1,0:T(8,128)S(1)} %add.30.a_ref), channel_id=1, source_target_pairs={{0,2},{1,3},{2,0},{3,1},{4,6},{5,7},{6,4},{7,5},{8,10},{9,11},{10,... | collective-permute-start | bytes 208904 | tf_op jit(solution)/shard_map/ppermute | solution.py:398
  87.2 7.2 %collective-permute-start.21 = (s16[288,128]{1,0:T(8,128)(2,1)S(1)}, s16[288,128]{1,0:T(8,128)(2,1)S(1)}, u32[]{:S(2)}, u32[]{:S(2)}) collective-permute-start(s16[288,128]{1,0:T(8,128)(2,1)S(1)} %up_coded.5), channel_id=1, source_target_pairs={{0,4},{4,8},{8,12},{12,0},{1,5},{5,9},{9,13},{13,1},{2,6},{6,10},{... | collective-permute-start | bytes 221192 | tf_op jit(solution)/shard_map/ppermute | solution.py:384
  87.2 7.2 %collective-permute-start.20 = (s16[288,128]{1,0:T(8,128)(2,1)S(1)}, s16[288,128]{1,0:T(8,128)(2,1)S(1)}, u32[]{:S(2)}, u32[]{:S(2)}) collective-permute-start(s16[288,128]{1,0:T(8,128)(2,1)S(1)} %up_coded.6), channel_id=1, source_target_pairs={{0,12},{4,0},{8,4},{12,8},{1,13},{5,1},{9,5},{13,9},{2,14},{6,2},{... | collective-permute-start | bytes 221192 | tf_op jit(solution)/shard_map/ppermute | solution.py:384
  91.6 6.5 %collective-permute-start.24 = (s16[288,128]{1,0:T(8,128)(2,1)S(1)}, s16[288,128]{1,0:T(8,128)(2,1)S(1)}, u32[]{:S(2)}, u32[]{:S(2)}) collective-permute-start(s16[288,128]{1,0:T(8,128)(2,1)S(1)} %up_coded.7), channel_id=1, source_target_pairs={{0,8},{4,12},{8,0},{12,4},{1,9},{5,13},{9,1},{13,5},{2,10},{6,14},... | collective-permute-start | bytes 221192 | tf_op jit(solution)/shard_map/ppermute | solution.py:384

commit v7 on v6

--- a/solution.py
+++ b/solution.py
@@ -134,7 +134,7 @@
 
 def route_pack(me, index_row, storage_row, tokens, owners, holder, first, late):
     count, features = tokens.shape
-    tiles = 2 if features % 512 == 0 else 1
+    tiles = 1
     in_hbm = pl.BlockSpec(memory_space=pltpu.HBM)
     long = first + late + 1
     return pl.pallas_call(
@@ -476,7 +476,7 @@
         back = [shifted(x, -s) for s, x in zip(shifts, done)]
         return gather_add(dest, [(late_start + late, late + 1, 0)] * len(back), [total], back, F32)
 
-    across, far, near = lax.optimization_barrier((across, far, near))
+    across, far, below_done = lax.optimization_barrier((across, far, below_done))
     joined = [
         (first, [(0, 0)], [1], part, flag_at, 0),
         (late + 1, [(1, 0)], [1], part, flag_at, first),

time: 99.4 us -> 99.3 us (level)
  no operation moved by 1% of the time
where the time goes in v7:
time: 99.3 us; the launch traced here: 99.1 us
  waiting for transfers between devices  55.1 us (55%)
  starting transfers between devices  21.1 us (21%)
  Pallas kernels  19.6 us (20%)
  between operations  2.78 us (3%)
    ppermute x7, waiting for transfers between devices, along(): return lax.ppermute(x, 'own', pairs)  36.3 us
    ppermute x10, waiting for transfers between devices, partner(): lax.ppermute(x, 'tp', [(i, i ^ bit) for i in range(lax.axis_size('tp'))])  18.8 us
    ppermute x7, starting transfers between devices, along(): return lax.ppermute(x, 'own', pairs)  13.4 us
    ppermute x10, starting transfers between devices, partner(): lax.ppermute(x, 'tp', [(i, i ^ bit) for i in range(lax.axis_size('tp'))])  7.69 us
    pallas_call x3, Pallas kernels, low_rank(): pl.pallas_call(functools.partial(low_rank_kernel, blocks, joined, holder,...  6.94 us
    pallas_call x1, Pallas kernels, base_blocks(): pl.pallas_call(functools.partial(base_kernel, parts), out_shape=[jax.Shap...  2.97 us
    pallas_call x1, Pallas kernels, route_pack(): pl.pallas_call(functools.partial(route_pack_kernel, owners, holder, first...  2.55 us
    pallas_call x3, Pallas kernels, gather_add(): pl.pallas_call(functools.partial(gather_add_kernel, ranges, len(terms)),...  2.08 us
  transfers between devices with their start and end apart: 17, of which 13 were waited for; matrix products, arithmetic and copies ran while one was open for 0% of the time, Pallas kernels for 14%

profile of v7, /device:TPU:0, one launch (start us, length us, event | category | flops | bytes accessed | tf_op | source)
XLA Modules:
  0.0 99.1 jit_solution(4471312969852718426)
XLA Ops:
  0.0 2.6 %route_pack.1 = (bf16[272,2048]{1,0:T(8,128)(2,1)S(1)}, s32[1,512]{1,0:T(1,128)S(1)}, s32[1,512]{1,0:T(1,128)S(1)}, s32[1]{0:T(128)}) custom-call(s32[1]{0:T(128)} %bitcast.me_ref, s32[1,512]{1,0:T(1,128)} %bitcast.19, s32[1,32]{1,0:T(1,128)} %bitcast.21, bf16[512,2048]{1,0:T(8,128)(2,1)} %tokens_ref.5), custom_call_target="tpu_custom_call" | custom-call | flops 1 | bytes 1 | tf_op jit(solution)/shard_map/route_pack/pallas_call | solution.py:140
  2.6 0.0 copy-start.1
  2.6 5.1 %collective-permute-start.9 = (bf16[272,2048]{1,0:T(8,128)(2,1)S(1)}, bf16[272,2048]{1,0:T(8,128)(2,1)S(1)}, u32[]{:S(2)}, u32[]{:S(2)}) collective-permute-start(bf16[272,2048]{1,0:T(8,128)(2,1)S(1)} %get-tuple-element.75.third_ref), channel_id=1, source_target_pairs={{0,12},{4,0},{8,4},{12,8},{1,13},{5,1},{9,5},{13,9},{2,14},{6,2},{... | collective-permute-start | bytes 3342344 | tf_op jit(solution)/shard_map/ppermute | solution.py:384
  7.7 3.0 %base_blocks.1 = (f32[512,256]{1,0:T(8,128)S(1)}, f32[512,256]{1,0:T(8,128)S(1)}) custom-call(s32[1]{0:T(128)} %bitcast.3.me_ref, bf16[512,2048]{1,0:T(8,128)(2,1)} %tokens_ref.5, bf16[2048,512]{1,0:T(8,128)(2,1)S(1)} %copy-done), custom_call_target="tpu_custom_call" | custom-call | flops 1 | bytes 1 | tf_op jit(solution)/shard_map/base_blocks/pallas_call | solution.py:337
  10.7 0.0 copy-start.2
  10.7 0.1 collective-permute-start.10
  10.8 1.8 %pack_more.1 = (bf16[272,2048]{1,0:T(8,128)(2,1)}, bf16[144,2048]{1,0:T(8,128)(2,1)S(1)}) custom-call(s32[1,512]{1,0:T(1,128)S(1)} %get-tuple-element.73.dest_ref, bf16[512,2048]{1,0:T(8,128)(2,1)S(1)} %copy-done.1, bf16[272,2048]{1,0:T(8,128)(2,1)S(1)} %get-tuple-element.75.third_ref), custom_call_target="tpu_custom_call" | custom-call | flops 1 | bytes 1 | tf_op jit(solution)/shard_map/pack_more/pallas_call | solution.py:170
  12.5 1.3 %low_rank_home.1 = f32[64,512]{1,0:T(8,128)S(1)} custom-call(s32[1,512]{1,0:T(1,128)S(1)} %get-tuple-element.80.ids_ref, bf16[512,2048]{1,0:T(8,128)(2,1)S(1)} %bitcast.10, bf16[512,2048]{1,0:T(8,128)(2,1)S(1)} %copy-done.1), custom_call_target="tpu_custom_call" | custom-call | flops 1 | bytes 1 | tf_op jit(solution)/shard_map/low_rank_home/pallas_call | solution.py:254
  13.8 0.6 collective-permute-start.12
  14.4 1.0 collective-permute-done.12
  15.4 0.0 copy-start.5
  15.4 1.6 %collective-permute-start.13 = (f32[64,512]{1,0:T(8,128)S(1)}, f32[64,512]{1,0:T(8,128)S(1)}, u32[]{:S(2)}, u32[]{:S(2)}) collective-permute-start(f32[64,512]{1,0:T(8,128)S(1)} %add.26.a_ref), channel_id=1, source_target_pairs={{0,2},{1,3},{2,0},{3,1},{4,6},{5,7},{6,4},{7,5},{8,10},{9,11},{10,... | collective-permute-start | bytes 393224 | tf_op jit(solution)/shard_map/ppermute | solution.py:398
  17.0 0.1 add.25
  17.1 0.6 collective-permute-start.11
  17.7 4.1 %collective-permute-done.13.b_ref = f32[64,512]{1,0:T(8,128)S(1)} collective-permute-done((f32[64,512]{1,0:T(8,128)S(1)}, f32[64,512]{1,0:T(8,128)S(1)}, u32[]{:S(2)}, u32[]{:S(2)}) %collective-permute-start.13) | collective-permute-done | bytes 131104 | tf_op jit(solution)/shard_map/ppermute | solution.py:398
  21.8 0.5 up_project.1
  22.3 4.5 %collective-permute-done.11.refs_1_ = f32[512,128]{1,0:T(8,128)S(1)} collective-permute-done((f32[512,128]{1,0:T(8,128)S(1)}, f32[512,128]{1,0:T(8,128)S(1)}, u32[]{:S(2)}, u32[]{:S(2)}) %collective-permute-start.11) | collective-permute-done | bytes 262176 | tf_op jit(solution)/shard_map/ppermute | solution.py:398
  26.9 5.8 %collective-permute-done.9.refs_0_ = bf16[272,2048]{1,0:T(8,128)(2,1)S(1)} collective-permute-done((bf16[272,2048]{1,0:T(8,128)(2,1)S(1)}, bf16[272,2048]{1,0:T(8,128)(2,1)S(1)}, u32[]{:S(2)}, u32[]{:S(2)}) %collective-permute-start.9) | collective-permute-done | bytes 1114144 | tf_op jit(solution)/shard_map/ppermute | solution.py:384
  32.7 1.7 %low_rank.5 = (f32[64,272]{1,0:T(8,128)S(1)}, s32[1,272]{1,0:T(1,128)S(1)}, s32[1]{0:T(128)}) custom-call(s32[1]{0:T(128)} %bitcast.me_ref, bf16[512,2048]{1,0:T(8,128)(2,1)S(1)} %bitcast.11, bf16[272,2048]{1,0:T(8,128)(2,1)S(1)} %collective-permute-done.9.refs_0_), custom_call_target="tpu_custom_call" | custom-call | flops 1 | bytes 1 | tf_op jit(solution)/shard_map/low_rank/pallas_call | solution.py:228
  34.4 0.1 collective-permute-start.14
  34.5 1.3 %collective-permute-done.14 = f32[64,272]{1,0:T(8,128)S(1)} collective-permute-done((f32[64,272]{1,0:T(8,128)S(1)}, f32[64,272]{1,0:T(8,128)S(1)}, u32[]{:S(2)}, u32[]{:S(2)}) %collective-permute-start.14) | collective-permute-done | bytes 69664 | tf_op jit(solution)/shard_map/ppermute | solution.py:398
  35.8 1.6 %collective-permute-start.15 = (f32[64,272]{1,0:T(8,128)S(1)}, f32[64,272]{1,0:T(8,128)S(1)}, u32[]{:S(2)}, u32[]{:S(2)}) collective-permute-start(f32[64,272]{1,0:T(8,128)S(1)} %add.27.a_ref), channel_id=1, source_target_pairs={{0,2},{1,3},{2,0},{3,1},{4,6},{5,7},{6,4},{7,5},{8,10},{9,11},{10,... | collective-permute-start | bytes 208904 | tf_op jit(solution)/shard_map/ppermute | solution.py:398
  37.4 1.4 %collective-permute-start.16 = (bf16[144,2048]{1,0:T(8,128)(2,1)S(1)}, bf16[144,2048]{1,0:T(8,128)(2,1)S(1)}, u32[]{:S(2)}, u32[]{:S(2)}) collective-permute-start(bf16[144,2048]{1,0:T(8,128)(2,1)S(1)} %get-tuple-element.87), channel_id=1, source_target_pairs={{0,8},{4,12},{8,0},{12,4},{1,9},{5,13},{9,1},{13,5},{2,10},{6,14},... | collective-permute-start | bytes 1769480 | tf_op jit(solution)/shard_map/ppermute | solution.py:384
  38.8 1.9 %collective-permute-done.15.b_ref = f32[64,272]{1,0:T(8,128)S(1)} collective-permute-done((f32[64,272]{1,0:T(8,128)S(1)}, f32[64,272]{1,0:T(8,128)S(1)}, u32[]{:S(2)}, u32[]{:S(2)}) %collective-permute-start.15) | collective-permute-done | bytes 69664 | tf_op jit(solution)/shard_map/ppermute | solution.py:398
  40.7 0.5 up_coded.5
  41.2 16.3 %collective-permute-done.8.refs_0_ = bf16[272,2048]{1,0:T(8,128)(2,1)S(1)} collective-permute-done((bf16[272,2048]{1,0:T(8,128)(2,1)}, bf16[272,2048]{1,0:T(8,128)(2,1)S(1)}, u32[]{:S(2)}, u32[]{:S(2)}) %collective-permute-start.8) | collective-permute-done | bytes 1114144 | tf_op jit(solution)/shard_map/ppermute | solution.py:384
  57.5 0.1 slice_select_fusion
  57.6 1.6 %collective-permute-start.17 = (bf16[128,2048]{1,0:T(8,128)(2,1)S(1)}, bf16[128,2048]{1,0:T(8,128)(2,1)S(1)}, u32[]{:S(2)}, u32[]{:S(2)}) collective-permute-start(bf16[128,2048]{1,0:T(8,128)(2,1)S(1)} %slice_select_fusion), channel_id=1, source_target_pairs={{0,4},{4,0},{8,12},{12,8},{1,5},{5,1},{9,13},{13,9},{2,6},{6,2},{1... | collective-permute-start | bytes 1572872 | tf_op jit(solution)/shard_map/ppermute | solution.py:384
  59.2 3.5 %low_rank.6 = (f32[64,272]{1,0:T(8,128)S(1)}, s32[1,272]{1,0:T(1,128)S(1)}, s32[1]{0:T(128)}) custom-call(s32[1]{0:T(128)} %bitcast.me_ref, bf16[512,2048]{1,0:T(8,128)(2,1)} %bitcast.9, bf16[272,2048]{1,0:T(8,128)(2,1)S(1)} %collective-permute-done.8.refs_0_), custom_call_target="tpu_custom_call" | custom-call | flops 1 | bytes 1 | tf_op jit(solution)/shard_map/low_rank/pallas_call | solution.py:228
  62.6 0.1 collective-permute-start.18
  62.7 1.3 %collective-permute-done.18 = f32[64,272]{1,0:T(8,128)S(1)} collective-permute-done((f32[64,272]{1,0:T(8,128)S(1)}, f32[64,272]{1,0:T(8,128)S(1)}, u32[]{:S(2)}, u32[]{:S(2)}) %collective-permute-start.18) | collective-permute-done | bytes 69664 | tf_op jit(solution)/shard_map/ppermute | solution.py:398
  64.0 1.6 %collective-permute-start.19 = (f32[64,272]{1,0:T(8,128)S(1)}, f32[64,272]{1,0:T(8,128)S(1)}, u32[]{:S(2)}, u32[]{:S(2)}) collective-permute-start(f32[64,272]{1,0:T(8,128)S(1)} %add.29.a_ref), channel_id=1, source_target_pairs={{0,2},{1,3},{2,0},{3,1},{4,6},{5,7},{6,4},{7,5},{8,10},{9,11},{10,... | collective-permute-start | bytes 208904 | tf_op jit(solution)/shard_map/ppermute | solution.py:398
  65.6 3.4 %collective-permute-done.19.b_ref = f32[64,272]{1,0:T(8,128)S(1)} collective-permute-done((f32[64,272]{1,0:T(8,128)S(1)}, f32[64,272]{1,0:T(8,128)S(1)}, u32[]{:S(2)}, u32[]{:S(2)}) %collective-permute-start.19) | collective-permute-done | bytes 69664 | tf_op jit(solution)/shard_map/ppermute | solution.py:398
  68.9 0.5 up_coded.6
  69.5 12.2 %collective-permute-done.16.refs_0_ = bf16[144,2048]{1,0:T(8,128)(2,1)S(1)} collective-permute-done((bf16[144,2048]{1,0:T(8,128)(2,1)S(1)}, bf16[144,2048]{1,0:T(8,128)(2,1)S(1)}, u32[]{:S(2)}, u32[]{:S(2)}) %collective-permute-start.16) | collective-permute-done | bytes 589856 | tf_op jit(solution)/shard_map/ppermute | solution.py:384
  81.7 0.7 collective-permute-done.17.refs_1_
  82.3 1.8 %low_rank.7 = (f32[64,272]{1,0:T(8,128)S(1)}, s32[1,272]{1,0:T(1,128)S(1)}, s32[1]{0:T(128)}) custom-call(s32[1]{0:T(128)} %bitcast.me_ref, bf16[512,2048]{1,0:T(8,128)(2,1)S(1)} %bitcast.12, bf16[144,2048]{1,0:T(8,128)(2,1)S(1)} %collective-permute-done.16.refs_0_, bf16[128,2048]{1,0:T(8,128)(2,1)S(1)} %collective-permute-done.17.refs_1_), custom_call_target="tpu_custom_call" | custom-call | flops 1 | bytes 1 | tf_op jit(solution)/shard_map/low_rank/pallas_call | solution.py:228
  84.1 0.0 copy-start.6
  84.1 0.1 collective-permute-start.22
  84.2 1.3 %collective-permute-done.22 = f32[64,272]{1,0:T(8,128)S(1)} collective-permute-done((f32[64,272]{1,0:T(8,128)S(1)}, f32[64,272]{1,0:T(8,128)S(1)}, u32[]{:S(2)}, u32[]{:S(2)}) %collective-permute-start.22) | collective-permute-done | bytes 69664 | tf_op jit(solution)/shard_map/ppermute | solution.py:398
  85.5 1.6 %collective-permute-start.23 = (f32[64,272]{1,0:T(8,128)S(1)}, f32[64,272]{1,0:T(8,128)S(1)}, u32[]{:S(2)}, u32[]{:S(2)}) collective-permute-start(f32[64,272]{1,0:T(8,128)S(1)} %add.30.a_ref), channel_id=1, source_target_pairs={{0,2},{1,3},{2,0},{3,1},{4,6},{5,7},{6,4},{7,5},{8,10},{9,11},{10,... | collective-permute-start | bytes 208904 | tf_op jit(solution)/shard_map/ppermute | solution.py:398
  87.1 3.8 %collective-permute-start.20 = (s16[288,128]{1,0:T(8,128)(2,1)S(1)}, s16[288,128]{1,0:T(8,128)(2,1)S(1)}, u32[]{:S(2)}, u32[]{:S(2)}) collective-permute-start(s16[288,128]{1,0:T(8,128)(2,1)S(1)} %up_coded.6), channel_id=1, source_target_pairs={{0,12},{4,0},{8,4},{12,8},{1,13},{5,1},{9,5},{13,9},{2,14},{6,2},{... | collective-permute-start | bytes 221192 | tf_op jit(solution)/shard_map/ppermute | solution.py:384
  90.9 0.5 up_coded.7
  91.4 1.5 %collective-permute-start.24 = (s16[288,128]{1,0:T(8,128)(2,1)S(1)}, s16[288,128]{1,0:T(8,128)(2,1)S(1)}, u32[]{:S(2)}, u32[]{:S(2)}) collective-permute-start(s16[288,128]{1,0:T(8,128)(2,1)S(1)} %up_coded.7), channel_id=1, source_target_pairs={{0,8},{4,12},{8,0},{12,4},{1,9},{5,13},{9,1},{13,5},{2,10},{6,14},... | collective-permute-start | bytes 221192 | tf_op jit(solution)/shard_map/ppermute | solution.py:384
  94.2 0.8 gather_add.6
  96.3 0.2 conditional.1
  96.5 1.4 %collective-permute-done.24.refs_1_ = s16[288,128]{1,0:T(8,128)(2,1)S(1)} collective-permute-done((s16[288,128]{1,0:T(8,128)(2,1)S(1)}, s16[288,128]{1,0:T(8,128)(2,1)S(1)}, u32[]{:S(2)}, u32[]{:S(2)}) %collective-permute-start.24) | collective-permute-done | bytes 73760 | tf_op jit(solution)/shard_map/ppermute | solution.py:384
  97.9 1.2 %gather_add.7 = bf16[512,128]{1,0:T(8,128)(2,1)} custom-call(s32[1,512]{1,0:T(1,128)S(1)} %get-tuple-element.73.dest_ref, f32[512,128]{1,0:T(8,128)S(1)} %get-tuple-element.98.refs_0_, s16[288,128]{1,0:T(8,128)(2,1)S(1)} %collective-permute-done.24.refs_1_), custom_call_target="tpu_custom_call" | custom-call | flops 1 | bytes 1 | tf_op jit(solution)/shard_map/gather_add/pallas_call | solution.py:372
  (23 shorter events, 0.2 us)
Async XLA Ops:
  0.0 7.7 %copy-start = (bf16[2048,512]{1,0:T(8,128)(2,1)S(1)}, bf16[2048,512]{1,0:T(8,128)(2,1)}, u32[]{:S(2)}) copy-start(bf16[2048,512]{1,0:T(8,128)(2,1)} %value_ref.1) | copy-start | bytes 6291460
  2.6 8.2 %copy-start.1 = (bf16[512,2048]{1,0:T(8,128)(2,1)S(1)}, bf16[512,2048]{1,0:T(8,128)(2,1)}, u32[]{:S(2)}) copy-start(bf16[512,2048]{1,0:T(8,128)(2,1)} %tokens_ref.5) | copy-start | bytes 6291460
  2.6 30.1 %collective-permute-start.9 = (bf16[272,2048]{1,0:T(8,128)(2,1)S(1)}, bf16[272,2048]{1,0:T(8,128)(2,1)S(1)}, u32[]{:S(2)}, u32[]{:S(2)}) collective-permute-start(bf16[272,2048]{1,0:T(8,128)(2,1)S(1)} %get-tuple-element.75.third_ref), channel_id=1, source_target_pairs={{0,12},{4,0},{8,4},{12,8},{1,13},{5,1},{9,5},{13,9},{2,14},{6,2},{... | collective-permute-start | bytes 3342344 | tf_op jit(solution)/shard_map/ppermute | solution.py:384
  10.7 1.9 %copy-start.2 = (bf16[8,2048,64]{1,2,0:T(8,128)(2,1)S(1)}, bf16[8,2048,64]{1,2,0:T(8,128)(2,1)}, u32[]{:S(2)}) copy-start(bf16[8,2048,64]{1,2,0:T(8,128)(2,1)} %param.12) | copy-start | bytes 6291460
  10.7 6.3 %collective-permute-start.10 = (f32[512,256]{1,0:T(8,128)S(1)}, f32[512,256]{1,0:T(8,128)S(1)}, u32[]{:S(2)}, u32[]{:S(2)}) collective-permute-start(f32[512,256]{1,0:T(8,128)S(1)} %get-tuple-element.79), channel_id=1, source_target_pairs={{0,1},{1,0},{2,3},{3,2},{4,5},{5,4},{6,7},{7,6},{8,9},{9,8},{10,11... | collective-permute-start | bytes 1572872 | tf_op jit(solution)/shard_map/ppermute | solution.py:398
  12.5 45.0 %collective-permute-start.8 = (bf16[272,2048]{1,0:T(8,128)(2,1)}, bf16[272,2048]{1,0:T(8,128)(2,1)S(1)}, u32[]{:S(2)}, u32[]{:S(2)}) collective-permute-start(bf16[272,2048]{1,0:T(8,128)(2,1)} %get-tuple-element.76), channel_id=1, source_target_pairs={{0,4},{4,8},{8,12},{12,0},{1,5},{5,9},{9,13},{13,1},{2,6},{6,10},{... | collective-permute-start | bytes 3342344 | tf_op jit(solution)/shard_map/ppermute | solution.py:384
  13.8 1.5 %collective-permute-start.12 = (f32[64,512]{1,0:T(8,128)S(1)}, f32[64,512]{1,0:T(8,128)S(1)}, u32[]{:S(2)}, u32[]{:S(2)}) collective-permute-start(f32[64,512]{1,0:T(8,128)S(1)} %low_rank_home.1), channel_id=1, source_target_pairs={{0,1},{1,0},{2,3},{3,2},{4,5},{5,4},{6,7},{7,6},{8,9},{9,8},{10,11... | collective-permute-start | bytes 393224 | tf_op jit(solution)/shard_map/ppermute | solution.py:398
  15.4 6.4 %copy-start.5 = (bf16[8,64,128]{2,1,0:T(8,128)(2,1)S(1)}, bf16[8,64,128]{2,1,0:T(8,128)(2,1)}, u32[]{:S(2)}) copy-start(bf16[8,64,128]{2,1,0:T(8,128)(2,1)} %param.13) | copy-start | bytes 393220
  15.4 6.4 %collective-permute-start.13 = (f32[64,512]{1,0:T(8,128)S(1)}, f32[64,512]{1,0:T(8,128)S(1)}, u32[]{:S(2)}, u32[]{:S(2)}) collective-permute-start(f32[64,512]{1,0:T(8,128)S(1)} %add.26.a_ref), channel_id=1, source_target_pairs={{0,2},{1,3},{2,0},{3,1},{4,6},{5,7},{6,4},{7,5},{8,10},{9,11},{10,... | collective-permute-start | bytes 393224 | tf_op jit(solution)/shard_map/ppermute | solution.py:398
  17.1 9.8 %collective-permute-start.11 = (f32[512,128]{1,0:T(8,128)S(1)}, f32[512,128]{1,0:T(8,128)S(1)}, u32[]{:S(2)}, u32[]{:S(2)}) collective-permute-start(f32[512,128]{1,0:T(8,128)S(1)} %get-tuple-element.96), channel_id=1, source_target_pairs={{0,2},{1,3},{2,0},{3,1},{4,6},{5,7},{6,4},{7,5},{8,10},{9,11},{10,... | collective-permute-start | bytes 786440 | tf_op jit(solution)/shard_map/ppermute | solution.py:398
  34.4 1.4 %collective-permute-start.14 = (f32[64,272]{1,0:T(8,128)S(1)}, f32[64,272]{1,0:T(8,128)S(1)}, u32[]{:S(2)}, u32[]{:S(2)}) collective-permute-start(f32[64,272]{1,0:T(8,128)S(1)} %get-tuple-element.83), channel_id=1, source_target_pairs={{0,1},{1,0},{2,3},{3,2},{4,5},{5,4},{6,7},{7,6},{8,9},{9,8},{10,11... | collective-permute-start | bytes 208904 | tf_op jit(solution)/shard_map/ppermute | solution.py:398
  35.8 4.9 %collective-permute-start.15 = (f32[64,272]{1,0:T(8,128)S(1)}, f32[64,272]{1,0:T(8,128)S(1)}, u32[]{:S(2)}, u32[]{:S(2)}) collective-permute-start(f32[64,272]{1,0:T(8,128)S(1)} %add.27.a_ref), channel_id=1, source_target_pairs={{0,2},{1,3},{2,0},{3,1},{4,6},{5,7},{6,4},{7,5},{8,10},{9,11},{10,... | collective-permute-start | bytes 208904 | tf_op jit(solution)/shard_map/ppermute | solution.py:398
  37.4 44.3 %collective-permute-start.16 = (bf16[144,2048]{1,0:T(8,128)(2,1)S(1)}, bf16[144,2048]{1,0:T(8,128)(2,1)S(1)}, u32[]{:S(2)}, u32[]{:S(2)}) collective-permute-start(bf16[144,2048]{1,0:T(8,128)(2,1)S(1)} %get-tuple-element.87), channel_id=1, source_target_pairs={{0,8},{4,12},{8,0},{12,4},{1,9},{5,13},{9,1},{13,5},{2,10},{6,14},... | collective-permute-start | bytes 1769480 | tf_op jit(solution)/shard_map/ppermute | solution.py:384
  57.6 24.8 %collective-permute-start.17 = (bf16[128,2048]{1,0:T(8,128)(2,1)S(1)}, bf16[128,2048]{1,0:T(8,128)(2,1)S(1)}, u32[]{:S(2)}, u32[]{:S(2)}) collective-permute-start(bf16[128,2048]{1,0:T(8,128)(2,1)S(1)} %slice_select_fusion), channel_id=1, source_target_pairs={{0,4},{4,0},{8,12},{12,8},{1,5},{5,1},{9,13},{13,9},{2,6},{6,2},{1... | collective-permute-start | bytes 1572872 | tf_op jit(solution)/shard_map/ppermute | solution.py:384
  59.2 23.2 %copy-start.3 = (bf16[8,2048,64]{1,2,0:T(8,128)(2,1)S(1)}, bf16[8,2048,64]{1,2,0:T(8,128)(2,1)}, u32[]{:S(2)}) copy-start(bf16[8,2048,64]{1,2,0:T(8,128)(2,1)} %param.12) | copy-start | bytes 6291460
  62.6 1.4 %collective-permute-start.18 = (f32[64,272]{1,0:T(8,128)S(1)}, f32[64,272]{1,0:T(8,128)S(1)}, u32[]{:S(2)}, u32[]{:S(2)}) collective-permute-start(f32[64,272]{1,0:T(8,128)S(1)} %get-tuple-element.89), channel_id=1, source_target_pairs={{0,1},{1,0},{2,3},{3,2},{4,5},{5,4},{6,7},{7,6},{8,9},{9,8},{10,11... | collective-permute-start | bytes 208904 | tf_op jit(solution)/shard_map/ppermute | solution.py:398
  64.0 4.9 %collective-permute-start.19 = (f32[64,272]{1,0:T(8,128)S(1)}, f32[64,272]{1,0:T(8,128)S(1)}, u32[]{:S(2)}, u32[]{:S(2)}) collective-permute-start(f32[64,272]{1,0:T(8,128)S(1)} %add.29.a_ref), channel_id=1, source_target_pairs={{0,2},{1,3},{2,0},{3,1},{4,6},{5,7},{6,4},{7,5},{8,10},{9,11},{10,... | collective-permute-start | bytes 208904 | tf_op jit(solution)/shard_map/ppermute | solution.py:398
  84.1 12.2 %copy-start.6 = (s32[512]{0:T(512)S(1)}, s32[512]{0:T(512)}, u32[]{:S(2)}) copy-start(s32[512]{0:T(512)} %param.9) | copy-start | bytes 6148
  84.1 12.2 %copy-start.7 = (s32[32]{0:T(128)S(1)}, s32[32]{0:T(128)}, u32[]{:S(2)}) copy-start(s32[32]{0:T(128)} %param.10) | copy-start | bytes 388
  84.1 1.4 %collective-permute-start.22 = (f32[64,272]{1,0:T(8,128)S(1)}, f32[64,272]{1,0:T(8,128)S(1)}, u32[]{:S(2)}, u32[]{:S(2)}) collective-permute-start(f32[64,272]{1,0:T(8,128)S(1)} %get-tuple-element.95), channel_id=1, source_target_pairs={{0,1},{1,0},{2,3},{3,2},{4,5},{5,4},{6,7},{7,6},{8,9},{9,8},{10,11... | collective-permute-start | bytes 208904 | tf_op jit(solution)/shard_map/ppermute | solution.py:398
  85.5 5.4 %collective-permute-start.23 = (f32[64,272]{1,0:T(8,128)S(1)}, f32[64,272]{1,0:T(8,128)S(1)}, u32[]{:S(2)}, u32[]{:S(2)}) collective-permute-start(f32[64,272]{1,0:T(8,128)S(1)} %add.30.a_ref), channel_id=1, source_target_pairs={{0,2},{1,3},{2,0},{3,1},{4,6},{5,7},{6,4},{7,5},{8,10},{9,11},{10,... | collective-permute-start | bytes 208904 | tf_op jit(solution)/shard_map/ppermute | solution.py:398
  87.1 7.1 %collective-permute-start.21 = (s16[288,128]{1,0:T(8,128)(2,1)S(1)}, s16[288,128]{1,0:T(8,128)(2,1)S(1)}, u32[]{:S(2)}, u32[]{:S(2)}) collective-permute-start(s16[288,128]{1,0:T(8,128)(2,1)S(1)} %up_coded.5), channel_id=1, source_target_pairs={{0,4},{4,8},{8,12},{12,0},{1,5},{5,9},{9,13},{13,1},{2,6},{6,10},{... | collective-permute-start | bytes 221192 | tf_op jit(solution)/shard_map/ppermute | solution.py:384
  87.1 7.2 %collective-permute-start.20 = (s16[288,128]{1,0:T(8,128)(2,1)S(1)}, s16[288,128]{1,0:T(8,128)(2,1)S(1)}, u32[]{:S(2)}, u32[]{:S(2)}) collective-permute-start(s16[288,128]{1,0:T(8,128)(2,1)S(1)} %up_coded.6), channel_id=1, source_target_pairs={{0,12},{4,0},{8,4},{12,8},{1,13},{5,1},{9,5},{13,9},{2,14},{6,2},{... | collective-permute-start | bytes 221192 | tf_op jit(solution)/shard_map/ppermute | solution.py:384
  91.4 6.5 %collective-permute-start.24 = (s16[288,128]{1,0:T(8,128)(2,1)S(1)}, s16[288,128]{1,0:T(8,128)(2,1)S(1)}, u32[]{:S(2)}, u32[]{:S(2)}) collective-permute-start(s16[288,128]{1,0:T(8,128)(2,1)S(1)} %up_coded.7), channel_id=1, source_target_pairs={{0,8},{4,12},{8,0},{12,4},{1,9},{5,13},{9,1},{13,5},{2,10},{6,14},... | collective-permute-start | bytes 221192 | tf_op jit(solution)/shard_map/ppermute | solution.py:384
